TPU v7x, 128 devices: a whole 4x4x4 slice. The times are simulated.
128 devices in a mesh: ctx: 16 (over z, x_hi, core), exp: 8 (over x_lo, y).
Axes of the slice: x: 4 (x_hi: 2, x_lo: 2; x = x_hi * 2 + x_lo), y: 4, z: 4, core: 2. Of those that a mesh axis runs over, the one named last changes fastest.
Arguments:
- tokens: bfloat16 [8, 2048, 768], P('exp', 'ctx'), may hold values from -6 to 6
- cotangent: bfloat16 [8, 2048, 768], P('exp', 'ctx'), may hold values from -6 to 6
- routes: int32 [8, 2048, 1], P('exp', 'ctx'), may hold values from 0 to 15; in each aligned block of 128 rows (0 to 127, 128 to 255, ..., all dimensions but the last counted through in order) at most 10 rows name the same one
- query_weight: bfloat16 [768, 768], P(('ctx', 'exp')), may hold values from -0.0546875 to 0.0546875
- kv_weight: bfloat16 [768, 1536], P(('ctx', 'exp')), may hold values from -0.21875 to 0.21875
- out_weight: bfloat16 [768, 768], P(('ctx', 'exp')), may hold values from -3.5 to 3.5
- norm_gain_one: bfloat16 [768], P(('ctx', 'exp')), may hold values from 0.5 to 1.5
- norm_gain_two: bfloat16 [768], P(('ctx', 'exp')), may hold values from 0.5 to 1.5
- router_weight: bfloat16 [768, 16], P(('ctx', 'exp')), may hold values from -0.15625 to 0.15625
- bias_table: bfloat16 [384], P(('ctx', 'exp')), may hold values from -5 to 5
- expert_in: bfloat16 [16, 768, 3072], P('exp', None, 'ctx'), may hold values from -0.21875 to 0.21875
- expert_out: bfloat16 [16, 3072, 768], P('exp', 'ctx'), may hold values from -1.75 to 1.75
Outputs:
- mixed: bfloat16 [8, 2048, 768], P('exp', 'ctx')
- grad_tokens: float32 [8, 2048, 768], P('exp', 'ctx')
- grad_query_weight: float32 [768, 768], P(('ctx', 'exp'))
- grad_kv_weight: float32 [768, 1536], P(('ctx', 'exp'))
- grad_out_weight: float32 [768, 768], P(('ctx', 'exp'))
- grad_norm_gain_one: float32 [768], P(('ctx', 'exp'))
- grad_norm_gain_two: float32 [768], P(('ctx', 'exp'))
- grad_router_weight: float32 [768, 16], P(('ctx', 'exp'))
- grad_bias_table: float32 [384], P(('ctx', 'exp'))
- grad_expert_in: float32 [16, 768, 3072], P('exp', None, 'ctx')
- grad_expert_out: float32 [16, 3072, 768], P('exp', 'ctx')
Inputs may be any that keep to these rules, and one draw needn't show every extreme that they name: `routes`: in the rows of one device each expert is named at most 10 times, a bound that some block reaches.
All inputs are finite; a program needn't handle non-finite values.
Results may differ from a plain program's by a relative error of at most 0.018.
Values may be sent and summed in bfloat16 or wider, within the bound.
A program may use at most 128 MiB of HBM per device.

v0:
```python
import math

import jax
import jax.numpy as jnp
from jax import lax
from jax.sharding import PartitionSpec as P

HEADS = 12
HEAD_DIM = 64
NUM_BUCKETS = 32


epsilon = 1e-06
bucket_edges = (12, 16, 23, 32, 46, 64, 91)
key_width = 512


def side_by_side(arrays, axis, dim, along):
    widths = [math.prod(a.shape[along:]) for a in arrays]
    both = jnp.concatenate(
        [a.reshape(*a.shape[:along], w) for a, w in zip(arrays, widths)], axis=along
    )
    filled = lax.all_gather(both, axis, axis=dim, tiled=True)
    parts = jnp.split(filled, [sum(widths[:k]) for k in range(1, len(widths))], axis=along)
    return tuple(
        (b.reshape(*filled.shape[:along], *a.shape[along:]) for a, b in zip(arrays, parts))
    )


def cut_along(shard, dim, length):
    before, after = (shard.shape[:dim], shard.shape[dim + 1 :])
    return jnp.moveaxis(shard.reshape(*before, length, -1, *after), dim, 0)


def one_scatter(arrays, axis, dims):
    length = lax.axis_size(axis)
    parts = [cut_along(a, dim, length) for a, dim in zip(arrays, dims)]
    lines = jnp.concatenate([b.reshape(length, -1) for b in parts], axis=1)
    rows = max(16, -(-lines.shape[1] // 1024) * 8)
    lines = jnp.pad(lines, ((0, 0), (0, rows * 128 - lines.shape[1]))).reshape(-1, 128)
    vector, at, finished = (lax.psum_scatter(lines, axis, tiled=True).reshape(-1), 0, [])
    for b in parts:
        part = b[0]
        finished.append(vector[at : at + part.size].reshape(part.shape))
        at += part.size
    return tuple(finished)


def rms_scale(values_in, gain_vec):
    return (
        values_in
        * lax.rsqrt(jnp.mean(values_in * values_in, axis=-1, keepdims=True) + epsilon)
        * gain_vec
    )


def bucket_ids(query_location, key_pos):
    offset = key_pos[None, :] - query_location[:, None]
    distance = jnp.abs(offset)
    far_bucket = jnp.full(distance.shape, 8, jnp.int32)
    for edge_value in bucket_edges:
        far_bucket = far_bucket + (distance >= edge_value).astype(jnp.int32)
    half_bucket = jnp.where(distance < 8, distance, far_bucket)
    return half_bucket + NUM_BUCKETS // 2 * (offset > 0).astype(jnp.int32)


def shards(
    tokens,
    cotangent,
    routes,
    query_weight,
    kv_weight,
    out_weight,
    norm_gain_one,
    norm_gain_two,
    router_weight,
    bias_table,
    expert_in,
    expert_out,
):
    highest = lax.Precision.HIGHEST
    tok_count = tokens.shape[1]
    model_width = tokens.shape[2]
    local_experts = expert_in.shape[0]
    expert_count = local_experts * lax.axis_size("exp")
    capacity = 5 * tok_count // (4 * expert_count)
    x_rows = tokens[0].astype(jnp.float32)
    query_full, kv_full, out_full, gain_one, gain_two, router_full, table_flat = (
        *side_by_side(
            (query_weight, kv_weight, out_weight, norm_gain_one, norm_gain_two, router_weight),
            ("ctx", "exp"),
            0,
            1,
        ),
        lax.all_gather(bias_table, ("ctx", "exp"), axis=0, tiled=True),
    )
    position_bias_matrix = table_flat.reshape(NUM_BUCKETS, HEADS)
    normed_one, norm_one_back = jax.vjp(rms_scale, x_rows, gain_one.astype(jnp.float32))
    h_one = normed_one.astype(jnp.bfloat16)
    queries = jnp.dot(h_one, query_full, preferred_element_type=jnp.float32).astype(jnp.bfloat16)
    keyval = jnp.dot(h_one, kv_full, preferred_element_type=jnp.float32).astype(jnp.bfloat16)
    keyval_all = lax.all_gather(keyval, "ctx", axis=0, tiled=True)
    seq_length = keyval_all.shape[0]
    block_rows = min(key_width, seq_length)
    block_count = seq_length // block_rows
    query_heads = queries.reshape(tok_count, HEADS, HEAD_DIM)
    key_heads = keyval_all[:, :model_width].reshape(block_count, block_rows, HEADS, HEAD_DIM)
    per_head_values = keyval_all[:, model_width:].reshape(block_count, block_rows, HEADS, HEAD_DIM)
    block_index = jnp.arange(block_count, dtype=jnp.int32)
    query_location = lax.axis_index("ctx") * tok_count + jnp.arange(tok_count, dtype=jnp.int32)
    bucket_range = jnp.arange(NUM_BUCKETS, dtype=jnp.int32)

    def block_scores(index_value, keys_here):
        key_pos = index_value * block_rows + jnp.arange(block_rows, dtype=jnp.int32)
        bucket_indicator = (
            bucket_range[:, None, None] == bucket_ids(query_location, key_pos)[None]
        ).astype(jnp.bfloat16)
        pair_bias = jnp.einsum(
            "uri,uj->jri",
            bucket_indicator,
            position_bias_matrix,
            preferred_element_type=jnp.float32,
        )
        scores = jnp.einsum(
            "qhd,khd->hqk", query_heads, keys_here, preferred_element_type=jnp.float32
        )
        return (scores + pair_bias, bucket_indicator)

    def stats_step(carried, inputs):
        row_max, row_total = carried
        scores = block_scores(inputs[0], inputs[1])[0]
        new_max = jnp.maximum(row_max, jnp.max(scores, axis=2, keepdims=True))
        row_total = row_total * jnp.exp(row_max - new_max) + jnp.sum(
            jnp.exp(scores - new_max), axis=2, keepdims=True
        )
        return ((new_max, row_total), None)

    start_max = jnp.full((HEADS, tok_count, 1), -1e30, jnp.float32)
    stats, unused = lax.scan(
        stats_step, (start_max, jnp.zeros_like(start_max)), (block_index, key_heads)
    )
    log_total = stats[0] + jnp.log(stats[1])

    def value_step(totals, inputs):
        total_value, exact_value = totals
        scores = block_scores(inputs[0], inputs[1])[0]
        soft_probs = jnp.exp(scores - log_total)
        probs_low = soft_probs.astype(jnp.bfloat16)
        total_value = total_value + jnp.einsum(
            "hqk,khd->qhd", probs_low, inputs[2], preferred_element_type=jnp.float32
        )
        exact_value = exact_value + jnp.einsum(
            "hqk,khd->qhd", soft_probs, inputs[2].astype(jnp.float32), precision=highest
        )
        return ((total_value, exact_value), None)

    zero_attended = jnp.zeros((tok_count, HEADS, HEAD_DIM), jnp.float32)
    value_sums, unused = lax.scan(
        value_step, (zero_attended, zero_attended), (block_index, key_heads, per_head_values)
    )
    attended, attended_exact = value_sums
    attended_low = attended.reshape(tok_count, model_width).astype(jnp.bfloat16)
    residual = x_rows + jnp.dot(attended_low, out_full, preferred_element_type=jnp.float32)
    normed_two, norm_two_back = jax.vjp(rms_scale, residual, gain_two.astype(jnp.float32))
    h_two = normed_two.astype(jnp.bfloat16)
    h_two_wide = h_two.astype(jnp.float32)
    router_wide = router_full.astype(jnp.float32)
    route_probs = jax.nn.softmax(jnp.dot(h_two_wide, router_wide, precision=highest), axis=-1)
    route_ids = routes[0, :, 0]
    choose = (route_ids[:, None] == jnp.arange(expert_count, dtype=jnp.int32)[None, :]).astype(
        jnp.int32
    )
    earlier = jnp.cumsum(choose, axis=0) - choose
    target = route_ids * capacity + jnp.sum(earlier * choose, axis=1)
    dispatch = (
        jnp.arange(expert_count * capacity, dtype=jnp.int32)[:, None] == target[None, :]
    ).astype(jnp.bfloat16)
    choose_wide = choose.astype(jnp.float32)
    gate_value = jnp.sum(route_probs * choose_wide, axis=1)
    outgoing = (
        jnp.dot(dispatch, h_two, preferred_element_type=jnp.float32)
        .astype(jnp.bfloat16)
        .reshape(expert_count, capacity, model_width)
    )
    received = lax.all_to_all(outgoing, "exp", split_axis=0, concat_axis=1, tiled=True)
    rows_all = lax.all_gather(received, "ctx", axis=1, tiled=True)
    pre_act = jnp.einsum("erd,edf->erf", rows_all, expert_in, preferred_element_type=jnp.float32)
    hidden_wide, gelu_back = jax.vjp(jax.nn.gelu, pre_act)
    hidden = hidden_wide.astype(jnp.bfloat16)
    partial_value = jnp.einsum(
        "erf,efd->erd", hidden, expert_out, preferred_element_type=jnp.float32
    )
    expert_y = lax.psum_scatter(partial_value, "ctx", scatter_dimension=1, tiled=True).astype(
        jnp.bfloat16
    )
    returned = lax.all_to_all(expert_y, "exp", split_axis=1, concat_axis=0, tiled=True)
    expert_tokens = jnp.einsum(
        "st,sd->td",
        dispatch,
        returned.reshape(expert_count * capacity, model_width),
        preferred_element_type=jnp.float32,
    )
    mixed_rows = (residual + gate_value[:, None] * expert_tokens).astype(jnp.bfloat16)
    grad_out = cotangent[0].astype(jnp.float32)
    grad_gate = jnp.sum(grad_out * expert_tokens, axis=1)
    grad_y = (gate_value[:, None] * grad_out).astype(jnp.bfloat16)
    grad_slots = (
        jnp.dot(dispatch, grad_y, preferred_element_type=jnp.float32)
        .astype(jnp.bfloat16)
        .reshape(expert_count, capacity, model_width)
    )
    grad_received = lax.all_to_all(grad_slots, "exp", split_axis=0, concat_axis=1, tiled=True)
    grad_rows_y = lax.all_gather(grad_received, "ctx", axis=1, tiled=True)
    grad_hidden = jnp.einsum(
        "erd,efd->erf", grad_rows_y, expert_out, preferred_element_type=jnp.float32
    )
    grad_pre = gelu_back(grad_hidden)[0].astype(jnp.bfloat16)
    grad_expert_out = jnp.einsum(
        "erf,erd->efd", hidden, grad_rows_y, preferred_element_type=jnp.float32
    )
    grad_expert_in = jnp.einsum(
        "erd,erf->edf", rows_all, grad_pre, preferred_element_type=jnp.float32
    )
    partial_back = jnp.einsum(
        "erf,edf->erd", grad_pre, expert_in, preferred_element_type=jnp.float32
    )
    grad_rows = lax.psum_scatter(partial_back, "ctx", scatter_dimension=1, tiled=True).astype(
        jnp.bfloat16
    )
    grad_back = lax.all_to_all(grad_rows, "exp", split_axis=1, concat_axis=0, tiled=True)
    grad_h_two = jnp.einsum(
        "st,sd->td",
        dispatch,
        grad_back.reshape(expert_count * capacity, model_width),
        preferred_element_type=jnp.float32,
    )
    grad_choice = choose_wide * grad_gate[:, None]
    grad_logits = route_probs * (
        grad_choice - jnp.sum(route_probs * grad_choice, axis=1, keepdims=True)
    )
    grad_router = jnp.dot(h_two_wide.T, grad_logits, precision=highest)
    grad_h_two = grad_h_two + jnp.dot(grad_logits, router_wide.T, precision=highest)
    grad_resid_norm, grad_gain_two = norm_two_back(grad_h_two)
    grad_residual = grad_out + grad_resid_norm
    grad_branch = grad_residual.astype(jnp.bfloat16)
    grad_out_weight = jnp.dot(attended_low.T, grad_branch, preferred_element_type=jnp.float32)
    grad_attended = (
        jnp.dot(grad_branch, out_full.T, preferred_element_type=jnp.float32)
        .astype(jnp.bfloat16)
        .reshape(tok_count, HEADS, HEAD_DIM)
    )
    row_delta = jnp.einsum("qhd,qhd->hq", grad_attended.astype(jnp.float32), attended_exact)[
        :, :, None
    ]

    def gradient_increment(carried, inputs):
        grad_query_sum, grad_grid = carried
        scores, bucket_indicator = block_scores(inputs[0], inputs[1])
        soft_probs = jnp.exp(scores - log_total)
        grad_probs = jnp.einsum(
            "qhd,khd->hqk", grad_attended, inputs[2], preferred_element_type=jnp.float32
        )
        score_float = soft_probs * (grad_probs - row_delta)
        score_gradient = score_float.astype(jnp.bfloat16)
        grad_query_sum = grad_query_sum + jnp.einsum(
            "hqk,khd->qhd", score_gradient, inputs[1], preferred_element_type=jnp.float32
        )
        grad_grid = grad_grid + jnp.einsum(
            "lyv,syv->sl", score_float, bucket_indicator.astype(jnp.float32), precision=highest
        )
        grad_keys = jnp.einsum(
            "hqk,qhd->khd", score_gradient, query_heads, preferred_element_type=jnp.float32
        )
        grad_values = jnp.einsum(
            "hqk,qhd->khd",
            soft_probs.astype(jnp.bfloat16),
            grad_attended,
            preferred_element_type=jnp.float32,
        )
        block_terms = jnp.concatenate(
            [
                grad_keys.reshape(block_rows, model_width),
                grad_values.reshape(block_rows, model_width),
            ],
            axis=1,
        )
        return ((grad_query_sum, grad_grid), block_terms)

    start_grads = (
        jnp.zeros((tok_count, HEADS, HEAD_DIM), jnp.float32),
        jnp.zeros((NUM_BUCKETS, HEADS), jnp.float32),
    )
    attention_grads, kv_terms = lax.scan(
        gradient_increment, start_grads, (block_index, key_heads, per_head_values)
    )
    grad_keyval = lax.psum_scatter(
        kv_terms.reshape(seq_length, 2 * model_width), "ctx", scatter_dimension=0, tiled=True
    ).astype(jnp.bfloat16)
    grad_queries = attention_grads[0].reshape(tok_count, model_width).astype(jnp.bfloat16)
    grad_query_weight = jnp.dot(h_one.T, grad_queries, preferred_element_type=jnp.float32)
    grad_kv_weight = jnp.dot(h_one.T, grad_keyval, preferred_element_type=jnp.float32)
    grad_h_one = jnp.dot(grad_queries, query_full.T, preferred_element_type=jnp.float32) + jnp.dot(
        grad_keyval, kv_full.T, preferred_element_type=jnp.float32
    )
    grad_x_norm, grad_gain_one = norm_one_back(grad_h_one)
    grad_tokens = grad_residual + grad_x_norm
    shared_grads = one_scatter(
        (
            grad_query_weight,
            grad_kv_weight,
            grad_out_weight,
            grad_gain_one,
            grad_gain_two,
            grad_router,
            attention_grads[1].reshape(-1),
        ),
        ("ctx", "exp"),
        (0, 0, 0, 0, 0, 0, 0),
    )
    return (
        mixed_rows[None],
        grad_tokens[None],
        shared_grads[0],
        shared_grads[1],
        shared_grads[2],
        shared_grads[3],
        shared_grads[4],
        shared_grads[5],
        shared_grads[6],
        grad_expert_in,
        grad_expert_out,
    )


def solution(mesh):
    return jax.shard_map(
        shards,
        mesh=mesh,
        in_specs=(
            P("exp", "ctx", None),
            P("exp", "ctx", None),
            P("exp", "ctx", None),
            P(("ctx", "exp"), None),
            P(("ctx", "exp"), None),
            P(("ctx", "exp"), None),
            P(("ctx", "exp")),
            P(("ctx", "exp")),
            P(("ctx", "exp"), None),
            P(("ctx", "exp")),
            P("exp", None, "ctx"),
            P("exp", "ctx", None),
        ),
        out_specs=(
            P("exp", "ctx", None),
            P("exp", "ctx", None),
            P(("ctx", "exp"), None),
            P(("ctx", "exp"), None),
            P(("ctx", "exp"), None),
            P(("ctx", "exp")),
            P(("ctx", "exp")),
            P(("ctx", "exp"), None),
            P(("ctx", "exp")),
            P("exp", None, "ctx"),
            P("exp", "ctx", None),
        ),
        check_vma=False,
    )
```

profile of v0, /device:TPU:1, one launch (start us, length us, event | category | flops | bytes accessed | tf_op | source)
XLA Modules:
  0.0 1393.2 jit_solution(2475021658002987542)
XLA Ops:
  12.0 311.7 %all-gather.12.cloned.1.call-done = bf16[128,6,3090]{2,1,0:T(8,128)(2,1)} async-done(((bf16[1,6,3090]{2,1,0:T(8,128)(2,1)}), bf16[128,6,3090]{2,1,0:T(8,128)(2,1)}) %all-gather.12.cloned.1.call-update) | async-done | bytes 4746256 | tf_op jit(solution)/shard_map/all_gather | solution.py:23
  323.7 9.9 reshape.396
  338.2 76.2 %all-reduce.1 = bf16[384]{0:T(512)(128)(2,1)S(1)} all-reduce(bf16[384]{0:T(512)(128)(2,1)S(1)} %dynamic-update-slice), channel_id=1, replica_groups=mesh['ctx'=16,'exp'=8] {'ctx','exp'}, use_global_device_ids=true, to_apply=%add.1 | all-reduce | flops 384 | bytes 1536
  416.9 5.9 fusion.169
  422.8 4.7 copy.97
  427.5 6.2 reshape.372
  433.7 4.3 copy.102
  438.0 52.4 %while.41 = (s32[]{:T(128)}, f32[12,128,1]{1,0,2:T(8,128)S(1)}, f32[12,128,1]{1,0,2:T(8,128)S(1)}, bf16[4,512,12,64]{1,3,2,0:T(8,128)(2,1)}, bf16[128,12,64]{0,2...) while((s32[]{:T(128)}, f32[12,128,1]{1,0,2:T(8,128)S(1)}, ...), condition=%wide.region_4.5_spmd.clone, body=%wide.region_1.4_spmd.clone.sunk | while | flops 158081152 | bytes 20467616 | solution.py:139
  442.9 4.9 copy.161
  456.0 4.9 copy.161
  469.1 4.9 copy.161
  482.2 4.9 copy.161
  490.4 4.7 copy.96
  495.1 6.2 reshape.371
  501.3 4.3 copy.101
  505.6 59.5 %while.42 = (s32[]{:T(128)}, f32[128,12,64]{0,2,1:T(8,128)S(1)}, f32[128,12,64]{0,2,1:T(8,128)S(1)}, bf16[4,512,12,64]{1,3,2,0:T(8,128)(2,1)}, bf16[4,512,12,64]...) while((s32[]{:T(128)}, f32[128,12,64]{0,2,1:T(8,128)S(1)}, ...), condition=%wide.region_6.7_spmd.clone, body=%wide.region_5.6_spmd.clone.sunk | while | flops 862323328 | bytes 39268308 | solution.py:158
  510.8 4.9 copy.162
  525.6 4.9 copy.162
  540.4 4.9 copy.162
  555.2 4.9 copy.162
  568.0 11.1 all_to_all.66
  580.1 53.6 %all-gather.8.cloned.1.call-done = bf16[2,1280,768]{2,1,0:T(8,128)(2,1)} async-done(((bf16[2,80,768]{2,1,0:T(8,128)(2,1)}), bf16[2,1280,768]{2,1,0:T(8,128)(2,1)}) %all-gather.8.cloned.1.call-update) | async-done | bytes 3932176 | tf_op jit(solution)/shard_map/all_gather | solution.py:186
  637.3 4.4 fusion.167
  641.7 93.2 %reduce-scatter.4.cloned.1.call-done = f32[2,80,768]{2,1,0:T(8,128)} async-done(((f32[2,1280,768]{2,1,0:T(8,128)}), f32[2,80,768]{2,1,0:T(8,128)}) %reduce-scatter.4.cloned.1.call-update) | async-done | bytes 491536 | tf_op jit(solution)/shard_map/reduce_scatter | solution.py:193
  736.9 4.1 all-to-all-start.1
  758.8 10.2 all_to_all.67
  770.0 56.2 %all-gather.10.cloned.1.call-done = bf16[2,1280,768]{2,1,0:T(8,128)(2,1)} async-done(((bf16[2,80,768]{2,1,0:T(8,128)(2,1)}), bf16[2,1280,768]{2,1,0:T(8,128)(2,1)}) %all-gather.10.cloned.1.call-update) | async-done | bytes 3932176 | tf_op jit(solution)/shard_map/all_gather | solution.py:213
  826.2 4.1 fusion.103
  831.3 4.4 fusion.173
  835.8 93.3 %reduce-scatter.6.cloned.1.call-done = f32[2,80,768]{2,1,0:T(8,128)} async-done(((f32[2,1280,768]{2,1,0:T(8,128)}), f32[2,80,768]{2,1,0:T(8,128)}) %reduce-scatter.6.cloned.1.call-update) | async-done | bytes 491536 | tf_op jit(solution)/shard_map/reduce_scatter | solution.py:227
  931.0 4.0 all-to-all-start.3
  935.2 5.9 all-to-all-done.3
  947.1 101.5 %while.43 = (s32[]{:T(128)}, f32[128,12,64]{0,2,1:T(8,128)S(1)}, f32[32,12]{0,1:T(8,128)S(1)}, f32[4,512,1536]{2,1,0:T(8,128)}, bf16[4,512,12,64]{1,3,2,0:T(8,12...) while((s32[]{:T(128)}, f32[128,12,64]{0,2,1:T(8,128)S(1)}, ...), condition=%wide.region_19.20_spmd.clone, body=%wide.region_18.19_spmd.clone.sunk | while | flops 868156800 | bytes 68705264 | solution.py:293
  962.8 5.5 fusion.270
  975.0 3.7 constant_dynamic-update-slice_fusion.2
  986.0 5.5 fusion.270
  998.2 3.9 constant_dynamic-update-slice_fusion.2
  1009.3 5.5 fusion.270
  1021.5 3.8 constant_dynamic-update-slice_fusion.2
  1032.7 5.5 fusion.270
  1044.9 3.7 constant_dynamic-update-slice_fusion.2
  1059.5 111.1 %reduce-scatter.8.cloned.1.call-done = f32[128,1536]{1,0:T(8,128)} async-done(((f32[2048,1536]{1,0:T(8,128)}), f32[128,1536]{1,0:T(8,128)}) %reduce-scatter.8.cloned.1.call-update) | async-done | bytes 786448 | tf_op jit(solution)/shard_map/reduce_scatter | solution.py:296
  1179.2 6.2 reshape_reshape.16
  1185.4 12.3 concatenate.10
  1197.8 8.5 pad.4
  1206.3 10.2 reshape.383
  1216.6 4.5 fusion.174
  1224.2 155.8 %all-reduce.5.cloned.1.call-done = f32[19456,128]{1,0:T(8,128)} async-done(((f32[19456,128]{1,0:T(8,128)}), f32[19456,128]{1,0:T(8,128)}) %all-reduce.5.cloned.1.call-update) | async-done | bytes 9961488
  (337 shorter events, 196.0 us)
Async XLA Ops:
  7.2 630.1 %copy-start = (bf16[2,192,768]{2,1,0:T(8,128)(2,1)S(1)}, bf16[2,192,768]{2,1,0:T(8,128)(2,1)}, u32[]{:S(2)}) copy-start(bf16[2,192,768]{2,1,0:T(8,128)(2,1)} %param.29) | copy-start | bytes 1769476
  7.2 316.5 %all-gather.12.cloned.1.call-start = ((), (), s32[]{:S(2)}) async-start(), calls=%async_computation.13 | async-start | bytes 6604800 | tf_op jit(solution)/shard_map/all_gather | solution.py:23
  10.3 406.6 %all-gather.6.cloned.1.call-start = ((), (), s32[]{:S(2)}) async-start(), calls=%async_computation.7 | async-start | bytes 6684672 | tf_op jit(solution)/shard_map/all_gather | solution.py:102
  11.9 403.1 %copy-start.36 = (f32[128]{0:T(128)}, f32[128]{0:T(128)S(1)}, u32[]{:S(2)}) copy-start(f32[128]{0:T(128)S(1)} %fusion.159) | copy-start | bytes 1540
  12.0 322.9 %copy-start.8 = (bf16[1,128,768]{2,1,0:T(8,128)(2,1)S(1)}, bf16[1,128,768]{2,1,0:T(8,128)(2,1)}, u32[]{:S(2)}) copy-start(bf16[1,128,768]{2,1,0:T(8,128)(2,1)} %param.18) | copy-start | bytes 589828
  333.6 4.4 copy-start.48
  333.6 81.1 %copy-start.29 = (s32[1,128,1]{1,2,0:T(1,128)S(1)}, s32[1,128,1]{1,2,0:T(1,128)}, u32[]{:S(2)}) copy-start(s32[1,128,1]{1,2,0:T(1,128)} %param.20) | copy-start | bytes 1540
  334.9 81.8 %copy-start.25 = (f32[768]{0:T(1024)}, f32[768]{0:T(1024)S(1)}, u32[]{:S(2)}) copy-start(f32[768]{0:T(1024)S(1)} %get-tuple-element.409) | copy-start | bytes 9220
  337.9 295.8 %all-gather.8.cloned.1.call-start = ((), (), s32[]{:S(2)}) async-start(), calls=%async_computation.8 | async-start | bytes 4177920 | tf_op jit(solution)/shard_map/all_gather | solution.py:186
  415.0 152.6 %copy-start.34 = (s32[128]{0:T(128)}, s32[128]{0:T(128)S(1)}, u32[]{:S(2)}) copy-start(s32[128]{0:T(128)S(1)} %multiply_add_fusion) | copy-start | bytes 1540
  565.1 14.9 %copy-start.15 = (bf16[128,12,64]{0,2,1:T(8,128)(2,1)}, bf16[128,12,64]{0,2,1:T(8,128)(2,1)S(1)}, u32[]{:S(2)}) copy-start(bf16[128,12,64]{0,2,1:T(8,128)(2,1)S(1)} %convert_element_type.281) | copy-start | bytes 589828
  566.9 374.6 %copy-start.7 = (f32[128,768]{1,0:T(8,128)}, f32[128,768]{1,0:T(8,128)S(1)}, u32[]{:S(2)}) copy-start(f32[128,768]{1,0:T(8,128)S(1)} %get-tuple-element.489) | copy-start | bytes 1179652
  567.6 12.4 copy-start.12
  580.0 154.9 %reduce-scatter.4.cloned.1.call-start = ((), (), s32[]{:S(2)}) async-start(), calls=%async_computation.9 | async-start | bytes 8355840 | tf_op jit(solution)/shard_map/reduce_scatter | solution.py:193
  637.3 188.9 %copy-start.5 = (f32[2,1280,192]{1,2,0:T(8,128)}, f32[2,1280,192]{1,2,0:T(8,128)S(1)}, u32[]{:S(2)}) copy-start(f32[2,1280,192]{1,2,0:T(8,128)S(1)} %fusion.172) | copy-start | bytes 5898244
  736.9 10.3 all-to-all-start.1
  741.0 85.2 %all-gather.10.cloned.1.call-start = ((), (), s32[]{:S(2)}) async-start(), calls=%async_computation.10 | async-start | bytes 4177920 | tf_op jit(solution)/shard_map/all_gather | solution.py:213
  770.0 159.1 %reduce-scatter.6.cloned.1.call-start = ((), (), s32[]{:S(2)}) async-start(), calls=%async_computation.11 | async-start | bytes 8355840 | tf_op jit(solution)/shard_map/reduce_scatter | solution.py:227
  826.2 5.1 copy-start.14
  835.7 105.6 %copy-start.35 = (s32[128]{0:T(128)S(1)}, s32[128]{0:T(128)}, u32[]{:S(2)}) copy-start(s32[128]{0:T(128)} %copy-done.34) | copy-start | bytes 1540
  835.7 105.8 %copy-start.24 = (f32[128,16]{0,1:T(8,128)S(1)}, f32[128,16]{0,1:T(8,128)}, u32[]{:S(2)}) copy-start(f32[128,16]{0,1:T(8,128)} %copy-done.23) | copy-start | bytes 24580
  835.7 105.8 %copy-start.28 = (f32[128]{0:T(128)S(1)}, f32[128]{0:T(128)}, u32[]{:S(2)}) copy-start(f32[128]{0:T(128)} %copy-done.27) | copy-start | bytes 1540
  835.7 105.8 %copy-start.30 = (s32[1,128,1]{1,2,0:T(1,128)S(1)}, s32[1,128,1]{1,2,0:T(1,128)}, u32[]{:S(2)}) copy-start(s32[1,128,1]{1,2,0:T(1,128)} %param.20) | copy-start | bytes 1540
  835.8 105.8 %copy-start.32 = (f32[128]{0:T(128)S(1)}, f32[128]{0:T(128)}, u32[]{:S(2)}) copy-start(f32[128]{0:T(128)} %copy-done.31) | copy-start | bytes 1540
  835.8 105.8 %copy-start.33 = (f32[128]{0:T(128)S(1)}, f32[128]{0:T(128)}, u32[]{:S(2)}) copy-start(f32[128]{0:T(128)} %fusion.151) | copy-start | bytes 1540
  835.8 105.8 %copy-start.38 = (f32[128]{0:T(128)S(1)}, f32[128]{0:T(128)}, u32[]{:S(2)}) copy-start(f32[128]{0:T(128)} %get-tuple-element.414) | copy-start | bytes 1540
  835.8 105.8 %copy-start.42 = (f32[128]{0:T(128)S(1)}, f32[128]{0:T(128)}, u32[]{:S(2)}) copy-start(f32[128]{0:T(128)} %copy-done.41) | copy-start | bytes 1540
  835.8 107.3 %copy-start.46 = (f32[128]{0:T(128)S(1)}, f32[128]{0:T(128)}, u32[]{:S(2)}) copy-start(f32[128]{0:T(128)} %copy-done.45) | copy-start | bytes 1540
  835.8 107.3 %copy-start.17 = (bf16[1,128,768]{2,1,0:T(8,128)(2,1)S(1)}, bf16[1,128,768]{2,1,0:T(8,128)(2,1)}, u32[]{:S(2)}) copy-start(bf16[1,128,768]{2,1,0:T(8,128)(2,1)} %param.19) | copy-start | bytes 589828
  835.8 107.3 %copy-start.18 = (f32[128,768]{1,0:T(8,128)S(1)}, f32[128,768]{1,0:T(8,128)}, u32[]{:S(2)}) copy-start(f32[128,768]{1,0:T(8,128)} %get-tuple-element.491) | copy-start | bytes 1179652
  835.8 107.3 %copy-start.40 = (f32[128]{0:T(128)S(1)}, f32[128]{0:T(128)}, u32[]{:S(2)}) copy-start(f32[128]{0:T(128)} %copy-done.39) | copy-start | bytes 1540
  931.0 10.1 all-to-all-start.3
  935.1 235.5 %reduce-scatter.8.cloned.1.call-start = ((), (), s32[]{:S(2)}) async-start(), calls=%async_computation.12 | async-start | bytes 13369344 | tf_op jit(solution)/shard_map/reduce_scatter | solution.py:296
  955.4 3.2 copy-start.2
  978.7 3.2 copy-start.2
  1002.0 3.2 copy-start.2
  1048.6 331.3 %all-reduce.5.cloned.1.call-start = ((), (), s32[]{:S(2)}) async-start(), calls=%async_computation.14 | async-start | bytes 19922944
  1053.3 3.9 copy-start.9
  1053.3 3.9 copy-start.26
  1053.3 3.9 copy-start.37
  1170.6 5.6 copy-start.11
  1179.2 6.2 copy-start.4
  1179.2 6.2 copy-start.20
  1179.2 6.2 copy-start.21
  1179.2 6.2 copy-start.22
  1216.5 4.5 copy-start.6
  1216.6 4.5 copy-start.47
  1221.1 165.1 %copy-start.1 = (bf16[2,192,768]{2,1,0:T(8,128)(2,1)S(1)}, bf16[2,192,768]{2,1,0:T(8,128)(2,1)}, u32[]{:S(2)}) copy-start(bf16[2,192,768]{2,1,0:T(8,128)(2,1)} %param.29) | copy-start | bytes 1769476
  (17 other events, 28.7 us)
Sparse Core Ops, SparseCore 0:
  10.4 313.2 all-gather.11
  338.0 65.0 all-gather.5
  580.1 53.4 all-gather.7
  641.8 93.0 reduce-scatter.3
  770.1 56.0 all-gather.9
  835.8 93.2 reduce-scatter.5
  1048.7 121.8 reduce-scatter.7
  1216.7 163.2 all-reduce.4
where the time goes:
time: 1400 us; the launch traced here: 1390 us
  waiting for transfers between devices  884 us (63%)
  local copies, waits for them, and re-layouts  190 us (14%)
  matrix products  156 us (11%)
  blocking collectives  97.5 us (7%)
  other arithmetic  23.2 us (2%)
  loops' own time  18.4 us (1%)
  between operations  15.2 us (1%)
    all_gather x1, waiting for transfers between devices, side_by_side(): filled = lax.all_gather(both, axis, axis=dim, tiled=True)  312 us
    unnamed x9, waiting for transfers between devices  156 us
    reduce_scatter x1, waiting for transfers between devices, shards(): lax.psum_scatter(kv_terms.reshape(seq_length, 2 * model_width), 'ctx', sc...  111 us
    reduce_scatter x1, waiting for transfers between devices, shards(): lax.psum_scatter(partial_back, 'ctx', scatter_dimension=1, tiled=True)  93.3 us
    reduce_scatter x1, waiting for transfers between devices, shards(): lax.psum_scatter(partial_value, 'ctx', scatter_dimension=1, tiled=True)  93.2 us
    unnamed x1, blocking collectives  76.2 us
    all_gather x1, waiting for transfers between devices, shards(): grad_rows_y = lax.all_gather(grad_received, 'ctx', axis=1, tiled=True)  56.2 us
    all_gather x1, waiting for transfers between devices, shards(): rows_all = lax.all_gather(received, 'ctx', axis=1, tiled=True)  53.6 us
  transfers between devices with their start and end apart: 10, of which 9 were waited for; matrix products, arithmetic and copies ran while one was open for 2% of the time, Pallas kernels for 0%

commit v1 on v0

v1 whole, which is shorter than its diff:
```python
import functools

import jax
import jax.numpy as jnp
from jax import lax
from jax.experimental import pallas as pl
from jax.experimental.pallas import tpu as pltpu
from jax.sharding import PartitionSpec as P

MESH = pl.DeviceIdType.MESH
HEADS = 12
HEAD_DIM = 64
BUCKETS = 32
TOK = 128
D = 768
CAP = 10
SLOTS = 48
CTX, EXP, ZED = 16, 8, 4
LEN = TOK * CTX
QUERIES = 256
CHUNK = 128
epsilon = 1e-06
bucket_edges = (12, 16, 23, 32, 46, 64, 91)
low = jnp.bfloat16
wide = jnp.float32
ANY = pl.BlockSpec(memory_space=pl.ANY)


def spot():
    c, e = lax.axis_index("ctx"), lax.axis_index("exp")
    return c, e, c // 4, (c // 2) % 2, c % 2


def greet(peers):
    barrier = pltpu.get_barrier_semaphore()
    for peer in peers:
        pl.semaphore_signal(barrier, inc=1, device_id=peer, device_id_type=MESH)
    pl.semaphore_wait(barrier, len(peers))


def push(src, dst, send, recv, to):
    return pltpu.make_async_remote_copy(
        src_ref=src, dst_ref=dst, send_sem=send, recv_sem=recv, device_id=to, device_id_type=MESH
    )


def group(kind):
    c, e, z, xh, k = spot()
    if kind == "exp":
        return EXP, e, lambda i: (c, i)
    if kind == "z":
        return ZED, z, lambda i: (i * 4 + xh * 2 + k, e)
    if kind == "x":
        return 2, xh, lambda i: (z * 4 + i * 2 + k, e)
    return 2, k, lambda i: (z * 4 + xh * 2 + i, e)


def swap_kernel(kind, axis, x, out, here, send, recv):
    size, me, device = group(kind)
    part = (lambda i: x) if axis is None else (lambda i: x.at[(slice(None),) * axis + (i,)])
    peers = [lax.rem(me + i, size) for i in range(1, size)]
    greet([device(p) for p in peers])
    copies = [
        push(part(p), out.at[me], send.at[i], recv.at[i], device(p)) for i, p in enumerate(peers)
    ]
    for copy in copies:
        copy.start()
    own = pltpu.make_async_copy(part(me), out.at[me], here)
    own.start()
    for copy in copies:
        copy.wait()
    own.wait()


def swap(x, kind, ident, axis=None):
    size = {"exp": EXP, "z": ZED, "x": 2, "core": 2}[kind]
    block = x.shape if axis is None else x.shape[:axis] + x.shape[axis + 1 :]
    return pl.pallas_call(
        functools.partial(swap_kernel, kind, axis),
        out_shape=jax.ShapeDtypeStruct((size, *block), x.dtype),
        in_specs=[ANY],
        out_specs=ANY,
        scratch_shapes=[
            pltpu.SemaphoreType.DMA,
            pltpu.SemaphoreType.DMA((size - 1,)),
            pltpu.SemaphoreType.DMA((size - 1,)),
        ],
        compiler_params=pltpu.CompilerParams(collective_id=ident, has_side_effects=True),
    )(x)


def weights_kernel(x, out, here, send, recv):
    c, e, z, xh, k = spot()
    zs = [lax.rem(z + i, 4) for i in range(1, 4)]
    back = [lax.rem(z + 4 - i, 4) for i in range(1, 4)]
    at = lambda z, xh, k: z * 4 + xh * 2 + k
    side, twin = (at(z, 1 - xh, k), e), (at(z, xh, 1 - k), e)
    rows = [(at(p, xh, k), e) for p in zs]
    greet([side, twin, *rows])
    mine, theirs = at(z, xh, k), at(z, 1 - xh, k)
    across = push(x, out.at[mine], send.at[0], recv.at[0], side)
    across.start()
    first = [push(x, out.at[mine], send.at[1 + i], recv.at[1 + i], d) for i, d in enumerate(rows)]
    for copy in first:
        copy.start()
    own = pltpu.make_async_copy(x, out.at[mine], here)
    own.start()
    pair = [push(x, out.at[mine], send.at[7], recv.at[7], twin)]
    pair[0].start()

    def hand(n, block):
        copy = push(out.at[block], out.at[block], send.at[7 + n], recv.at[7 + n], twin)
        copy.start()
        pair.append(copy)

    across.wait_recv()
    second = [
        push(out.at[theirs], out.at[theirs], send.at[4 + i], recv.at[4 + i], d)
        for i, d in enumerate(rows)
    ]
    for copy in second:
        copy.start()
    hand(1, theirs)
    for i, p in enumerate(back):
        first[i].wait_recv()
        hand(2 + i, at(p, xh, k))
    for i, p in enumerate(back):
        second[i].wait_recv()
        hand(5 + i, at(p, 1 - xh, k))
    for copy in pair:
        copy.wait()
    across.wait_send()
    for copy in first + second:
        copy.wait_send()
    own.wait()


def gather_weights(x, ident):
    return pl.pallas_call(
        weights_kernel,
        out_shape=jax.ShapeDtypeStruct((CTX, *x.shape), x.dtype),
        in_specs=[ANY],
        out_specs=ANY,
        scratch_shapes=[
            pltpu.SemaphoreType.DMA,
            pltpu.SemaphoreType.DMA((15,)),
            pltpu.SemaphoreType.DMA((15,)),
        ],
        compiler_params=pltpu.CompilerParams(collective_id=ident, has_side_effects=True),
    )(x)


def quad_kernel(x, out, here, send, recv):
    c, e, z, xh, k = spot()
    at = lambda xh, k: z * 4 + xh * 2 + k
    side, twin = (at(1 - xh, k), e), (at(xh, 1 - k), e)
    mine, theirs = xh * 2 + k, (1 - xh) * 2 + k
    greet([side, twin])
    across = push(x, out.at[:, :, mine], send.at[0], recv.at[0], side)
    across.start()
    pair = push(x, out.at[:, :, mine], send.at[1], recv.at[1], twin)
    pair.start()
    own = pltpu.make_async_copy(x, out.at[:, :, mine], here)
    own.start()
    across.wait_recv()
    hand = push(out.at[:, :, theirs], out.at[:, :, theirs], send.at[2], recv.at[2], twin)
    hand.start()
    across.wait_send()
    pair.wait()
    hand.wait()
    own.wait()


def gather_experts(x, ident):
    return pl.pallas_call(
        quad_kernel,
        out_shape=jax.ShapeDtypeStruct((2, 2, 4, *x.shape[2:]), x.dtype),
        in_specs=[ANY],
        out_specs=ANY,
        scratch_shapes=[
            pltpu.SemaphoreType.DMA,
            pltpu.SemaphoreType.DMA((3,)),
            pltpu.SemaphoreType.DMA((3,)),
        ],
        compiler_params=pltpu.CompilerParams(collective_id=ident, has_side_effects=True),
    )(x)


def head_of(c):
    return jnp.minimum((c // 4) * 3 + c % 4, HEADS - 1)


def owns(c):
    return c % 4 < 3


def columns(c):
    return pl.ds(pl.multiple_of(c * TOK, TOK), TOK)


def to_heads_kernel(x, out, here, send, recv):
    c, e, z, xh, k = spot()
    peers = [lax.rem(c + i, CTX) for i in range(1, CTX)]
    greet([(p, e) for p in peers])
    copies = [
        push(x.at[:, head_of(p)], out.at[:, :, columns(c)], send.at[i], recv.at[i], (p, e))
        for i, p in enumerate(peers)
    ]
    own = pltpu.make_async_copy(x.at[:, head_of(c)], out.at[:, :, columns(c)], here)
    for p, copy in zip(peers, copies):
        pl.when(owns(p))(copy.start)
    pl.when(owns(c))(own.start)
    for p, copy in zip(peers, copies):
        pl.when(owns(p))(copy.wait_send)
        pl.when(owns(c))(copy.wait_recv)
    pl.when(owns(c))(own.wait)


def from_heads_kernel(x, out, here, send, recv):
    c, e, z, xh, k = spot()
    peers = [lax.rem(c + i, CTX) for i in range(1, CTX)]
    sources = [lax.rem(c + CTX - i, CTX) for i in range(1, CTX)]
    greet([(p, e) for p in peers])
    copies = [
        push(x.at[:, :, columns(p)], out.at[:, head_of(c)], send.at[i], recv.at[i], (p, e))
        for i, p in enumerate(peers)
    ]
    own = pltpu.make_async_copy(x.at[:, :, columns(c)], out.at[:, head_of(c)], here)

    @pl.when(owns(c))
    def _():
        for copy in copies:
            copy.start()
        own.start()

    for s, copy in zip(sources, copies):
        pl.when(owns(c))(copy.wait_send)
        pl.when(owns(s))(copy.wait_recv)
    pl.when(owns(c))(own.wait)


def heads_call(kernel, x, shape, ident):
    return pl.pallas_call(
        kernel,
        out_shape=jax.ShapeDtypeStruct(shape, x.dtype),
        in_specs=[ANY],
        out_specs=ANY,
        scratch_shapes=[
            pltpu.SemaphoreType.DMA,
            pltpu.SemaphoreType.DMA((CTX - 1,)),
            pltpu.SemaphoreType.DMA((CTX - 1,)),
        ],
        compiler_params=pltpu.CompilerParams(collective_id=ident, has_side_effects=True),
    )(x)


def to_heads(x, ident):
    return heads_call(to_heads_kernel, x, (x.shape[0], HEAD_DIM, LEN), ident)


def from_heads(x, ident):
    return heads_call(from_heads_kernel, x, (x.shape[0], HEADS, HEAD_DIM, TOK), ident)


def near_buckets():
    shape = (6 * CHUNK, QUERIES)
    offset = (
        lax.broadcasted_iota(jnp.int32, shape, 0)
        - 2 * CHUNK
        - lax.broadcasted_iota(jnp.int32, shape, 1)
    )
    distance = jnp.abs(offset)
    far = jnp.full(shape, 8, jnp.int32)
    for edge in bucket_edges:
        far = far + (distance >= edge).astype(jnp.int32)
    return jnp.where(distance < 8, distance, far) + jnp.where(offset > 0, BUCKETS // 2, 0)


def tile_rows(chunk, block):
    tile = jnp.clip(chunk - 2 * block + 2, 0, 5)
    return pl.ds(pl.multiple_of(tile * CHUNK, CHUNK), CHUNK)


def chunk_rows(chunk):
    return pl.ds(pl.multiple_of(chunk * CHUNK, CHUNK), CHUNK)


def forward_kernel(qkv_ref, table_ref, p_ref, o_ref, low_ref, inv_ref, keys, bias, scores):
    block = pl.program_id(0)

    @pl.when(block == 0)
    def _():
        keys[...] = qkv_ref[1].T
        ids = near_buckets()
        tiles = jnp.zeros(ids.shape, wide)
        for b in range(BUCKETS):
            tiles = jnp.where(ids == b, table_ref[b], tiles)
        bias[...] = tiles

    here = pl.ds(pl.multiple_of(block * QUERIES, QUERIES), QUERIES)
    queries = qkv_ref[0, :, here]

    def score(chunk, top):
        rows = chunk_rows(chunk)
        part = jnp.dot(keys[rows, :], queries, preferred_element_type=wide)
        part = part + bias[tile_rows(chunk, block), :]
        scores[rows, :] = part
        return jnp.maximum(top, jnp.max(part.reshape(CHUNK // 8, 8, QUERIES), axis=0))

    top = lax.fori_loop(
        0, LEN // CHUNK, score, jnp.full((8, QUERIES), -1e30, wide), unroll=2
    )
    top = jnp.max(top, axis=0, keepdims=True)

    def weigh(chunk, total):
        rows = chunk_rows(chunk)
        part = jnp.exp(scores[rows, :] - top)
        p_ref[rows, :] = part.astype(low)
        return total + jnp.sum(part.reshape(CHUNK // 8, 8, QUERIES), axis=0)

    total = lax.fori_loop(0, LEN // CHUNK, weigh, jnp.zeros((8, QUERIES), wide), unroll=2)
    inverse = 1.0 / jnp.sum(total, axis=0, keepdims=True)
    out = jnp.dot(qkv_ref[2], p_ref[...], preferred_element_type=wide) * inverse
    o_ref[...] = out
    low_ref[0] = out.astype(low)
    inv_ref[...] = inverse


def attend(qkv, table):
    whole = lambda *shape: pl.BlockSpec(shape, lambda i: (0,) * len(shape))
    return pl.pallas_call(
        forward_kernel,
        grid=(LEN // QUERIES,),
        out_shape=(
            jax.ShapeDtypeStruct((LEN, LEN), low),
            jax.ShapeDtypeStruct((HEAD_DIM, LEN), wide),
            jax.ShapeDtypeStruct((1, HEAD_DIM, LEN), low),
            jax.ShapeDtypeStruct((1, LEN), wide),
        ),
        in_specs=[whole(3, HEAD_DIM, LEN), pl.BlockSpec(memory_space=pltpu.SMEM)],
        out_specs=(
            pl.BlockSpec((LEN, QUERIES), lambda i: (0, i)),
            pl.BlockSpec((HEAD_DIM, QUERIES), lambda i: (0, i)),
            pl.BlockSpec((1, HEAD_DIM, QUERIES), lambda i: (0, 0, i)),
            pl.BlockSpec((1, QUERIES), lambda i: (0, i)),
        ),
        scratch_shapes=[
            pltpu.VMEM((LEN, HEAD_DIM), low),
            pltpu.VMEM((6 * CHUNK, QUERIES), wide),
            pltpu.VMEM((LEN, QUERIES), wide),
        ],
        compiler_params=pltpu.CompilerParams(vmem_limit_bytes=32 << 20),
    )(qkv, table)


def backward_kernel(
    qkv_ref, p_ref, o_ref, inv_ref, do_ref, grad_ref, sums_ref, values, dk, dv, tiles, slopes
):
    block = pl.program_id(0)

    @pl.when(block == 0)
    def _():
        values[...] = qkv_ref[2].T
        dk[...] = jnp.zeros(dk.shape, wide)
        dv[...] = jnp.zeros(dv.shape, wide)
        tiles[...] = jnp.zeros(tiles.shape, wide)

    here = pl.ds(pl.multiple_of(block * QUERIES, QUERIES), QUERIES)
    scaled = (do_ref[0].astype(wide) * inv_ref[...]).astype(low)
    delta = jnp.sum(scaled.astype(wide) * o_ref[...], axis=0, keepdims=True)

    def slope(chunk, carry):
        rows = chunk_rows(chunk)
        part = jnp.dot(values[rows, :], scaled, preferred_element_type=wide)
        part = p_ref[rows, :].astype(wide) * (part - delta)
        slopes[rows, :] = part.astype(low)
        near = tile_rows(chunk, block)
        tiles[near, :] = tiles[near, :] + part
        return carry

    lax.fori_loop(0, LEN // CHUNK, slope, 0, unroll=2)
    grad_ref[0, :, here] = jnp.dot(
        qkv_ref[1], slopes[...], preferred_element_type=wide
    ).astype(low)
    queries = qkv_ref[0, :, here].T
    turned = scaled.T

    def gather(chunk, carry):
        rows = pl.ds(pl.multiple_of(chunk * 512, 512), 512)
        dk[rows, :] = dk[rows, :] + jnp.dot(
            slopes[rows, :], queries, preferred_element_type=wide
        )
        dv[rows, :] = dv[rows, :] + jnp.dot(p_ref[rows, :], turned, preferred_element_type=wide)
        return carry

    lax.fori_loop(0, LEN // 512, gather, 0)

    @pl.when(block == LEN // QUERIES - 1)
    def _():
        grad_ref[1] = dk[...].T.astype(low)
        grad_ref[2] = dv[...].T.astype(low)
        sums_ref[...] = tiles[...]


def attend_back(qkv, probs, out, inverse, grad_out):
    whole = lambda *shape: pl.BlockSpec(shape, lambda i: (0,) * len(shape))
    return pl.pallas_call(
        backward_kernel,
        grid=(LEN // QUERIES,),
        out_shape=(
            jax.ShapeDtypeStruct((3, HEAD_DIM, LEN), low),
            jax.ShapeDtypeStruct((6 * CHUNK, QUERIES), wide),
        ),
        in_specs=[
            whole(3, HEAD_DIM, LEN),
            pl.BlockSpec((LEN, QUERIES), lambda i: (0, i)),
            pl.BlockSpec((HEAD_DIM, QUERIES), lambda i: (0, i)),
            pl.BlockSpec((1, QUERIES), lambda i: (0, i)),
            pl.BlockSpec((1, HEAD_DIM, QUERIES), lambda i: (0, 0, i)),
        ],
        out_specs=(whole(3, HEAD_DIM, LEN), whole(6 * CHUNK, QUERIES)),
        scratch_shapes=[
            pltpu.VMEM((LEN, HEAD_DIM), low),
            pltpu.VMEM((LEN, HEAD_DIM), wide),
            pltpu.VMEM((LEN, HEAD_DIM), wide),
            pltpu.VMEM((6 * CHUNK, QUERIES), wide),
            pltpu.VMEM((LEN, QUERIES), low),
        ],
        compiler_params=pltpu.CompilerParams(vmem_limit_bytes=32 << 20),
    )(qkv, probs, out, inverse, grad_out)


def rms_scale(values_in, gain_vec):
    return (
        values_in
        * lax.rsqrt(jnp.mean(values_in * values_in, axis=-1, keepdims=True) + epsilon)
        * gain_vec
    )


def dot(a, b, dims=(1, 0)):
    return lax.dot_general(
        a, b, (((dims[0],), (dims[1],)), ((), ())), preferred_element_type=wide
    )


def shards(
    tokens,
    cotangent,
    routes,
    query_weight,
    kv_weight,
    out_weight,
    norm_gain_one,
    norm_gain_two,
    router_weight,
    bias_table,
    expert_in,
    expert_out,
):
    highest = lax.Precision.HIGHEST
    experts = 16
    x_rows = tokens[0].astype(wide)
    c = lax.axis_index("ctx")

    matrix = jnp.concatenate([query_weight, kv_weight, out_weight], axis=1).reshape(16, 1152)
    small = jnp.concatenate(
        [
            router_weight,
            norm_gain_one[:, None],
            norm_gain_two[:, None],
            jnp.pad(bias_table, (0, 3))[:, None],
        ],
        axis=1,
    ).reshape(1, 114)
    packed = jnp.concatenate([matrix, jnp.pad(small, ((0, 15), (0, 14)))], axis=1)
    eight = swap(packed, "exp", 1)
    block = jnp.concatenate(
        [
            eight[:, :, :1152].reshape(48, 4 * D),
            jnp.pad(eight[:, 0, 1152:1266].reshape(48, 19), ((0, 0), (0, 109))),
        ],
        axis=1,
    )
    full = gather_weights(block, 2).reshape(D, 4 * D + 128)
    experts_here = gather_experts(
        jnp.stack([jnp.swapaxes(expert_in, 1, 2), expert_out]), 3
    ).reshape(2, 2, D, D)
    qkv_full = full[:, : 3 * D]
    out_full = full[:, 3 * D : 4 * D]
    router_wide = full[:, 4 * D : 4 * D + 16].astype(wide)
    gain_one = full[:, 4 * D + 16].astype(wide)
    gain_two = full[:, 4 * D + 17].astype(wide)
    table = full[:, 4 * D + 18].astype(wide).reshape(128, 6)[:, :3].reshape(BUCKETS, HEADS)
    head = head_of(c)
    my_head = (jnp.arange(HEADS, dtype=jnp.int32) == head) & owns(c)
    head_table = jnp.sum(jnp.where(my_head[None, :], table, 0.0), axis=1)

    normed_one, norm_one_back = jax.vjp(rms_scale, x_rows, gain_one)
    h_one = normed_one.astype(low)
    qkv = dot(qkv_full, h_one, (0, 1)).astype(low).reshape(3, HEADS, HEAD_DIM, TOK)
    head_qkv = to_heads(qkv, 4)
    probs, attended, attended_head, inverse = attend(head_qkv, head_table)
    attended_low = from_heads(attended_head, 5).reshape(D, TOK)
    residual = x_rows + dot(attended_low, out_full, (0, 0))
    normed_two, norm_two_back = jax.vjp(rms_scale, residual, gain_two)
    h_two = normed_two.astype(low)
    h_two_wide = h_two.astype(wide)
    route_probs = jax.nn.softmax(jnp.dot(h_two_wide, router_wide, precision=highest), axis=-1)

    route_ids = routes[0, :, 0]
    choose = route_ids[:, None] == jnp.arange(experts, dtype=jnp.int32)[None, :]
    choose_wide = choose.astype(wide)
    index = jnp.arange(TOK, dtype=jnp.int32)
    before = (index[None, :] < index[:, None]).astype(low)
    earlier = dot(before, choose.astype(low))
    slot = jnp.sum(earlier * choose_wide, axis=1).astype(jnp.int32)
    target = route_ids // 2 * SLOTS + route_ids % 2 * CAP + slot
    target = jnp.concatenate([target, target + 2 * CAP])
    dispatch = (
        jnp.arange(EXP * SLOTS, dtype=jnp.int32)[:, None] == target[None, :]
    ).astype(low)
    gate_value = jnp.sum(route_probs * choose_wide, axis=1)
    grad_out = cotangent[0].astype(wide)
    grad_y = (gate_value[:, None] * grad_out).astype(low)
    outgoing = dot(dispatch, jnp.concatenate([h_two, grad_y])).astype(low)
    received = swap(outgoing.reshape(EXP, SLOTS, D), "exp", 6, 0).reshape(EXP * SLOTS, D)

    row = jnp.arange(4 * 80, dtype=jnp.int32)
    source = row % 80 // CAP * SLOTS + row // 80 * CAP + row % CAP
    compact = (source[:, None] == jnp.arange(EXP * SLOTS, dtype=jnp.int32)[None, :]).astype(low)
    lists = swap(dot(compact, received).astype(low), "z", 7).reshape(ZED, 4, 80, D)
    partial, grads_in, grads_out = [], [], []
    for n in range(2):
        rows = lists[:, n].reshape(ZED * 80, D)
        grads = lists[:, 2 + n].reshape(ZED * 80, D)
        weight_in, weight_out = experts_here[0, n], experts_here[1, n]
        pre_act = dot(rows, weight_in, (1, 1))
        hidden_wide, gelu_back = jax.vjp(jax.nn.gelu, pre_act)
        hidden = hidden_wide.astype(low)
        grad_hidden = dot(grads, weight_out, (1, 1))
        grad_pre = gelu_back(grad_hidden)[0].astype(low)
        partial.append(dot(hidden, weight_out).astype(low).reshape(ZED, 80, D))
        partial.append(dot(grad_pre, weight_in).astype(low).reshape(ZED, 80, D))
        grads_in.append(dot(grad_pre, rows, (0, 0)).astype(low))
        grads_out.append(dot(hidden, grads, (0, 0)).astype(low))
    partial = jnp.stack([partial[0], partial[2], partial[1], partial[3]], axis=1)
    summed = jnp.sum(
        swap(partial.reshape(ZED, 320, D), "z", 8, 0).astype(wide), axis=0
    ).astype(low)
    back = swap(dot(compact, summed, (0, 0)).astype(low).reshape(EXP, SLOTS, D), "exp", 9, 0)
    returned = dot(dispatch, back.reshape(EXP * SLOTS, D), (0, 0))
    expert_tokens, grad_h_two = returned[:TOK], returned[TOK:]

    mixed_rows = (residual + gate_value[:, None] * expert_tokens).astype(low)
    grad_gate = jnp.sum(grad_out * expert_tokens, axis=1)
    grad_choice = choose_wide * grad_gate[:, None]
    grad_logits = route_probs * (
        grad_choice - jnp.sum(route_probs * grad_choice, axis=1, keepdims=True)
    )
    grad_router = jnp.dot(h_two_wide.T, grad_logits, precision=highest)
    grad_h_two = grad_h_two + jnp.dot(grad_logits, router_wide.T, precision=highest)
    grad_resid_norm, grad_gain_two = norm_two_back(grad_h_two)
    grad_residual = grad_out + grad_resid_norm
    grad_branch = grad_residual.astype(low)
    grad_attended = dot(out_full, grad_branch, (1, 1)).astype(low)
    head_grad = to_heads(grad_attended.reshape(1, HEADS, HEAD_DIM, TOK), 10)
    head_grads, tile_sums = attend_back(head_qkv, probs, attended, inverse, head_grad)
    grad_qkv = from_heads(head_grads, 11).reshape(3 * D, TOK)

    expert_grads = jnp.stack([jnp.stack(grads_in), jnp.stack(grads_out)])
    expert_grads = swap(expert_grads.reshape(2, 2, 2, 2, 192, D), "core", 12, 3)
    expert_grads = jnp.sum(expert_grads.astype(wide), axis=0).astype(low)
    expert_grads = jnp.sum(swap(expert_grads, "x", 13, 2).astype(wide), axis=0)
    grad_expert_in = jnp.swapaxes(expert_grads[0], 1, 2)
    grad_expert_out = expert_grads[1]

    grad_h_one = dot(grad_qkv, qkv_full, (0, 1))
    grad_x_norm, grad_gain_one = norm_one_back(grad_h_one)
    grad_tokens = grad_residual + grad_x_norm
    bucket_sums = jnp.sum(
        jnp.where(
            near_buckets()[None] == jnp.arange(BUCKETS, dtype=jnp.int32)[:, None, None],
            tile_sums[None],
            0.0,
        ),
        axis=(1, 2),
    )
    grad_table = jnp.where(my_head[None, :], bucket_sums[:, None], 0.0)
    table_column = jnp.pad(grad_table.reshape(128, 3), ((0, 0), (0, 3))).reshape(D, 1)
    shared = jnp.concatenate(
        [
            dot(h_one, grad_qkv, (0, 1)).astype(low),
            dot(attended_low, grad_branch).astype(low),
            grad_router.astype(low),
            grad_gain_one[:, None].astype(low),
            grad_gain_two[:, None].astype(low),
            table_column.astype(low),
            jnp.zeros((D, 109), low),
        ],
        axis=1,
    )
    total = lambda v: jnp.sum(v.astype(wide), axis=0)
    shared = total(swap(shared.reshape(8, 2, 48, 3200), "core", 14, 1)).astype(low)
    shared = total(swap(shared.reshape(4, 2, 48, 3200), "z", 15, 0)).astype(low)
    shared = total(swap(shared, "x", 16, 0)).astype(low)
    lines = jnp.concatenate(
        [
            shared[:, : 4 * D].reshape(EXP, 16, 1152),
            jnp.pad(
                shared[:, 4 * D : 4 * D + 19].reshape(EXP, 1, 114), ((0, 0), (0, 15), (0, 14))
            ),
        ],
        axis=2,
    )
    lines = total(swap(lines, "exp", 17, 0))
    matrix = lines[:, :1152].reshape(6, 4 * D)
    small = lines[0, 1152:1266].reshape(6, 19)
    return (
        mixed_rows[None],
        grad_tokens[None],
        matrix[:, :D],
        matrix[:, D : 3 * D],
        matrix[:, 3 * D :],
        small[:, 16],
        small[:, 17],
        small[:, :16],
        small[:3, 18],
        grad_expert_in,
        grad_expert_out,
    )


def solution(mesh):
    rows = P("exp", "ctx", None)
    shared, vector = P(("ctx", "exp"), None), P(("ctx", "exp"))
    expert_in, expert_out = P("exp", None, "ctx"), P("exp", "ctx", None)
    return jax.shard_map(
        shards,
        mesh=mesh,
        in_specs=(rows, rows, rows, shared, shared, shared, vector, vector, shared, vector)
        + (expert_in, expert_out),
        out_specs=(rows, rows, shared, shared, shared, vector, vector, shared, vector)
        + (expert_in, expert_out),
        check_vma=False,
    )
```

time: 1400 us -> 607 us (0.43)
  waiting for transfers between devices: 884 us -> 0 us
  Pallas kernels: 0 us -> 489 us
  local copies, waits for them, and re-layouts: 190 us -> 35.1 us
  matrix products: 156 us -> 37.8 us
  blocking collectives: 97.5 us -> 0 us
  loops' own time: 18.4 us -> 0 us
    pallas_call x0 -> x19, Pallas kernels: none -> 489 us  [the longest x11 319 us: swap(): pl.pallas_call(functools.partial(swap_kernel, kind, axis), out_shape=jax....]
    all_gather x4 -> x0, waiting for transfers between devices: 421 us -> none  [the longest x1 312 us: side_by_side(): filled = lax.all_gather(both, axis, axis=dim, tiled=True)]
    reduce_scatter x3 -> x0, waiting for transfers between devices: 298 us -> none  [the longest x1 111 us: shards(): lax.psum_scatter(kv_terms.reshape(seq_length, 2 * model_width), 'ctx', sc...]
    unnamed x9 -> x0, waiting for transfers between devices: 156 us -> none
    dot_general x71 -> x23, matrix products: 152 us -> 34.9 us  [dot(): lax.dot_general(a, b, (((dims[0],), (dims[1],)), ((), ())), preferred_ele...]
    unnamed x1 -> x0, blocking collectives: 76.2 us -> none
    dot_general x8 -> x0, local copies, waits for them, and re-layouts: 39.1 us -> none  [block_scores(): jnp.einsum('uri,uj->jri', bucket_indicator, position_bias_matrix, preferr...]
    reshape x17 -> x6, local copies, waits for them, and re-layouts: 32.3 us -> 0.97 us  [the longest x1 0.36 us: shards(): eight[:, :, :1152].reshape(48, 4 * D)]
  transfers between devices with their start and end apart: 10 -> 0, of which waited for: 9 -> 0; matrix products, arithmetic and copies ran while one was open for 2% -> 0% of each run, Pallas kernels for 0% -> 0%
where the time goes in v1:
time: 607 us; the launch traced here: 600 us
  Pallas kernels  489 us (81%)
  matrix products  37.8 us (6%)
  other arithmetic  36.4 us (6%)
  local copies, waits for them, and re-layouts  35.1 us (6%)
    pallas_call x11, Pallas kernels, swap(): pl.pallas_call(functools.partial(swap_kernel, kind, axis), out_shape=jax....  319 us
    pallas_call x4, Pallas kernels, heads_call(): pl.pallas_call(kernel, out_shape=jax.ShapeDtypeStruct(shape, x.dtype), in...  46.1 us
    pallas_call x1, Pallas kernels, gather_experts(): pl.pallas_call(quad_kernel, out_shape=jax.ShapeDtypeStruct((2, 2, 4, *x.s...  40 us
    pallas_call x1, Pallas kernels, gather_weights(): pl.pallas_call(weights_kernel, out_shape=jax.ShapeDtypeStruct((CTX, *x.sh...  37.7 us
    dot_general x23, matrix products, dot(): lax.dot_general(a, b, (((dims[0],), (dims[1],)), ((), ())), preferred_ele...  34.9 us
    pallas_call x1, Pallas kernels, attend_back(): pl.pallas_call(backward_kernel, grid=(LEN // QUERIES,), out_shape=(jax.Sh...  25.4 us
    pallas_call x1, Pallas kernels, attend(): pl.pallas_call(forward_kernel, grid=(LEN // QUERIES,), out_shape=(jax.Sha...  21.1 us

profile of v1, /device:TPU:1, one launch (start us, length us, event | category | flops | bytes accessed | tf_op | source)
XLA Modules:
  0.0 600.2 jit_solution(15807753059006892270)
XLA Ops:
  5.2 10.0 %shard_map.203 = bf16[8,16,1280]{2,1,0:T(8,128)(2,1)} custom-call(bf16[16,1280]{1,0:T(8,128)(2,1)} %fusion.76.x), custom_call_target="tpu_custom_call" | custom-call | tf_op jit(solution)/shard_map/pallas_call | solution.py:78
  18.1 37.7 %shard_map.204 = bf16[16,48,3200]{2,1,0:T(8,128)(2,1)} custom-call(bf16[48,3200]{1,0:T(8,128)(2,1)} %fusion.57.x), custom_call_target="tpu_custom_call" | custom-call | tf_op jit(solution)/shard_map/pallas_call | solution.py:139
  55.9 1.4 fusion.120
  57.6 4.0 convolution_convert_fusion.1
  61.6 13.5 %shard_map.205.qkv_ref = bf16[3,64,2048]{2,1,0:T(8,128)(2,1)} custom-call(bf16[3,12,64,128]{3,2,1,0:T(8,128)(2,1)} %bitcast.178), custom_call_target="tpu_custom_call" | custom-call | tf_op jit(solution)/shard_map/pallas_call | solution.py:243
  76.9 21.1 %shard_map.206 = (bf16[2048,2048]{1,0:T(8,128)(2,1)S(1)}, f32[64,2048]{1,0:T(8,128)S(1)}, bf16[1,64,2048]{2,1,0:T(8,128)(2,1)S(1)}, f32[1,2048]{1,0:T(1,128)S(1)}) custom-call(bf16[3,64,2048]{2,1,0:T(8,128)(2,1)S(1)} %copy-done.2, f32[32]{0:T(128)S(1)} %reduce_sum.221.table_ref), custom_call_target="tpu_custom_call" | custom-call | tf_op jit(solution)/shard_map/pallas_call | solution.py:331
  98.0 3.2 copy-done
  101.9 8.6 %shard_map.207 = bf16[1,12,64,128]{3,2,1,0:T(8,128)(2,1)} custom-call(bf16[1,64,2048]{2,1,0:T(8,128)(2,1)} %copy-done.6), custom_call_target="tpu_custom_call" | custom-call | tf_op jit(solution)/shard_map/pallas_call | solution.py:243
  110.5 1.8 multiply_reduce_fusion.2
  112.7 1.2 fusion.123
  115.4 9.1 %shard_map.208 = bf16[8,48,768]{2,1,0:T(8,128)(2,1)} custom-call(bf16[8,48,768]{2,1,0:T(8,128)(2,1)} %bitcast.175), custom_call_target="tpu_custom_call" | custom-call | tf_op jit(solution)/shard_map/pallas_call | solution.py:78
  124.5 2.3 convolution_convert_fusion.9.x
  126.8 23.6 %shard_map.209 = bf16[4,320,768]{2,1,0:T(8,128)(2,1)} custom-call(bf16[320,768]{1,0:T(8,128)(2,1)} %convolution_convert_fusion.9.x), custom_call_target="tpu_custom_call" | custom-call | tf_op jit(solution)/shard_map/pallas_call | solution.py:78
  150.5 2.6 fusion.121
  153.1 1.2 pad_maximum_fusion.1.x
  154.3 40.0 %shard_map.210 = bf16[2,2,4,192,768]{4,3,2,1,0:T(8,128)(2,1)} custom-call(bf16[2,2,192,768]{3,2,1,0:T(8,128)(2,1)} %pad_maximum_fusion.1.x), custom_call_target="tpu_custom_call" | custom-call | tf_op jit(solution)/shard_map/pallas_call | solution.py:175
  194.3 1.9 fusion.6
  196.3 2.6 fusion.23
  204.0 1.5 pad_maximum_fusion
  205.5 24.8 %shard_map.211 = bf16[4,320,768]{2,1,0:T(8,128)(2,1)} custom-call(bf16[4,320,768]{2,1,0:T(8,128)(2,1)} %bitcast.157), custom_call_target="tpu_custom_call" | custom-call | tf_op jit(solution)/shard_map/pallas_call | solution.py:78
  230.3 2.1 reduce_sum.226
  232.4 1.4 convolution_convert_fusion.7
  233.8 11.1 %shard_map.212 = bf16[8,48,768]{2,1,0:T(8,128)(2,1)} custom-call(bf16[8,48,768]{2,1,0:T(8,128)(2,1)} %bitcast.174), custom_call_target="tpu_custom_call" | custom-call | tf_op jit(solution)/shard_map/pallas_call | solution.py:78
  244.9 1.5 fusion.55
  247.2 1.5 multiply_reduce_fusion
  249.0 2.4 convolution_convert_fusion.14
  251.4 11.8 %shard_map.213.do_ref = bf16[1,64,2048]{2,1,0:T(8,128)(2,1)} custom-call(bf16[1,12,64,128]{3,2,1,0:T(8,128)(2,1)} %bitcast.187), custom_call_target="tpu_custom_call" | custom-call | tf_op jit(solution)/shard_map/pallas_call | solution.py:243
  263.2 3.4 copy-done.1
  267.5 25.4 %shard_map.214 = (bf16[3,64,2048]{2,1,0:T(8,128)(2,1)S(1)}, f32[768,256]{1,0:T(8,128)S(1)}) custom-call(bf16[3,64,2048]{2,1,0:T(8,128)(2,1)S(1)} %copy-done.3, bf16[2048,2048]{1,0:T(8,128)(2,1)S(1)} %copy-done.1, f32[64,2048]{1,0:T(8,128)S(1)} %get-tuple-element.19.o_ref, f32[1,2048]{1,0:T(1,128)S(1)} %get-tuple-element.20.inv_ref, ...), custom_call_target="tpu_custom_call" | custom-call | tf_op jit(solution)/shard_map/pallas_call | solution.py:407
  293.8 12.2 %shard_map.215 = bf16[3,12,64,128]{3,2,1,0:T(8,128)(2,1)} custom-call(bf16[3,64,2048]{2,1,0:T(8,128)(2,1)} %copy-done.5), custom_call_target="tpu_custom_call" | custom-call | tf_op jit(solution)/shard_map/pallas_call | solution.py:243
  306.0 3.6 fusion.43
  310.6 3.0 convolution_convert_fusion
  315.9 3.7 select_reduce_fusion
  320.1 8.4 %concatenate.43.x = bf16[8,2,48,3200]{3,2,1,0:T(8,128)(2,1)} concatenate(bf16[8,2,48,2304]{3,2,1,0:T(8,128)(2,1)} %bitcast.139, bf16[8,2,48,768]{3,2,1,0:T(8,128)(2,1)S(1)} %bitcast.158, bf16[8,2,48,16]{3,2,1,0:T(8,128)(2,1)S(1)} %bitcast.173, bf16[8,2,48,1]{3,2,1,0:T(8,128)(2,1)S(1)} %convert_element_type.304, bf16[8,2,48,1]{3,2,1,0:T(8,128)(2,1)S(1)} %convert_element_type.305, ...), dimensions={3} | concatenate | bytes 9830400 | tf_op jit(solution)/shard_map/concatenate | solution.py:591
  328.6 76.4 %shard_map.216 = bf16[2,8,48,3200]{3,2,1,0:T(8,128)(2,1)} custom-call(bf16[8,2,48,3200]{3,2,1,0:T(8,128)(2,1)} %concatenate.43.x), custom_call_target="tpu_custom_call" | custom-call | tf_op jit(solution)/shard_map/pallas_call | solution.py:78
  405.0 5.4 reduce_sum.234
  410.4 30.6 %shard_map.217 = bf16[4,2,48,3200]{3,2,1,0:T(8,128)(2,1)} custom-call(bf16[4,2,48,3200]{3,2,1,0:T(8,128)(2,1)} %bitcast.155), custom_call_target="tpu_custom_call" | custom-call | tf_op jit(solution)/shard_map/pallas_call | solution.py:78
  441.0 3.0 reduce_sum.235.x
  444.0 14.1 %shard_map.218 = bf16[2,48,3200]{2,1,0:T(8,128)(2,1)} custom-call(bf16[2,48,3200]{2,1,0:T(8,128)(2,1)} %reduce_sum.235.x), custom_call_target="tpu_custom_call" | custom-call | tf_op jit(solution)/shard_map/pallas_call | solution.py:78
  458.2 1.3 reduce_sum.236
  460.7 6.3 %shard_map.219 = bf16[8,16,1280]{2,1,0:T(8,128)(2,1)} custom-call(bf16[8,16,1280]{2,1,0:T(8,128)(2,1)} %fusion.56.x), custom_call_target="tpu_custom_call" | custom-call | tf_op jit(solution)/shard_map/pallas_call | solution.py:78
  470.9 1.9 convolution_convert_fusion.2
  475.7 2.4 maximum_maximum_fusion.x
  478.1 75.5 %shard_map.220 = bf16[2,2,2,2,192,768]{5,4,3,2,1,0:T(8,128)(2,1)} custom-call(bf16[2,2,2,2,192,768]{5,4,3,2,1,0:T(8,128)(2,1)} %maximum_maximum_fusion.x), custom_call_target="tpu_custom_call" | custom-call | tf_op jit(solution)/shard_map/pallas_call | solution.py:78
  553.5 5.3 reduce_sum.238.x
  558.8 37.0 %shard_map.221 = bf16[2,2,2,192,768]{4,3,2,1,0:T(8,128)(2,1)} custom-call(bf16[2,2,2,192,768]{4,3,2,1,0:T(8,128)(2,1)} %reduce_sum.238.x), custom_call_target="tpu_custom_call" | custom-call | tf_op jit(solution)/shard_map/pallas_call | solution.py:78
  595.9 2.3 convert_reduce_fusion
  598.2 1.6 slice_bitcast_fusion
  (138 shorter events, 31.3 us)
Async XLA Ops:
  18.1 39.3 %copy-start.8 = (bf16[1,128,768]{2,1,0:T(8,128)(2,1)S(1)}, bf16[1,128,768]{2,1,0:T(8,128)(2,1)}, u32[]{:S(2)}) copy-start(bf16[1,128,768]{2,1,0:T(8,128)(2,1)} %param.12) | copy-start | bytes 589828
  61.6 52.3 %copy-start.15 = (bf16[1,128,768]{2,1,0:T(8,128)(2,1)S(1)}, bf16[1,128,768]{2,1,0:T(8,128)(2,1)}, u32[]{:S(2)}) copy-start(bf16[1,128,768]{2,1,0:T(8,128)(2,1)} %param.13) | copy-start | bytes 589828
  75.2 38.8 %copy-start.26 = (s32[1,128,1]{1,2,0:T(1,128)S(1)}, s32[1,128,1]{1,2,0:T(1,128)}, u32[]{:S(2)}) copy-start(s32[1,128,1]{1,2,0:T(1,128)} %param.14) | copy-start | bytes 1540
  75.7 1.1 copy-start.2
  98.0 3.2 copy-start
  101.2 0.7 copy-start.6
  112.7 37.8 %copy-start.13 = (bf16[128,768]{1,0:T(8,128)(2,1)}, bf16[128,768]{1,0:T(8,128)(2,1)S(1)}, u32[]{:S(2)}) copy-start(bf16[128,768]{1,0:T(8,128)(2,1)S(1)} %multiply_convert_fusion.2) | copy-start | bytes 589828
  150.5 2.7 copy-start.20
  150.5 2.7 copy-start.21
  153.1 41.2 %copy-start.10 = (bf16[4,1,80,768]{3,2,1,0:T(8,128)(2,1)}, bf16[4,1,80,768]{3,2,1,0:T(8,128)(2,1)S(1)}, u32[]{:S(2)}) copy-start(bf16[4,1,80,768]{3,2,1,0:T(8,128)(2,1)S(1)} %get-tuple-element.38) | copy-start | bytes 1474564
  194.3 1.9 copy-start.24
  196.3 6.2 %copy-start.16 = (f32[320,768]{1,0:T(8,128)}, f32[320,768]{1,0:T(8,128)S(1)}, u32[]{:S(2)}) copy-start(f32[320,768]{1,0:T(8,128)S(1)} %fusion.6) | copy-start | bytes 2949124
  196.3 3.0 copy-start.7
  199.3 0.8 copy-start.27
  199.3 1.4 copy-start.22
  200.7 2.5 copy-start.18
  201.7 0.8 copy-start.29
  247.2 16.0 %copy-start.3 = (bf16[3,64,2048]{2,1,0:T(8,128)(2,1)S(1)}, bf16[3,64,2048]{2,1,0:T(8,128)(2,1)}, u32[]{:S(2)}) copy-start(bf16[3,64,2048]{2,1,0:T(8,128)(2,1)} %shard_map.205.qkv_ref) | copy-start | bytes 2359300
  263.2 3.4 copy-start.1
  266.6 0.9 copy-start.4
  292.9 0.9 copy-start.5
  306.0 4.6 copy-start.9
  310.5 3.0 copy-start.12
  310.6 3.4 copy-start.14
  458.1 12.8 %copy-start.17 = (f32[320,768]{1,0:T(8,128)S(1)}, f32[320,768]{1,0:T(8,128)}, u32[]{:S(2)}) copy-start(f32[320,768]{1,0:T(8,128)} %copy-done.16) | copy-start | bytes 2949124
  468.1 4.8 copy-start.19
  468.1 4.8 copy-start.23
  469.5 4.3 copy-start.25
  472.8 1.0 copy-start.11
  472.8 1.2 copy-start.28
  472.9 2.0 copy-start.30

commit v2 on v1

--- a/solution.py
+++ b/solution.py
@@ -55,41 +55,69 @@
     return 2, k, lambda i: (z * 4 + xh * 2 + i, e)
 
 
-def swap_kernel(kind, axis, x, out, here, send, recv):
-    size, me, device = group(kind)
-    part = (lambda i: x) if axis is None else (lambda i: x.at[(slice(None),) * axis + (i,)])
-    peers = [lax.rem(me + i, size) for i in range(1, size)]
-    greet([device(p) for p in peers])
-    copies = [
-        push(part(p), out.at[me], send.at[i], recv.at[i], device(p)) for i, p in enumerate(peers)
-    ]
-    for copy in copies:
-        copy.start()
-    own = pltpu.make_async_copy(part(me), out.at[me], here)
-    own.start()
+SIZES = {"exp": EXP, "z": ZED, "x": 2, "core": 2}
+
+
+def swaps_kernel(plan, *refs):
+    n = len(plan)
+    xs, outs, (send, recv, here) = refs[:n], refs[n : 2 * n], refs[2 * n :]
+    peers = {}
+    for kind, axis, keep in plan:
+        size, me, device = group(kind)
+        peers[kind] = [device(lax.rem(me + i, size)) for i in range(1, size)]
+    greet([p for kind in peers for p in peers[kind]])
+    copies, count = [], 0
+    for (kind, axis, keep), x, out in zip(plan, xs, outs):
+        size, me, device = group(kind)
+        part = (lambda i: x) if axis is None else (lambda i: x.at[(slice(None),) * axis + (i,)])
+        for i in range(1, size):
+            to = lax.rem(me + i, size)
+            slot = me if keep else i - 1
+            copy = push(part(to), out.at[slot], send.at[count], recv.at[count], device(to))
+            copy.start()
+            copies.append(copy)
+            count += 1
+    for n, ((kind, axis, keep), x, out) in enumerate(zip(plan, xs, outs)):
+        if keep:
+            size, me, device = group(kind)
+            own = x if axis is None else x.at[(slice(None),) * axis + (me,)]
+            copy = pltpu.make_async_copy(own, out.at[me], here.at[n])
+            copy.start()
+            copies.append(copy)
     for copy in copies:
         copy.wait()
-    own.wait()
+
+
+def swaps(ident, *items):
+    shapes, total = [], 0
+    for x, kind, axis, keep in items:
+        block = x.shape if axis is None else x.shape[:axis] + x.shape[axis + 1 :]
+        shapes.append(jax.ShapeDtypeStruct((SIZES[kind] - (not keep), *block), x.dtype))
+        total += SIZES[kind] - 1
+    return pl.pallas_call(
+        functools.partial(swaps_kernel, [item[1:] for item in items]),
+        out_shape=shapes,
+        in_specs=[ANY] * len(items),
+        out_specs=[ANY] * len(items),
+        scratch_shapes=[
+            pltpu.SemaphoreType.DMA((total,)),
+            pltpu.SemaphoreType.DMA((total,)),
+            pltpu.SemaphoreType.DMA((len(items),)),
+        ],
+        compiler_params=pltpu.CompilerParams(collective_id=ident, has_side_effects=True),
+    )(*[item[0] for item in items])
 
 
 def swap(x, kind, ident, axis=None):
-    size = {"exp": EXP, "z": ZED, "x": 2, "core": 2}[kind]
-    block = x.shape if axis is None else x.shape[:axis] + x.shape[axis + 1 :]
-    return pl.pallas_call(
-        functools.partial(swap_kernel, kind, axis),
-        out_shape=jax.ShapeDtypeStruct((size, *block), x.dtype),
-        in_specs=[ANY],
-        out_specs=ANY,
-        scratch_shapes=[
-            pltpu.SemaphoreType.DMA,
-            pltpu.SemaphoreType.DMA((size - 1,)),
-            pltpu.SemaphoreType.DMA((size - 1,)),
-        ],
-        compiler_params=pltpu.CompilerParams(collective_id=ident, has_side_effects=True),
-    )(x)
-
-
-def weights_kernel(x, out, here, send, recv):
+    return swaps(ident, (x, kind, axis, True))[0]
+
+
+def add_up(x, kind, axis, others):
+    mine = lax.dynamic_index_in_dim(x, group(kind)[1], axis, keepdims=False)
+    return mine.astype(wide) + jnp.sum(others.astype(wide), axis=0)
+
+
+def weights_kernel(x, w, out, wide_out, here, send, recv):
     c, e, z, xh, k = spot()
     zs = [lax.rem(z + i, 4) for i in range(1, 4)]
     back = [lax.rem(z + 4 - i, 4) for i in range(1, 4)]
@@ -103,10 +131,17 @@
     first = [push(x, out.at[mine], send.at[1 + i], recv.at[1 + i], d) for i, d in enumerate(rows)]
     for copy in first:
         copy.start()
-    own = pltpu.make_async_copy(x, out.at[mine], here)
+    own = pltpu.make_async_copy(x, out.at[mine], here.at[0])
     own.start()
     pair = [push(x, out.at[mine], send.at[7], recv.at[7], twin)]
     pair[0].start()
+    slab = lambda xh, k: wide_out.at[:, :, xh * 2 + k]
+    w_across = push(w, slab(xh, k), send.at[15], recv.at[15], side)
+    w_across.start()
+    pair.append(push(w, slab(xh, k), send.at[16], recv.at[16], twin))
+    pair[1].start()
+    w_own = pltpu.make_async_copy(w, slab(xh, k), here.at[1])
+    w_own.start()
 
     def hand(n, block):
         copy = push(out.at[block], out.at[block], send.at[7 + n], recv.at[7 + n], twin)
@@ -124,66 +159,41 @@
     for i, p in enumerate(back):
         first[i].wait_recv()
         hand(2 + i, at(p, xh, k))
+    w_across.wait_recv()
+    other = slab(1 - xh, k)
+    pair.append(push(other, other, send.at[17], recv.at[17], twin))
+    pair[-1].start()
     for i, p in enumerate(back):
         second[i].wait_recv()
         hand(5 + i, at(p, 1 - xh, k))
     for copy in pair:
         copy.wait()
     across.wait_send()
+    w_across.wait_send()
     for copy in first + second:
         copy.wait_send()
     own.wait()
-
-
-def gather_weights(x, ident):
+    w_own.wait()
+
+
+def gather_weights(x, w, ident):
     return pl.pallas_call(
         weights_kernel,
-        out_shape=jax.ShapeDtypeStruct((CTX, *x.shape), x.dtype),
-        in_specs=[ANY],
-        out_specs=ANY,
+        out_shape=(
+            jax.ShapeDtypeStruct((CTX, *x.shape), x.dtype),
+            jax.ShapeDtypeStruct((2, 2, 4, *w.shape[2:]), w.dtype),
+        ),
+        in_specs=[ANY, pl.BlockSpec(memory_space=pltpu.VMEM)],
+        out_specs=(ANY, ANY),
         scratch_shapes=[
-            pltpu.SemaphoreType.DMA,
-            pltpu.SemaphoreType.DMA((15,)),
-            pltpu.SemaphoreType.DMA((15,)),
-        ],
-        compiler_params=pltpu.CompilerParams(collective_id=ident, has_side_effects=True),
-    )(x)
-
-
-def quad_kernel(x, out, here, send, recv):
-    c, e, z, xh, k = spot()
-    at = lambda xh, k: z * 4 + xh * 2 + k
-    side, twin = (at(1 - xh, k), e), (at(xh, 1 - k), e)
-    mine, theirs = xh * 2 + k, (1 - xh) * 2 + k
-    greet([side, twin])
-    across = push(x, out.at[:, :, mine], send.at[0], recv.at[0], side)
-    across.start()
-    pair = push(x, out.at[:, :, mine], send.at[1], recv.at[1], twin)
-    pair.start()
-    own = pltpu.make_async_copy(x, out.at[:, :, mine], here)
-    own.start()
-    across.wait_recv()
-    hand = push(out.at[:, :, theirs], out.at[:, :, theirs], send.at[2], recv.at[2], twin)
-    hand.start()
-    across.wait_send()
-    pair.wait()
-    hand.wait()
-    own.wait()
-
-
-def gather_experts(x, ident):
-    return pl.pallas_call(
-        quad_kernel,
-        out_shape=jax.ShapeDtypeStruct((2, 2, 4, *x.shape[2:]), x.dtype),
-        in_specs=[ANY],
-        out_specs=ANY,
-        scratch_shapes=[
-            pltpu.SemaphoreType.DMA,
-            pltpu.SemaphoreType.DMA((3,)),
-            pltpu.SemaphoreType.DMA((3,)),
-        ],
-        compiler_params=pltpu.CompilerParams(collective_id=ident, has_side_effects=True),
-    )(x)
+            pltpu.SemaphoreType.DMA((2,)),
+            pltpu.SemaphoreType.DMA((18,)),
+            pltpu.SemaphoreType.DMA((18,)),
+        ],
+        compiler_params=pltpu.CompilerParams(
+            collective_id=ident, has_side_effects=True, vmem_limit_bytes=16 << 20
+        ),
+    )(x, w)
 
 
 def head_of(c):
@@ -482,10 +492,10 @@
         ],
         axis=1,
     )
-    full = gather_weights(block, 2).reshape(D, 4 * D + 128)
-    experts_here = gather_experts(
-        jnp.stack([jnp.swapaxes(expert_in, 1, 2), expert_out]), 3
-    ).reshape(2, 2, D, D)
+    experts_local = jnp.stack([jnp.swapaxes(expert_in, 1, 2), expert_out])
+    full, experts_here = gather_weights(block, experts_local, 2)
+    full = full.reshape(D, 4 * D + 128)
+    experts_here = experts_here.reshape(2, 2, D, D)
     qkv_full = full[:, : 3 * D]
     out_full = full[:, 3 * D : 4 * D]
     router_wide = full[:, 4 * D : 4 * D + 16].astype(wide)
@@ -545,10 +555,13 @@
         grads_in.append(dot(grad_pre, rows, (0, 0)).astype(low))
         grads_out.append(dot(hidden, grads, (0, 0)).astype(low))
     partial = jnp.stack([partial[0], partial[2], partial[1], partial[3]], axis=1)
-    summed = jnp.sum(
-        swap(partial.reshape(ZED, 320, D), "z", 8, 0).astype(wide), axis=0
-    ).astype(low)
-    back = swap(dot(compact, summed, (0, 0)).astype(low).reshape(EXP, SLOTS, D), "exp", 9, 0)
+    partial = partial.reshape(ZED, 320, D)
+    summed = add_up(partial, "z", 0, swaps(8, (partial, "z", 0, False))[0]).astype(low)
+    spread = dot(compact, summed, (0, 0)).astype(low).reshape(EXP, SLOTS, D)
+    expert_grads = jnp.stack([jnp.stack(grads_in), jnp.stack(grads_out)])
+    expert_grads = expert_grads.reshape(2, 2, 2, 2, 192, D)
+    back, others = swaps(9, (spread, "exp", 0, True), (expert_grads, "core", 3, False))
+    expert_grads = add_up(expert_grads, "core", 3, others).astype(low)
     returned = dot(dispatch, back.reshape(EXP * SLOTS, D), (0, 0))
     expert_tokens, grad_h_two = returned[:TOK], returned[TOK:]
 
@@ -567,13 +580,6 @@
     head_grad = to_heads(grad_attended.reshape(1, HEADS, HEAD_DIM, TOK), 10)
     head_grads, tile_sums = attend_back(head_qkv, probs, attended, inverse, head_grad)
     grad_qkv = from_heads(head_grads, 11).reshape(3 * D, TOK)
-
-    expert_grads = jnp.stack([jnp.stack(grads_in), jnp.stack(grads_out)])
-    expert_grads = swap(expert_grads.reshape(2, 2, 2, 2, 192, D), "core", 12, 3)
-    expert_grads = jnp.sum(expert_grads.astype(wide), axis=0).astype(low)
-    expert_grads = jnp.sum(swap(expert_grads, "x", 13, 2).astype(wide), axis=0)
-    grad_expert_in = jnp.swapaxes(expert_grads[0], 1, 2)
-    grad_expert_out = expert_grads[1]
 
     grad_h_one = dot(grad_qkv, qkv_full, (0, 1))
     grad_x_norm, grad_gain_one = norm_one_back(grad_h_one)
@@ -600,10 +606,15 @@
         ],
         axis=1,
     )
-    total = lambda v: jnp.sum(v.astype(wide), axis=0)
-    shared = total(swap(shared.reshape(8, 2, 48, 3200), "core", 14, 1)).astype(low)
-    shared = total(swap(shared.reshape(4, 2, 48, 3200), "z", 15, 0)).astype(low)
-    shared = total(swap(shared, "x", 16, 0)).astype(low)
+    shared = shared.reshape(8, 2, 48, 3200)
+    shared = add_up(shared, "core", 1, swaps(14, (shared, "core", 1, False))[0])
+    shared = shared.astype(low).reshape(4, 2, 48, 3200)
+    others, expert_others = swaps(15, (shared, "z", 0, False), (expert_grads, "x", 2, False))
+    expert_grads = add_up(expert_grads, "x", 2, expert_others)
+    grad_expert_in = jnp.swapaxes(expert_grads[0], 1, 2)
+    grad_expert_out = expert_grads[1]
+    shared = add_up(shared, "z", 0, others).astype(low)
+    shared = add_up(shared, "x", 0, swaps(16, (shared, "x", 0, False))[0]).astype(low)
     lines = jnp.concatenate(
         [
             shared[:, : 4 * D].reshape(EXP, 16, 1152),
@@ -613,7 +624,7 @@
         ],
         axis=2,
     )
-    lines = total(swap(lines, "exp", 17, 0))
+    lines = add_up(lines, "exp", 0, swaps(17, (lines, "exp", 0, False))[0])
     matrix = lines[:, :1152].reshape(6, 4 * D)
     small = lines[0, 1152:1266].reshape(6, 19)
     return (

time: 607 us -> 396 us (0.65)
  Pallas kernels: 489 us -> 272 us
  local copies, waits for them, and re-layouts: 35.1 us -> 47 us
    pallas_call x13 -> x10, Pallas kernels: 396 us -> 182 us  [the longest x9 137 us: swaps(): pl.pallas_call(functools.partial(swaps_kernel, [item[1:] for item in item...]
    reduce_sum x7 -> x3, other arithmetic: 20.4 us -> 5.31 us  [add_up(): return mine.astype(wide) + jnp.sum(others.astype(wide), axis=0)]
    convert_element_type x0 -> x4, other arithmetic: none -> 9.27 us  [the longest x1 3.89 us: shards(): shared = shared.astype(low).reshape(4, 2, 48, 3200)]
    unnamed x64 -> x116, local copies, waits for them, and re-layouts: 11.7 us -> 16.7 us
where the time goes in v2:
time: 396 us; the launch traced here: 392 us
  Pallas kernels  272 us (69%)
  local copies, waits for them, and re-layouts  47 us (12%)
  matrix products  40.3 us (10%)
  other arithmetic  30.7 us (8%)
    pallas_call x9, Pallas kernels, swaps(): pl.pallas_call(functools.partial(swaps_kernel, [item[1:] for item in item...  137 us
    pallas_call x1, Pallas kernels, gather_weights(): pl.pallas_call(weights_kernel, out_shape=(jax.ShapeDtypeStruct((CTX, *x.s...  44.4 us
    pallas_call x4, Pallas kernels, heads_call(): pl.pallas_call(kernel, out_shape=jax.ShapeDtypeStruct(shape, x.dtype), in...  44.4 us
    dot_general x23, matrix products, dot(): lax.dot_general(a, b, (((dims[0],), (dims[1],)), ((), ())), preferred_ele...  36.8 us
    pallas_call x1, Pallas kernels, attend_back(): pl.pallas_call(backward_kernel, grid=(LEN // QUERIES,), out_shape=(jax.Sh...  25 us
    pallas_call x1, Pallas kernels, attend(): pl.pallas_call(forward_kernel, grid=(LEN // QUERIES,), out_shape=(jax.Sha...  21.1 us
    unnamed x116, local copies, waits for them, and re-layouts  16.7 us
    concatenate x1, local copies, waits for them, and re-layouts, shards(): jnp.concatenate([dot(h_one, grad_qkv, (0, 1)).astype(low), dot(attended_l...  8.44 us

profile of v2, /device:TPU:1, one launch (start us, length us, event | category | flops | bytes accessed | tf_op | source)
XLA Modules:
  0.0 392.1 jit_solution(6853909283573657924)
XLA Ops:
  5.3 10.0 %shard_map.203 = bf16[8,16,1280]{2,1,0:T(8,128)(2,1)} custom-call(bf16[16,1280]{1,0:T(8,128)(2,1)} %fusion.84.refs_0_), custom_call_target="tpu_custom_call" | custom-call | tf_op jit(solution)/shard_map/pallas_call | solution.py:97
  17.7 44.4 %shard_map.204 = (bf16[16,48,3200]{2,1,0:T(8,128)(2,1)S(1)}, bf16[2,2,4,192,768]{4,3,2,1,0:T(8,128)(2,1)S(1)}) custom-call(bf16[48,3200]{1,0:T(8,128)(2,1)S(1)} %fusion.64.x, bf16[2,2,192,768]{3,2,1,0:T(8,128)(2,1)S(1)} %pad_maximum_fusion.1.w), custom_call_target="tpu_custom_call" | custom-call | tf_op jit(solution)/shard_map/pallas_call | solution.py:180
  62.2 2.1 copy-done.4
  64.3 2.2 copy-done.6
  67.1 4.0 %convolution_convert_fusion.1 = bf16[2304,128]{1,0:T(8,128)(2,1)} fusion(bf16[768,3200]{1,0:T(8,128)(2,1)} %bitcast.182, bf16[1,128,768]{2,1,0:T(8,128)(2,1)S(1)} %copy-done.10, f32[768]{0:T(1024)S(1)} %convert_reduce_fusion.4, f32[128]{0:T(128)S(1)} %fusion.121), kind=kOutput, calls=%fused_computation.9 | convolution fusion | flops 453672960 | bytes 4328960 | tf_op jit(solution)/shard_map/dot_general | solution.py:452
  71.1 14.1 %shard_map.205.qkv_ref = bf16[3,64,2048]{2,1,0:T(8,128)(2,1)} custom-call(bf16[3,12,64,128]{3,2,1,0:T(8,128)(2,1)} %bitcast.216), custom_call_target="tpu_custom_call" | custom-call | tf_op jit(solution)/shard_map/pallas_call | solution.py:253
  87.3 21.1 %shard_map.206 = (bf16[2048,2048]{1,0:T(8,128)(2,1)S(1)}, f32[64,2048]{1,0:T(8,128)S(1)}, bf16[1,64,2048]{2,1,0:T(8,128)(2,1)S(1)}, f32[1,2048]{1,0:T(1,128)S(1)}) custom-call(bf16[3,64,2048]{2,1,0:T(8,128)(2,1)S(1)} %copy-done.2, f32[32]{0:T(128)S(1)} %reduce_sum.198.table_ref), custom_call_target="tpu_custom_call" | custom-call | tf_op jit(solution)/shard_map/pallas_call | solution.py:341
  108.5 3.2 copy-done
  112.4 8.4 %shard_map.207 = bf16[1,12,64,128]{3,2,1,0:T(8,128)(2,1)} custom-call(bf16[1,64,2048]{2,1,0:T(8,128)(2,1)} %copy-done.8), custom_call_target="tpu_custom_call" | custom-call | tf_op jit(solution)/shard_map/pallas_call | solution.py:253
  120.8 1.8 multiply_reduce_fusion.2
  125.6 9.4 %shard_map.208 = bf16[8,48,768]{2,1,0:T(8,128)(2,1)} custom-call(bf16[8,48,768]{2,1,0:T(8,128)(2,1)} %bitcast.213), custom_call_target="tpu_custom_call" | custom-call | tf_op jit(solution)/shard_map/pallas_call | solution.py:97
  135.0 2.3 convolution_convert_fusion.9.refs_0_
  137.4 23.2 %shard_map.209 = bf16[4,320,768]{2,1,0:T(8,128)(2,1)} custom-call(bf16[320,768]{1,0:T(8,128)(2,1)} %convolution_convert_fusion.9.refs_0_), custom_call_target="tpu_custom_call" | custom-call | tf_op jit(solution)/shard_map/pallas_call | solution.py:97
  160.5 1.6 fusion.130
  162.2 2.6 fusion.9
  164.8 2.6 fusion.26
  172.1 1.5 pad_maximum_fusion
  173.6 25.5 %shard_map.210 = bf16[3,320,768]{2,1,0:T(8,128)(2,1)} custom-call(bf16[4,320,768]{2,1,0:T(8,128)(2,1)} %bitcast.191), custom_call_target="tpu_custom_call" | custom-call | tf_op jit(solution)/shard_map/pallas_call | solution.py:97
  199.1 1.7 convert_reduce_fusion.1
  200.9 2.5 convolution_convert_fusion.7
  203.3 2.2 convolution_convert_fusion.2
  208.4 2.6 maximum_maximum_fusion.refs_1_
  210.9 13.6 %shard_map.211 = (bf16[8,48,768]{2,1,0:T(8,128)(2,1)}, bf16[1,2,2,2,192,768]{5,4,3,2,1,0:T(8,128)(2,1)}) custom-call(bf16[8,48,768]{2,1,0:T(8,128)(2,1)} %bitcast.198, bf16[2,2,2,2,192,768]{5,4,3,2,1,0:T(8,128)(2,1)} %maximum_maximum_fusion.refs_1_), custom_call_target="tpu_custom_call" | custom-call | tf_op jit(solution)/shard_map/pallas_call | solution.py:97
  224.6 1.5 fusion.62
  226.9 2.1 multiply_reduce_fusion
  229.9 2.4 convolution_convert_fusion.14
  232.3 10.0 %shard_map.212.do_ref = bf16[1,64,2048]{2,1,0:T(8,128)(2,1)} custom-call(bf16[1,12,64,128]{3,2,1,0:T(8,128)(2,1)} %bitcast.225), custom_call_target="tpu_custom_call" | custom-call | tf_op jit(solution)/shard_map/pallas_call | solution.py:253
  242.3 3.4 copy-done.1
  246.6 25.0 %shard_map.213 = (bf16[3,64,2048]{2,1,0:T(8,128)(2,1)S(1)}, f32[768,256]{1,0:T(8,128)S(1)}) custom-call(bf16[3,64,2048]{2,1,0:T(8,128)(2,1)S(1)} %copy-done.3, bf16[2048,2048]{1,0:T(8,128)(2,1)S(1)} %copy-done.1, f32[64,2048]{1,0:T(8,128)S(1)} %get-tuple-element.28.o_ref, f32[1,2048]{1,0:T(1,128)S(1)} %get-tuple-element.29.inv_ref, ...), custom_call_target="tpu_custom_call" | custom-call | tf_op jit(solution)/shard_map/pallas_call | solution.py:417
  272.5 11.9 %shard_map.214 = bf16[3,12,64,128]{3,2,1,0:T(8,128)(2,1)} custom-call(bf16[3,64,2048]{2,1,0:T(8,128)(2,1)} %copy-done.7), custom_call_target="tpu_custom_call" | custom-call | tf_op jit(solution)/shard_map/pallas_call | solution.py:253
  284.4 3.6 fusion.50
  289.0 3.0 convolution_convert_fusion
  294.5 2.7 select_reduce_fusion
  297.7 8.4 %concatenate.43.refs_0_ = bf16[8,2,48,3200]{3,2,1,0:T(8,128)(2,1)} concatenate(bf16[8,2,48,2304]{3,2,1,0:T(8,128)(2,1)} %bitcast.190, bf16[8,2,48,768]{3,2,1,0:T(8,128)(2,1)S(1)} %bitcast.196, bf16[8,2,48,16]{3,2,1,0:T(8,128)(2,1)S(1)} %bitcast.211, bf16[8,2,48,1]{3,2,1,0:T(8,128)(2,1)S(1)} %convert_element_type.390, bf16[8,2,48,1]{3,2,1,0:T(8,128)(2,1)S(1)} %convert_element_type.391, ...), dimensions={3} | concatenate | bytes 9830400 | tf_op jit(solution)/shard_map/concatenate | solution.py:597
  306.1 5.5 %shard_map.215 = bf16[1,8,48,3200]{3,2,1,0:T(8,128)(2,1)} custom-call(bf16[8,2,48,3200]{3,2,1,0:T(8,128)(2,1)} %concatenate.43.refs_0_), custom_call_target="tpu_custom_call" | custom-call | tf_op jit(solution)/shard_map/pallas_call | solution.py:97
  311.7 2.0 constant_dynamic-slice_fusion
  313.7 3.9 fusion.refs_0_
  317.6 2.1 fusion.1.refs_1_
  319.7 33.8 %shard_map.216 = (bf16[3,2,48,3200]{3,2,1,0:T(8,128)(2,1)}, bf16[1,2,2,192,768]{4,3,2,1,0:T(8,128)(2,1)}) custom-call(bf16[4,2,48,3200]{3,2,1,0:T(8,128)(2,1)} %fusion.refs_0_, bf16[2,2,2,192,768]{4,3,2,1,0:T(8,128)(2,1)} %fusion.1.refs_1_), custom_call_target="tpu_custom_call" | custom-call | tf_op jit(solution)/shard_map/pallas_call | solution.py:97
  353.5 1.9 convert_reduce_fusion
  355.4 2.0 fusion.5.refs_0_
  357.4 9.7 %shard_map.217 = bf16[1,48,3200]{2,1,0:T(8,128)(2,1)} custom-call(bf16[2,48,3200]{2,1,0:T(8,128)(2,1)} %fusion.5.refs_0_), custom_call_target="tpu_custom_call" | custom-call | tf_op jit(solution)/shard_map/pallas_call | solution.py:97
  369.3 2.1 reshape.356
  371.4 1.7 fusion.63.refs_0_
  373.1 6.8 %shard_map.218 = bf16[7,16,1280]{2,1,0:T(8,128)(2,1)} custom-call(bf16[8,16,1280]{2,1,0:T(8,128)(2,1)} %fusion.63.refs_0_), custom_call_target="tpu_custom_call" | custom-call | tf_op jit(solution)/shard_map/pallas_call | solution.py:97
  379.9 1.6 convert_reduce_fusion.2
  383.7 1.5 reshape.358
  390.6 1.6 slice_bitcast_fusion
  (192 shorter events, 37.4 us)
Async XLA Ops:
  0.6 16.9 %copy-start.23 = (bf16[2,192,768]{2,1,0:T(8,128)(2,1)S(1)}, bf16[2,192,768]{2,1,0:T(8,128)(2,1)}, u32[]{:S(2)}) copy-start(bf16[2,192,768]{2,1,0:T(8,128)(2,1)} %param.23) | copy-start | bytes 1769476
  0.7 16.9 %copy-start.24 = (bf16[2,768,192]{1,2,0:T(8,128)(2,1)S(1)}, bf16[2,768,192]{1,2,0:T(8,128)(2,1)}, u32[]{:S(2)}) copy-start(bf16[2,768,192]{1,2,0:T(8,128)(2,1)} %param.22) | copy-start | bytes 1769476
  17.6 49.4 %copy-start.10 = (bf16[1,128,768]{2,1,0:T(8,128)(2,1)S(1)}, bf16[1,128,768]{2,1,0:T(8,128)(2,1)}, u32[]{:S(2)}) copy-start(bf16[1,128,768]{2,1,0:T(8,128)(2,1)} %param.12) | copy-start | bytes 589828
  62.1 2.1 copy-start.4
  64.2 2.2 copy-start.6
  67.1 4.0 %copy-start.47 = (f32[128]{0:T(128)}, f32[128]{0:T(128)S(1)}, u32[]{:S(2)}) copy-start(f32[128]{0:T(128)S(1)} %fusion.51) | copy-start | bytes 1540
  67.1 4.0 %copy-start.45 = (f32[128]{0:T(128)}, f32[128]{0:T(128)S(1)}, u32[]{:S(2)}) copy-start(f32[128]{0:T(128)S(1)} %fusion.121) | copy-start | bytes 1540
  71.1 53.0 %copy-start.18 = (bf16[1,128,768]{2,1,0:T(8,128)(2,1)S(1)}, bf16[1,128,768]{2,1,0:T(8,128)(2,1)}, u32[]{:S(2)}) copy-start(bf16[1,128,768]{2,1,0:T(8,128)(2,1)} %param.13) | copy-start | bytes 589828
  85.3 38.8 %copy-start.37 = (s32[1,128,1]{1,2,0:T(1,128)S(1)}, s32[1,128,1]{1,2,0:T(1,128)}, u32[]{:S(2)}) copy-start(s32[1,128,1]{1,2,0:T(1,128)} %param.14) | copy-start | bytes 1540
  108.4 3.2 copy-start
  122.8 104.1 %copy-start.44 = (f32[128]{0:T(128)}, f32[128]{0:T(128)S(1)}, u32[]{:S(2)}) copy-start(f32[128]{0:T(128)S(1)} %fusion.122) | copy-start | bytes 1540
  124.0 102.8 %copy-start.33 = (f32[128]{0:T(128)}, f32[128]{0:T(128)S(1)}, u32[]{:S(2)}) copy-start(f32[128]{0:T(128)S(1)} %get-tuple-element.58) | copy-start | bytes 1540
  124.1 102.8 %copy-start.35 = (f32[128]{0:T(128)}, f32[128]{0:T(128)S(1)}, u32[]{:S(2)}) copy-start(f32[128]{0:T(128)S(1)} %fusion.88) | copy-start | bytes 1540
  137.3 30.1 %slice-start = ((s8[4718592]{0:T(1024)(128)(4,1)}), s8[524288]{0:T(1024)(128)(4,1)S(1)}, s32[]{:S(2)}) async-start(s8[4718592]{0:T(1024)(128)(4,1)} %bitcast.173), calls=%async_computation | async-start | bytes 1048576
  162.2 5.2 %copy-start.15 = (bf16[4,1,80,768]{3,2,1,0:T(8,128)(2,1)}, bf16[4,1,80,768]{3,2,1,0:T(8,128)(2,1)S(1)}, u32[]{:S(2)}) copy-start(bf16[4,1,80,768]{3,2,1,0:T(8,128)(2,1)S(1)} %get-tuple-element.50) | copy-start | bytes 1474564
  162.2 5.2 %copy-start.27 = (bf16[4,1,80,768]{3,2,1,0:T(8,128)(2,1)}, bf16[4,1,80,768]{3,2,1,0:T(8,128)(2,1)S(1)}, u32[]{:S(2)}) copy-start(bf16[4,1,80,768]{3,2,1,0:T(8,128)(2,1)S(1)} %get-tuple-element.49) | copy-start | bytes 1474564
  162.2 6.0 %copy-start.13 = (bf16[4,1,80,768]{3,2,1,0:T(8,128)(2,1)}, bf16[4,1,80,768]{3,2,1,0:T(8,128)(2,1)S(1)}, u32[]{:S(2)}) copy-start(bf16[4,1,80,768]{3,2,1,0:T(8,128)(2,1)S(1)} %get-tuple-element.51) | copy-start | bytes 1474564
  162.2 6.6 %copy-start.25 = (bf16[4,1,80,768]{3,2,1,0:T(8,128)(2,1)}, bf16[4,1,80,768]{3,2,1,0:T(8,128)(2,1)S(1)}, u32[]{:S(2)}) copy-start(bf16[4,1,80,768]{3,2,1,0:T(8,128)(2,1)S(1)} %get-tuple-element.48) | copy-start | bytes 1474564
  162.2 5.2 %slice-start.1 = ((s8[4718592]{0:T(1024)(128)(4,1)}), s8[4194304]{0:T(1024)(128)(4,1)S(1)}, s32[]{:S(2)}) async-start(s8[4718592]{0:T(1024)(128)(4,1)} %bitcast.173), calls=%async_computation.1 | async-start | bytes 8388608
  164.8 5.8 %copy-start.20 = (f32[320,768]{1,0:T(8,128)}, f32[320,768]{1,0:T(8,128)S(1)}, u32[]{:S(2)}) copy-start(f32[320,768]{1,0:T(8,128)S(1)} %fusion.9) | copy-start | bytes 2949124
  168.8 2.5 copy-start.21
  199.1 4.2 %copy-start.28 = (bf16[4,1,80,768]{3,2,1,0:T(8,128)(2,1)S(1)}, bf16[4,1,80,768]{3,2,1,0:T(8,128)(2,1)}, u32[]{:S(2)}) copy-start(bf16[4,1,80,768]{3,2,1,0:T(8,128)(2,1)} %copy-done.27) | copy-start | bytes 1474564
  203.3 2.2 copy-start.22
  203.3 2.2 copy-start.26
  205.5 1.2 copy-start.50
  205.6 2.0 copy-start.14
  205.6 2.0 copy-start.52
  226.8 2.2 copy-start.40
  226.9 2.1 copy-start.42
  226.9 15.4 %copy-start.3 = (bf16[3,64,2048]{2,1,0:T(8,128)(2,1)S(1)}, bf16[3,64,2048]{2,1,0:T(8,128)(2,1)}, u32[]{:S(2)}) copy-start(bf16[3,64,2048]{2,1,0:T(8,128)(2,1)} %shard_map.205.qkv_ref) | copy-start | bytes 2359300
  242.3 3.4 copy-start.1
  246.6 37.8 %copy-start.46 = (f32[128]{0:T(128)S(1)}, f32[128]{0:T(128)}, u32[]{:S(2)}) copy-start(f32[128]{0:T(128)} %copy-done.45) | copy-start | bytes 1540
  284.4 3.7 copy-start.48
  284.4 4.6 %copy-start.12 = (bf16[3,12,64,128]{3,2,1,0:T(8,128)(2,1)S(1)}, bf16[3,12,64,128]{3,2,1,0:T(8,128)(2,1)}, u32[]{:S(2)}) copy-start(bf16[3,12,64,128]{3,2,1,0:T(8,128)(2,1)} %shard_map.214) | copy-start | bytes 1769476
  289.0 3.0 copy-start.17
  289.0 3.5 copy-start.34
  289.0 3.5 copy-start.36
  289.0 3.5 copy-start.38
  289.0 3.5 copy-start.41
  289.0 3.5 copy-start.43
  289.0 4.2 %copy-start.39 = (bf16[768]{0:T(1024)(128)(2,1)S(1)}, bf16[768]{0:T(1024)(128)(2,1)}, u32[]{:S(2)}) copy-start(bf16[768]{0:T(1024)(128)(2,1)} %get-tuple-element.35) | copy-start | bytes 4612
  292.0 5.3 %copy-start.31 = (pred[32,4,3]{2,1,0:T(4,128)(4,1)S(1)}, pred[32,4,3]{2,1,0:T(4,128)(4,1)}, u32[]{:S(2)}) copy-start(pred[32,4,3]{2,1,0:T(4,128)(4,1)} %copy-done.30) | copy-start | bytes 1156
  306.1 11.5 %slice-start.2 = ((s8[4718592]{0:T(1024)(128)(4,1)}), s8[524288]{0:T(1024)(128)(4,1)S(1)}, s32[]{:S(2)}) async-start(s8[4718592]{0:T(1024)(128)(4,1)} %bitcast.188), calls=%async_computation.2 | async-start | bytes 1048576
  311.7 5.9 %slice-start.3 = ((s8[4718592]{0:T(1024)(128)(4,1)}), s8[4194304]{0:T(1024)(128)(4,1)S(1)}, s32[]{:S(2)}) async-start(s8[4718592]{0:T(1024)(128)(4,1)} %bitcast.188), calls=%async_computation.3 | async-start | bytes 8388608
  313.7 3.9 copy-start.11
  367.1 23.2 %copy-start.9 = (bf16[2,2,2,192,768]{4,3,2,1,0:T(8,128)(2,1)S(1)}, bf16[2,2,2,192,768]{4,3,2,1,0:T(8,128)(2,1)}, u32[]{:S(2)}) copy-start(bf16[2,2,2,192,768]{4,3,2,1,0:T(8,128)(2,1)} %fusion.1.refs_1_) | copy-start | bytes 7077892
  369.3 21.0 %copy-start.19 = (bf16[1,2,2,192,768]{4,3,2,1,0:T(8,128)(2,1)S(1)}, bf16[1,2,2,192,768]{4,3,2,1,0:T(8,128)(2,1)}, u32[]{:S(2)}) copy-start(bf16[1,2,2,192,768]{4,3,2,1,0:T(8,128)(2,1)} %get-tuple-element.34) | copy-start | bytes 3538948
  388.8 1.7 copy-start.32
  (9 other events, 7.5 us)

commit v3 on v2

--- a/solution.py
+++ b/solution.py
@@ -52,48 +52,108 @@
         return ZED, z, lambda i: (i * 4 + xh * 2 + k, e)
     if kind == "x":
         return 2, xh, lambda i: (z * 4 + i * 2 + k, e)
-    return 2, k, lambda i: (z * 4 + xh * 2 + i, e)
-
-
-SIZES = {"exp": EXP, "z": ZED, "x": 2, "core": 2}
+    if kind == "core":
+        return 2, k, lambda i: (z * 4 + xh * 2 + i, e)
+    if kind == "quad":
+        return 4, xh * 2 + k, lambda i: (z * 4 + i, e)
+    return CTX, c, lambda i: (i, e)
+
+
+SIZES = {"exp": EXP, "z": ZED, "x": 2, "core": 2, "quad": 4}
+
+
+def head_of(c):
+    return jnp.minimum((c // 4) * 3 + c % 4, HEADS - 1)
+
+
+def owns(c):
+    return c % 4 < 3
+
+
+def columns(c):
+    return pl.ds(pl.multiple_of(c * TOK, TOK), TOK)
+
+
+def when(condition, step):
+    if condition is None:
+        step()
+    else:
+        pl.when(condition)(step)
+
+
+def heads_parts(kind, me, x, out):
+    if kind == "to_heads":
+        return lambda to: x.at[:, head_of(to)], out.at[:, :, columns(me)], None, owns
+    if kind == "from_heads":
+        return lambda to: x.at[:, :, columns(to)], out.at[:, head_of(me)], owns, None
+    return lambda to: x.at[to], out.at[head_of(me)], owns, None
 
 
 def swaps_kernel(plan, *refs):
     n = len(plan)
     xs, outs, (send, recv, here) = refs[:n], refs[n : 2 * n], refs[2 * n :]
-    peers = {}
-    for kind, axis, keep in plan:
+    kinds = dict.fromkeys("ctx" if kind not in SIZES else kind for kind, axis, keep in plan)
+    if "ctx" in kinds:
+        kinds = [kind for kind in kinds if kind in ("ctx", "exp")]
+    peers = []
+    for kind in kinds:
         size, me, device = group(kind)
-        peers[kind] = [device(lax.rem(me + i, size)) for i in range(1, size)]
-    greet([p for kind in peers for p in peers[kind]])
+        peers += [device(lax.rem(me + i, size)) for i in range(1, size)]
+    greet(peers)
     copies, count = [], 0
     for (kind, axis, keep), x, out in zip(plan, xs, outs):
         size, me, device = group(kind)
-        part = (lambda i: x) if axis is None else (lambda i: x.at[(slice(None),) * axis + (i,)])
+        if kind in SIZES:
+            part = lambda i: x if axis is None else x.at[(slice(None),) * axis + (i,)]
+            sends = receives = None
+        else:
+            part, place, sends, receives = heads_parts(kind, me, x, out)
         for i in range(1, size):
-            to = lax.rem(me + i, size)
-            slot = me if keep else i - 1
-            copy = push(part(to), out.at[slot], send.at[count], recv.at[count], device(to))
-            copy.start()
-            copies.append(copy)
+            to, source = lax.rem(me + i, size), lax.rem(me + size - i, size)
+            if kind in SIZES:
+                place = out.at[me if keep else i - 1]
+            copy = push(part(to), place, send.at[count], recv.at[count], device(to))
+            if sends is not None:
+                out_if, in_if = sends(me), sends(source)
+            elif receives is not None:
+                out_if, in_if = receives(to), receives(me)
+            else:
+                out_if = in_if = None
+            when(out_if, copy.start)
+            copies.append((copy, out_if, in_if))
             count += 1
+    own = []
     for n, ((kind, axis, keep), x, out) in enumerate(zip(plan, xs, outs)):
-        if keep:
-            size, me, device = group(kind)
-            own = x if axis is None else x.at[(slice(None),) * axis + (me,)]
-            copy = pltpu.make_async_copy(own, out.at[me], here.at[n])
-            copy.start()
-            copies.append(copy)
-    for copy in copies:
-        copy.wait()
+        size, me, device = group(kind)
+        if kind in SIZES and keep:
+            part = x if axis is None else x.at[(slice(None),) * axis + (me,)]
+            own.append((pltpu.make_async_copy(part, out.at[me], here.at[n]), None))
+        elif kind not in SIZES:
+            part, place, sends, receives = heads_parts(kind, me, x, out)
+            own.append((pltpu.make_async_copy(part(me), place, here.at[n]), owns(me)))
+    for copy, condition in own:
+        when(condition, copy.start)
+    for copy, out_if, in_if in copies:
+        when(out_if, copy.wait_send)
+        when(in_if, copy.wait_recv)
+    for copy, condition in own:
+        when(condition, copy.wait)
 
 
 def swaps(ident, *items):
     shapes, total = [], 0
     for x, kind, axis, keep in items:
         block = x.shape if axis is None else x.shape[:axis] + x.shape[axis + 1 :]
-        shapes.append(jax.ShapeDtypeStruct((SIZES[kind] - (not keep), *block), x.dtype))
-        total += SIZES[kind] - 1
+        if kind == "to_heads":
+            shape = (x.shape[0], HEAD_DIM, LEN)
+        elif kind == "from_heads":
+            shape = (x.shape[0], HEADS, HEAD_DIM, TOK)
+        elif kind == "head_rows":
+            shape = (HEADS, *x.shape[1:])
+        else:
+            shape = (SIZES[kind] - (not keep), *block)
+        shapes.append(jax.ShapeDtypeStruct(shape, x.dtype))
+        total += SIZES.get(kind, CTX) - 1
     return pl.pallas_call(
         functools.partial(swaps_kernel, [item[1:] for item in items]),
         out_shape=shapes,
@@ -196,80 +256,66 @@
     )(x, w)
 
 
-def head_of(c):
-    return jnp.minimum((c // 4) * 3 + c % 4, HEADS - 1)
-
-
-def owns(c):
-    return c % 4 < 3
-
-
-def columns(c):
-    return pl.ds(pl.multiple_of(c * TOK, TOK), TOK)
-
-
-def to_heads_kernel(x, out, here, send, recv):
+def to_heads(x, ident):
+    return swaps(ident, (x, "to_heads", None, True))[0]
+
+
+def from_heads(x, ident):
+    return swaps(ident, (x, "from_heads", None, True))[0]
+
+
+def spread_tokens(x, out, here, send, recv, step, last):
     c, e, z, xh, k = spot()
-    peers = [lax.rem(c + i, CTX) for i in range(1, CTX)]
-    greet([(p, e) for p in peers])
-    copies = [
-        push(x.at[:, head_of(p)], out.at[:, :, columns(c)], send.at[i], recv.at[i], (p, e))
-        for i, p in enumerate(peers)
+    at = lambda z, xh, k: z * 4 + xh * 2 + k
+    forth = [lax.rem(z + i, 4) for i in range(1, 4)]
+    back = [lax.rem(z + 4 - i, 4) for i in range(1, 4)]
+    side, twin = (at(z, 1 - xh, k), e), (at(z, xh, 1 - k), e)
+    mine, theirs = at(z, xh, k), at(z, 1 - xh, k)
+    held = [mine, theirs] + [at(p, xh, k) for p in back] + [at(p, 1 - xh, k) for p in back]
+    across = push(x, out.at[mine], send.at[0], recv.at[0], side)
+    first = [
+        push(x, out.at[mine], send.at[1 + i], recv.at[1 + i], (at(p, xh, k), e))
+        for i, p in enumerate(forth)
     ]
-    own = pltpu.make_async_copy(x.at[:, head_of(c)], out.at[:, :, columns(c)], here)
-    for p, copy in zip(peers, copies):
-        pl.when(owns(p))(copy.start)
-    pl.when(owns(c))(own.start)
-    for p, copy in zip(peers, copies):
-        pl.when(owns(p))(copy.wait_send)
-        pl.when(owns(c))(copy.wait_recv)
-    pl.when(owns(c))(own.wait)
-
-
-def from_heads_kernel(x, out, here, send, recv):
-    c, e, z, xh, k = spot()
-    peers = [lax.rem(c + i, CTX) for i in range(1, CTX)]
-    sources = [lax.rem(c + CTX - i, CTX) for i in range(1, CTX)]
-    greet([(p, e) for p in peers])
-    copies = [
-        push(x.at[:, :, columns(p)], out.at[:, head_of(c)], send.at[i], recv.at[i], (p, e))
-        for i, p in enumerate(peers)
+    second = [
+        push(out.at[theirs], out.at[theirs], send.at[4 + i], recv.at[4 + i], (at(p, xh, k), e))
+        for i, p in enumerate(forth)
     ]
-    own = pltpu.make_async_copy(x.at[:, :, columns(c)], out.at[:, head_of(c)], here)
-
-    @pl.when(owns(c))
+    pair = [
+        push(x if n == 0 else out.at[b], out.at[b], send.at[7 + n], recv.at[7 + n], twin)
+        for n, b in enumerate(held)
+    ]
+    own = pltpu.make_async_copy(x, out.at[mine], here)
+
+    @pl.when(step == 0)
     def _():
-        for copy in copies:
+        greet([side, twin] + [(at(p, xh, k), e) for p in forth])
+        for copy in [across, *first, pair[0], own]:
             copy.start()
-        own.start()
-
-    for s, copy in zip(sources, copies):
-        pl.when(owns(c))(copy.wait_send)
-        pl.when(owns(s))(copy.wait_recv)
-    pl.when(owns(c))(own.wait)
-
-
-def heads_call(kernel, x, shape, ident):
-    return pl.pallas_call(
-        kernel,
-        out_shape=jax.ShapeDtypeStruct(shape, x.dtype),
-        in_specs=[ANY],
-        out_specs=ANY,
-        scratch_shapes=[
-            pltpu.SemaphoreType.DMA,
-            pltpu.SemaphoreType.DMA((CTX - 1,)),
-            pltpu.SemaphoreType.DMA((CTX - 1,)),
-        ],
-        compiler_params=pltpu.CompilerParams(collective_id=ident, has_side_effects=True),
-    )(x)
-
-
-def to_heads(x, ident):
-    return heads_call(to_heads_kernel, x, (x.shape[0], HEAD_DIM, LEN), ident)
-
-
-def from_heads(x, ident):
-    return heads_call(from_heads_kernel, x, (x.shape[0], HEADS, HEAD_DIM, TOK), ident)
+
+    @pl.when(step == 2)
+    def _():
+        across.wait_recv()
+        for copy in [*second, pair[1]]:
+            copy.start()
+
+    @pl.when(step == 5)
+    def _():
+        for copy, hand in zip(first, pair[2:5]):
+            copy.wait_recv()
+            hand.start()
+
+    def finish():
+        for copy, hand in zip(second, pair[5:]):
+            copy.wait_recv()
+            hand.start()
+        for copy in pair:
+            copy.wait()
+        for copy in [across, *first, *second]:
+            copy.wait_send()
+        own.wait()
+
+    return finish
 
 
 def near_buckets():
@@ -295,8 +341,11 @@
     return pl.ds(pl.multiple_of(chunk * CHUNK, CHUNK), CHUNK)
 
 
-def forward_kernel(qkv_ref, table_ref, p_ref, o_ref, low_ref, inv_ref, keys, bias, scores):
+def forward_kernel(
+    qkv_ref, table_ref, tok_ref, p_ref, o_ref, low_ref, inv_ref, all_ref, keys, bias, scores, *sems
+):
     block = pl.program_id(0)
+    finish = spread_tokens(tok_ref, all_ref, *sems, block, LEN // QUERIES - 1)
 
     @pl.when(block == 0)
     def _():
@@ -334,9 +383,10 @@
     o_ref[...] = out
     low_ref[0] = out.astype(low)
     inv_ref[...] = inverse
-
-
-def attend(qkv, table):
+    pl.when(block == LEN // QUERIES - 1)(finish)
+
+
+def attend(qkv, table, rows, ident):
     whole = lambda *shape: pl.BlockSpec(shape, lambda i: (0,) * len(shape))
     return pl.pallas_call(
         forward_kernel,
@@ -346,27 +396,42 @@
             jax.ShapeDtypeStruct((HEAD_DIM, LEN), wide),
             jax.ShapeDtypeStruct((1, HEAD_DIM, LEN), low),
             jax.ShapeDtypeStruct((1, LEN), wide),
+            jax.ShapeDtypeStruct((CTX, *rows.shape), rows.dtype),
         ),
-        in_specs=[whole(3, HEAD_DIM, LEN), pl.BlockSpec(memory_space=pltpu.SMEM)],
+        in_specs=[whole(3, HEAD_DIM, LEN), pl.BlockSpec(memory_space=pltpu.SMEM), ANY],
         out_specs=(
             pl.BlockSpec((LEN, QUERIES), lambda i: (0, i)),
             pl.BlockSpec((HEAD_DIM, QUERIES), lambda i: (0, i)),
             pl.BlockSpec((1, HEAD_DIM, QUERIES), lambda i: (0, 0, i)),
             pl.BlockSpec((1, QUERIES), lambda i: (0, i)),
+            ANY,
         ),
         scratch_shapes=[
             pltpu.VMEM((LEN, HEAD_DIM), low),
             pltpu.VMEM((6 * CHUNK, QUERIES), wide),
             pltpu.VMEM((LEN, QUERIES), wide),
+            pltpu.SemaphoreType.DMA,
+            pltpu.SemaphoreType.DMA((15,)),
+            pltpu.SemaphoreType.DMA((15,)),
         ],
-        compiler_params=pltpu.CompilerParams(vmem_limit_bytes=32 << 20),
-    )(qkv, table)
+        compiler_params=pltpu.CompilerParams(
+            collective_id=ident, has_side_effects=True, vmem_limit_bytes=32 << 20
+        ),
+    )(qkv, table, rows)
 
 
 def backward_kernel(
-    qkv_ref, p_ref, o_ref, inv_ref, do_ref, grad_ref, sums_ref, values, dk, dv, tiles, slopes
+    qkv_ref, p_ref, o_ref, inv_ref, do_ref, x_ref, grad_ref, sums_ref, y_ref,
+    values, dk, dv, tiles, slopes, send, recv,
 ):
     block = pl.program_id(0)
+    size, me, device = group("x")
+    across = push(x_ref.at[:, :, 1 - me], y_ref, send, recv, device(1 - me))
+
+    @pl.when(block == 0)
+    def _():
+        greet([device(1 - me)])
+        across.start()
 
     @pl.when(block == 0)
     def _():
@@ -410,9 +475,10 @@
         grad_ref[1] = dk[...].T.astype(low)
         grad_ref[2] = dv[...].T.astype(low)
         sums_ref[...] = tiles[...]
-
-
-def attend_back(qkv, probs, out, inverse, grad_out):
+        across.wait()
+
+
+def attend_back(qkv, probs, out, inverse, grad_out, grads, ident):
     whole = lambda *shape: pl.BlockSpec(shape, lambda i: (0,) * len(shape))
     return pl.pallas_call(
         backward_kernel,
@@ -420,6 +486,7 @@
         out_shape=(
             jax.ShapeDtypeStruct((3, HEAD_DIM, LEN), low),
             jax.ShapeDtypeStruct((6 * CHUNK, QUERIES), wide),
+            jax.ShapeDtypeStruct(grads.shape[:2] + grads.shape[3:], grads.dtype),
         ),
         in_specs=[
             whole(3, HEAD_DIM, LEN),
@@ -427,17 +494,22 @@
             pl.BlockSpec((HEAD_DIM, QUERIES), lambda i: (0, i)),
             pl.BlockSpec((1, QUERIES), lambda i: (0, i)),
             pl.BlockSpec((1, HEAD_DIM, QUERIES), lambda i: (0, 0, i)),
+            ANY,
         ],
-        out_specs=(whole(3, HEAD_DIM, LEN), whole(6 * CHUNK, QUERIES)),
+        out_specs=(whole(3, HEAD_DIM, LEN), whole(6 * CHUNK, QUERIES), ANY),
         scratch_shapes=[
             pltpu.VMEM((LEN, HEAD_DIM), low),
             pltpu.VMEM((LEN, HEAD_DIM), wide),
             pltpu.VMEM((LEN, HEAD_DIM), wide),
             pltpu.VMEM((6 * CHUNK, QUERIES), wide),
             pltpu.VMEM((LEN, QUERIES), low),
+            pltpu.SemaphoreType.DMA,
+            pltpu.SemaphoreType.DMA,
         ],
-        compiler_params=pltpu.CompilerParams(vmem_limit_bytes=32 << 20),
-    )(qkv, probs, out, inverse, grad_out)
+        compiler_params=pltpu.CompilerParams(
+            collective_id=ident, has_side_effects=True, vmem_limit_bytes=32 << 20
+        ),
+    )(qkv, probs, out, inverse, grad_out, grads)
 
 
 def rms_scale(values_in, gain_vec):
@@ -510,7 +582,12 @@
     h_one = normed_one.astype(low)
     qkv = dot(qkv_full, h_one, (0, 1)).astype(low).reshape(3, HEADS, HEAD_DIM, TOK)
     head_qkv = to_heads(qkv, 4)
-    probs, attended, attended_head, inverse = attend(head_qkv, head_table)
+    place = jnp.arange(D, dtype=jnp.int32)
+    place = place // 6 % EXP * TOK + place // 48 * 8 + place % 6
+    by_owner = (place[:, None] == jnp.arange(EXP * TOK, dtype=jnp.int32)[None, :]).astype(low)
+    probs, attended, attended_head, inverse, h_all = attend(
+        head_qkv, head_table, dot(h_one, by_owner).astype(low), 18
+    )
     attended_low = from_heads(attended_head, 5).reshape(D, TOK)
     residual = x_rows + dot(attended_low, out_full, (0, 0))
     normed_two, norm_two_back = jax.vjp(rms_scale, residual, gain_two)
@@ -577,13 +654,28 @@
     grad_residual = grad_out + grad_resid_norm
     grad_branch = grad_residual.astype(low)
     grad_attended = dot(out_full, grad_branch, (1, 1)).astype(low)
-    head_grad = to_heads(grad_attended.reshape(1, HEADS, HEAD_DIM, TOK), 10)
-    head_grads, tile_sums = attend_back(head_qkv, probs, attended, inverse, head_grad)
-    grad_qkv = from_heads(head_grads, 11).reshape(3 * D, TOK)
-
-    grad_h_one = dot(grad_qkv, qkv_full, (0, 1))
-    grad_x_norm, grad_gain_one = norm_one_back(grad_h_one)
-    grad_tokens = grad_residual + grad_x_norm
+    late = jnp.concatenate(
+        [
+            dot(attended_low, grad_branch).astype(low),
+            grad_router.astype(low),
+            grad_gain_two[:, None].astype(low),
+            jnp.zeros((D, 111), low),
+        ],
+        axis=1,
+    ).reshape(ZED, 4, 48, 896)
+    head_grad, others = swaps(
+        10,
+        (grad_attended.reshape(1, HEADS, HEAD_DIM, TOK), "to_heads", None, True),
+        (late, "quad", 1, False),
+    )
+    late = add_up(late, "quad", 1, others).astype(low)
+    head_grads, tile_sums, others = attend_back(
+        head_qkv, probs, attended, inverse, head_grad, expert_grads, 19
+    )
+    expert_grads = add_up(expert_grads, "x", 2, others[None])
+    grad_expert_in = jnp.swapaxes(expert_grads[0], 1, 2)
+    grad_expert_out = expert_grads[1]
+
     bucket_sums = jnp.sum(
         jnp.where(
             near_buckets()[None] == jnp.arange(BUCKETS, dtype=jnp.int32)[:, None, None],
@@ -592,51 +684,46 @@
         ),
         axis=(1, 2),
     )
-    grad_table = jnp.where(my_head[None, :], bucket_sums[:, None], 0.0)
-    table_column = jnp.pad(grad_table.reshape(128, 3), ((0, 0), (0, 3))).reshape(D, 1)
-    shared = jnp.concatenate(
-        [
-            dot(h_one, grad_qkv, (0, 1)).astype(low),
-            dot(attended_low, grad_branch).astype(low),
-            grad_router.astype(low),
-            grad_gain_one[:, None].astype(low),
-            grad_gain_two[:, None].astype(low),
-            table_column.astype(low),
-            jnp.zeros((D, 109), low),
-        ],
-        axis=1,
-    )
-    shared = shared.reshape(8, 2, 48, 3200)
-    shared = add_up(shared, "core", 1, swaps(14, (shared, "core", 1, False))[0])
-    shared = shared.astype(low).reshape(4, 2, 48, 3200)
-    others, expert_others = swaps(15, (shared, "z", 0, False), (expert_grads, "x", 2, False))
-    expert_grads = add_up(expert_grads, "x", 2, expert_others)
-    grad_expert_in = jnp.swapaxes(expert_grads[0], 1, 2)
-    grad_expert_out = expert_grads[1]
-    shared = add_up(shared, "z", 0, others).astype(low)
-    shared = add_up(shared, "x", 0, swaps(16, (shared, "x", 0, False))[0]).astype(low)
-    lines = jnp.concatenate(
-        [
-            shared[:, : 4 * D].reshape(EXP, 16, 1152),
-            jnp.pad(
-                shared[:, 4 * D : 4 * D + 19].reshape(EXP, 1, 114), ((0, 0), (0, 15), (0, 14))
-            ),
-        ],
-        axis=2,
-    )
-    lines = add_up(lines, "exp", 0, swaps(17, (lines, "exp", 0, False))[0])
-    matrix = lines[:, :1152].reshape(6, 4 * D)
-    small = lines[0, 1152:1266].reshape(6, 19)
+    sixth = jnp.arange(EXP * TOK, dtype=jnp.int32) % 8 == 6
+    head_weights = dot(h_all.reshape(LEN, EXP * TOK), head_grads.reshape(192, LEN), (0, 1))
+    head_weights = head_weights + jnp.where(
+        sixth[:, None], jnp.pad(bucket_sums, (0, 192 - BUCKETS))[None, :], 0.0
+    )
+    head_weights = head_weights.astype(low).reshape(EXP, TOK, 192)
+    grad_qkv, others, late_others = swaps(
+        11,
+        (head_grads, "from_heads", None, True),
+        (head_weights, "exp", 0, False),
+        (late, "z", 0, False),
+    )
+    grad_qkv = grad_qkv.reshape(3 * D, TOK)
+    head_weights = add_up(head_weights, "exp", 0, others).reshape(CTX, 8, 192)
+    late = add_up(late, "z", 0, late_others).reshape(EXP, 6, 896)
+    late = jnp.pad(late, ((0, 0), (0, 2), (0, 0)))
+    by_head, others = swaps(
+        12, (head_weights, "head_rows", None, True), (late, "exp", 0, False)
+    )
+    late = add_up(late, "exp", 0, others)
+    grad_qkv_weight = jnp.transpose(
+        by_head[:, :6].reshape(HEADS, 6, 3, HEAD_DIM), (1, 2, 0, 3)
+    ).reshape(6, 3 * D)
+    own_weight = jnp.concatenate([query_weight, kv_weight], axis=1).astype(wide)
+    grad_gain_one = jnp.sum(own_weight * grad_qkv_weight, axis=1) / norm_gain_one.astype(wide)
+    grad_table = by_head[:, 6, :BUCKETS].T.reshape(-1)
+    grad_table = lax.dynamic_slice(grad_table, (3 * (c * EXP + lax.axis_index("exp")),), (3,))
+
+    grad_h_one = dot(grad_qkv, qkv_full, (0, 1))
+    grad_tokens = grad_residual + norm_one_back(grad_h_one)[0]
     return (
         mixed_rows[None],
         grad_tokens[None],
-        matrix[:, :D],
-        matrix[:, D : 3 * D],
-        matrix[:, 3 * D :],
-        small[:, 16],
-        small[:, 17],
-        small[:, :16],
-        small[:3, 18],
+        grad_qkv_weight[:, :D],
+        grad_qkv_weight[:, D:],
+        late[:6, :D],
+        grad_gain_one,
+        late[:6, D + 16],
+        late[:6, D : D + 16],
+        grad_table,
         grad_expert_in,
         grad_expert_out,
     )

time: 396 us -> 384 us (0.970)
  Pallas kernels: 272 us -> 260 us
    pallas_call x4 -> x0, Pallas kernels: 44.4 us -> none  [heads_call(): pl.pallas_call(kernel, out_shape=jax.ShapeDtypeStruct(shape, x.dtype), in...]
    pallas_call x9 -> x10, Pallas kernels: 137 us -> 158 us  [swaps(): pl.pallas_call(functools.partial(swaps_kernel, [item[1:] for item in item...]
    pallas_call x1, Pallas kernels: 21.1 us -> 29.9 us  [attend(): pl.pallas_call(forward_kernel, grid=(LEN // QUERIES,), out_shape=(jax.Sha...]
    concatenate x1 -> x4, local copies, waits for them, and re-layouts: 8.44 us -> 1.56 us  [shards(): jnp.concatenate([dot(attended_low, grad_branch).astype(low), grad_router....]
    dot_general x23 -> x24, matrix products: 36.8 us -> 35.7 us  [dot(): lax.dot_general(a, b, (((dims[0],), (dims[1],)), ((), ())), preferred_ele...]
    unnamed x116 -> x92, local copies, waits for them, and re-layouts: 16.7 us -> 16.7 us
where the time goes in v3:
time: 384 us; the launch traced here: 381 us
  Pallas kernels  260 us (68%)
  local copies, waits for them, and re-layouts  48.8 us (13%)
  matrix products  38.4 us (10%)
  other arithmetic  32.6 us (8%)
    pallas_call x10, Pallas kernels, swaps(): pl.pallas_call(functools.partial(swaps_kernel, [item[1:] for item in item...  158 us
    pallas_call x1, Pallas kernels, gather_weights(): pl.pallas_call(weights_kernel, out_shape=(jax.ShapeDtypeStruct((CTX, *x.s...  44.4 us
    dot_general x24, matrix products, dot(): lax.dot_general(a, b, (((dims[0],), (dims[1],)), ((), ())), preferred_ele...  35.7 us
    pallas_call x1, Pallas kernels, attend(): pl.pallas_call(forward_kernel, grid=(LEN // QUERIES,), out_shape=(jax.Sha...  29.9 us
    pallas_call x1, Pallas kernels, attend_back(): pl.pallas_call(backward_kernel, grid=(LEN // QUERIES,), out_shape=(jax.Sh...  28 us
    unnamed x92, local copies, waits for them, and re-layouts  16.7 us

profile of v3, /device:TPU:1, one launch (start us, length us, event | category | flops | bytes accessed | tf_op | source)
XLA Modules:
  0.0 381.4 jit_solution(3533225510837996150)
XLA Ops:
  5.3 10.0 %shard_map.203 = bf16[8,16,1280]{2,1,0:T(8,128)(2,1)} custom-call(bf16[16,1280]{1,0:T(8,128)(2,1)} %fusion.75.refs_0_), custom_call_target="tpu_custom_call" | custom-call | tf_op jit(solution)/shard_map/pallas_call | solution.py:157
  17.7 44.4 %shard_map.204 = (bf16[16,48,3200]{2,1,0:T(8,128)(2,1)}, bf16[2,2,4,192,768]{4,3,2,1,0:T(8,128)(2,1)S(1)}) custom-call(bf16[48,3200]{1,0:T(8,128)(2,1)S(1)} %fusion.60.x, bf16[2,2,192,768]{3,2,1,0:T(8,128)(2,1)S(1)} %pad_maximum_fusion.1.w), custom_call_target="tpu_custom_call" | custom-call | tf_op jit(solution)/shard_map/pallas_call | solution.py:240
  62.2 2.1 copy-done.5
  64.3 1.4 fusion.138
  66.0 4.0 %convolution_convert_fusion = bf16[2304,128]{1,0:T(8,128)(2,1)} fusion(bf16[768,3200]{1,0:T(8,128)(2,1)} %bitcast.7, bf16[1,128,768]{2,1,0:T(8,128)(2,1)S(1)} %copy-done.19, f32[768]{0:T(1024)S(1)} %convert_reduce_fusion.5, f32[128]{0:T(128)S(1)} %fusion.130), kind=kOutput, calls=%fused_computation.5 | convolution fusion | flops 453672960 | bytes 4328960 | tf_op jit(solution)/shard_map/dot_general | solution.py:524
  70.0 14.0 %shard_map.205.qkv_ref = bf16[3,64,2048]{2,1,0:T(8,128)(2,1)} custom-call(bf16[3,12,64,128]{3,2,1,0:T(8,128)(2,1)} %bitcast.184), custom_call_target="tpu_custom_call" | custom-call | tf_op jit(solution)/shard_map/pallas_call | solution.py:157
  85.5 29.9 %shard_map.206 = (bf16[2048,2048]{1,0:T(8,128)(2,1)S(1)}, f32[64,2048]{1,0:T(8,128)S(1)}, bf16[1,64,2048]{2,1,0:T(8,128)(2,1)S(1)}, f32[1,2048]{1,0:T(1,128)S(1)}, bf16[16,128,1024]{2,1,0:T(8,128)(2,1)S(1)}) custom-call(bf16[3,64,2048]{2,1,0:T(8,128)(2,1)S(1)} %copy-done.2, f32[32]{0:T(128)S(1)} %reduce_sum.200.table_ref, bf16[128,1024]{1,0:T(8,128)(2,1)S(1)} %fusion.7.tok_ref), custom_call_target="tpu_custom_call" | custom-call | tf_op jit(solution)/shard_map/pallas_call | solution.py:391
  115.3 3.2 copy-done
  120.0 2.0 copy-done.11
  122.0 8.4 %shard_map.207 = bf16[1,12,64,128]{3,2,1,0:T(8,128)(2,1)} custom-call(bf16[1,64,2048]{2,1,0:T(8,128)(2,1)} %copy-done.9), custom_call_target="tpu_custom_call" | custom-call | tf_op jit(solution)/shard_map/pallas_call | solution.py:157
  130.4 1.8 multiply_reduce_fusion.2
  135.2 9.4 %shard_map.208 = bf16[8,48,768]{2,1,0:T(8,128)(2,1)} custom-call(bf16[8,48,768]{2,1,0:T(8,128)(2,1)} %bitcast.181), custom_call_target="tpu_custom_call" | custom-call | tf_op jit(solution)/shard_map/pallas_call | solution.py:157
  144.7 2.3 convolution_convert_fusion.8.refs_0_
  147.0 23.4 %shard_map.209 = bf16[4,320,768]{2,1,0:T(8,128)(2,1)} custom-call(bf16[320,768]{1,0:T(8,128)(2,1)} %convolution_convert_fusion.8.refs_0_), custom_call_target="tpu_custom_call" | custom-call | tf_op jit(solution)/shard_map/pallas_call | solution.py:157
  170.3 1.6 fusion.139
  172.0 2.6 fusion.14
  174.6 2.6 fusion.31
  181.9 1.5 pad_maximum_fusion
  183.4 25.1 %shard_map.210 = bf16[3,320,768]{2,1,0:T(8,128)(2,1)} custom-call(bf16[4,320,768]{2,1,0:T(8,128)(2,1)} %bitcast.161), custom_call_target="tpu_custom_call" | custom-call | tf_op jit(solution)/shard_map/pallas_call | solution.py:157
  208.5 1.7 convert_reduce_fusion
  210.3 2.5 convolution_convert_fusion.6
  212.7 2.2 convolution_convert_fusion.1
  217.8 2.3 maximum_maximum_fusion.refs_1_
  220.1 12.8 %shard_map.211 = (bf16[8,48,768]{2,1,0:T(8,128)(2,1)}, bf16[1,2,2,2,192,768]{5,4,3,2,1,0:T(8,128)(2,1)}) custom-call(bf16[8,48,768]{2,1,0:T(8,128)(2,1)} %bitcast.168, bf16[2,2,2,2,192,768]{5,4,3,2,1,0:T(8,128)(2,1)} %maximum_maximum_fusion.refs_1_), custom_call_target="tpu_custom_call" | custom-call | tf_op jit(solution)/shard_map/pallas_call | solution.py:157
  232.9 1.5 fusion.59
  235.2 1.5 multiply_reduce_fusion
  236.8 2.4 convolution_convert_fusion.13
  243.4 25.5 %shard_map.212 = (bf16[1,64,2048]{2,1,0:T(8,128)(2,1)}, bf16[3,4,48,896]{3,2,1,0:T(8,128)(2,1)}) custom-call(bf16[1,12,64,128]{3,2,1,0:T(8,128)(2,1)} %bitcast.193, bf16[4,4,48,896]{3,2,1,0:T(8,128)(2,1)} %copy.76.refs_1_), custom_call_target="tpu_custom_call" | custom-call | tf_op jit(solution)/shard_map/pallas_call | solution.py:157
  268.9 3.0 fusion.x_ref
  272.0 3.4 copy-done.1
  275.4 28.0 %shard_map.213 = (bf16[3,64,2048]{2,1,0:T(8,128)(2,1)S(1)}, f32[768,256]{1,0:T(8,128)S(1)}, bf16[2,2,192,768]{3,2,1,0:T(8,128)(2,1)S(1)}) custom-call(bf16[3,64,2048]{2,1,0:T(8,128)(2,1)S(1)} %copy-done.2, bf16[2048,2048]{1,0:T(8,128)(2,1)S(1)} %copy-done.1, f32[64,2048]{1,0:T(8,128)S(1)} %copy-done.8, f32[1,2048]{1,0:T(1,128)S(1)} %get-tuple-element.36.inv_ref, ...), custom_call_target="tpu_custom_call" | custom-call | tf_op jit(solution)/shard_map/pallas_call | solution.py:483
  305.3 3.7 select_reduce_fusion
  311.0 1.4 convert_reduce_fusion.1
  312.5 1.8 fusion.43.refs_2_
  314.2 18.3 %shard_map.214 = (bf16[3,12,64,128]{3,2,1,0:T(8,128)(2,1)}, bf16[7,128,192]{2,1,0:T(8,128)(2,1)}, bf16[3,48,896]{2,1,0:T(8,128)(2,1)}) custom-call(bf16[3,64,2048]{2,1,0:T(8,128)(2,1)} %copy-done.6, bf16[8,128,192]{2,1,0:T(8,128)(2,1)} %bitcast.165, bf16[4,48,896]{2,1,0:T(8,128)(2,1)} %fusion.43.refs_2_), custom_call_target="tpu_custom_call" | custom-call | tf_op jit(solution)/shard_map/pallas_call | solution.py:157
  332.6 3.6 fusion.55
  337.3 1.5 convert_add_fusion.5.refs_0_
  340.4 1.8 convert_reduce_fusion.3
  342.2 1.6 reduce_sum.218
  346.2 10.7 %shard_map.215 = (f32[12,8,192]{2,1,0:T(8,128)}, f32[7,8,896]{2,1,0:T(8,128)}) custom-call(f32[16,8,192]{2,1,0:T(8,128)} %convert_add_fusion.5.refs_0_, f32[8,8,896]{2,1,0:T(8,128)} %pad.24.refs_1_), custom_call_target="tpu_custom_call" | custom-call | tf_op jit(solution)/shard_map/pallas_call | solution.py:157
  357.0 1.7 reshape.364
  358.6 1.6 copy.78
  360.2 1.6 reshape.365
  363.2 1.4 slice.134
  364.6 1.6 reduce_sum.219
  369.5 1.6 reshape.377
  375.5 1.4 slice.113
  379.8 1.6 slice_bitcast_fusion
  (175 shorter events, 46.4 us)
Async XLA Ops:
  0.6 16.9 %copy-start.26 = (bf16[2,192,768]{2,1,0:T(8,128)(2,1)S(1)}, bf16[2,192,768]{2,1,0:T(8,128)(2,1)}, u32[]{:S(2)}) copy-start(bf16[2,192,768]{2,1,0:T(8,128)(2,1)} %param.23) | copy-start | bytes 1769476
  0.7 16.9 %copy-start.27 = (bf16[2,768,192]{1,2,0:T(8,128)(2,1)S(1)}, bf16[2,768,192]{1,2,0:T(8,128)(2,1)}, u32[]{:S(2)}) copy-start(bf16[2,768,192]{1,2,0:T(8,128)(2,1)} %param.22) | copy-start | bytes 1769476
  17.6 48.3 %copy-start.19 = (bf16[1,128,768]{2,1,0:T(8,128)(2,1)S(1)}, bf16[1,128,768]{2,1,0:T(8,128)(2,1)}, u32[]{:S(2)}) copy-start(bf16[1,128,768]{2,1,0:T(8,128)(2,1)} %param.12) | copy-start | bytes 589828
  62.2 2.1 copy-start.5
  66.0 4.0 %copy-start.36 = (f32[128]{0:T(128)}, f32[128]{0:T(128)S(1)}, u32[]{:S(2)}) copy-start(f32[128]{0:T(128)S(1)} %fusion.52) | copy-start | bytes 1540
  84.0 1.4 copy-start.2
  85.4 48.3 %copy-start.35 = (s32[1,128,1]{1,2,0:T(1,128)S(1)}, s32[1,128,1]{1,2,0:T(1,128)}, u32[]{:S(2)}) copy-start(s32[1,128,1]{1,2,0:T(1,128)} %param.14) | copy-start | bytes 1540
  85.4 48.3 %copy-start.22 = (bf16[1,128,768]{2,1,0:T(8,128)(2,1)S(1)}, bf16[1,128,768]{2,1,0:T(8,128)(2,1)}, u32[]{:S(2)}) copy-start(bf16[1,128,768]{2,1,0:T(8,128)(2,1)} %param.13) | copy-start | bytes 589828
  115.3 3.2 copy-start
  118.6 0.8 copy-start.7
  119.3 0.7 copy-start.9
  120.0 2.0 copy-start.11
  147.0 30.2 %slice-start = ((s8[4718592]{0:T(1024)(128)(4,1)}), s8[524288]{0:T(1024)(128)(4,1)S(1)}, s32[]{:S(2)}) async-start(s8[4718592]{0:T(1024)(128)(4,1)} %bitcast.151), calls=%async_computation | async-start | bytes 1048576
  172.0 5.2 %copy-start.17 = (bf16[4,1,80,768]{3,2,1,0:T(8,128)(2,1)}, bf16[4,1,80,768]{3,2,1,0:T(8,128)(2,1)S(1)}, u32[]{:S(2)}) copy-start(bf16[4,1,80,768]{3,2,1,0:T(8,128)(2,1)S(1)} %get-tuple-element.60) | copy-start | bytes 1474564
  172.0 5.2 %copy-start.30 = (bf16[4,1,80,768]{3,2,1,0:T(8,128)(2,1)}, bf16[4,1,80,768]{3,2,1,0:T(8,128)(2,1)S(1)}, u32[]{:S(2)}) copy-start(bf16[4,1,80,768]{3,2,1,0:T(8,128)(2,1)S(1)} %get-tuple-element.59) | copy-start | bytes 1474564
  172.0 6.0 %copy-start.15 = (bf16[4,1,80,768]{3,2,1,0:T(8,128)(2,1)}, bf16[4,1,80,768]{3,2,1,0:T(8,128)(2,1)S(1)}, u32[]{:S(2)}) copy-start(bf16[4,1,80,768]{3,2,1,0:T(8,128)(2,1)S(1)} %get-tuple-element.61) | copy-start | bytes 1474564
  172.0 6.6 %copy-start.28 = (bf16[4,1,80,768]{3,2,1,0:T(8,128)(2,1)}, bf16[4,1,80,768]{3,2,1,0:T(8,128)(2,1)S(1)}, u32[]{:S(2)}) copy-start(bf16[4,1,80,768]{3,2,1,0:T(8,128)(2,1)S(1)} %get-tuple-element.58) | copy-start | bytes 1474564
  172.0 5.2 %slice-start.1 = ((s8[4718592]{0:T(1024)(128)(4,1)}), s8[4194304]{0:T(1024)(128)(4,1)S(1)}, s32[]{:S(2)}) async-start(s8[4718592]{0:T(1024)(128)(4,1)} %bitcast.151), calls=%async_computation.1 | async-start | bytes 8388608
  174.6 5.8 %copy-start.23 = (f32[320,768]{1,0:T(8,128)}, f32[320,768]{1,0:T(8,128)S(1)}, u32[]{:S(2)}) copy-start(f32[320,768]{1,0:T(8,128)S(1)} %fusion.14) | copy-start | bytes 2949124
  177.2 0.8 copy-start.39
  178.6 2.5 copy-start.24
  179.6 0.8 copy-start.41
  208.5 4.2 %copy-start.31 = (bf16[4,1,80,768]{3,2,1,0:T(8,128)(2,1)S(1)}, bf16[4,1,80,768]{3,2,1,0:T(8,128)(2,1)}, u32[]{:S(2)}) copy-start(bf16[4,1,80,768]{3,2,1,0:T(8,128)(2,1)} %copy-done.30) | copy-start | bytes 1474564
  212.7 2.2 copy-start.25
  212.7 2.2 copy-start.29
  214.9 1.0 copy-start.18
  215.0 1.2 copy-start.40
  215.0 1.9 copy-start.16
  215.0 1.9 copy-start.42
  236.7 3.5 copy-start.21
  241.0 1.2 copy-start.13
  268.9 3.0 copy-start.8
  268.9 3.0 copy-start.10
  272.0 3.4 copy-start.1
  275.4 33.6 %copy-start.12 = (bf16[16,128,1024]{2,1,0:T(8,128)(2,1)S(1)}, bf16[16,128,1024]{2,1,0:T(8,128)(2,1)}, u32[]{:S(2)}) copy-start(bf16[16,128,1024]{2,1,0:T(8,128)(2,1)} %copy-done.11) | copy-start | bytes 12582916
  303.4 1.0 copy-start.3
  304.4 4.5 %copy-start.6 = (bf16[3,64,2048]{2,1,0:T(8,128)(2,1)}, bf16[3,64,2048]{2,1,0:T(8,128)(2,1)S(1)}, u32[]{:S(2)}) copy-start(bf16[3,64,2048]{2,1,0:T(8,128)(2,1)S(1)} %get-tuple-element.39.refs_0_) | copy-start | bytes 2359300
  332.6 3.7 copy-start.37
  332.6 3.7 copy-start.20
  332.6 4.6 %copy-start.32 = (bf16[7,128,192]{2,1,0:T(8,128)(2,1)S(1)}, bf16[7,128,192]{2,1,0:T(8,128)(2,1)}, u32[]{:S(2)}) copy-start(bf16[7,128,192]{2,1,0:T(8,128)(2,1)} %get-tuple-element.44) | copy-start | bytes 1032196
  337.2 30.9 %copy-start.34 = (bf16[6,768]{1,0:T(8,128)(2,1)S(1)}, bf16[6,768]{1,0:T(8,128)(2,1)}, u32[]{:S(2)}) copy-start(bf16[6,768]{1,0:T(8,128)(2,1)} %param.15) | copy-start | bytes 27652
  339.7 32.6 %copy-start.38 = (bf16[6]{0:T(256)(128)(2,1)S(1)}, bf16[6]{0:T(256)(128)(2,1)}, u32[]{:S(2)}) copy-start(bf16[6]{0:T(256)(128)(2,1)} %param.18) | copy-start | bytes 40
  340.4 39.2 %copy-start.4 = (bf16[2,2,192,768]{3,2,1,0:T(8,128)(2,1)S(1)}, bf16[2,2,192,768]{3,2,1,0:T(8,128)(2,1)}, u32[]{:S(2)}) copy-start(bf16[2,2,192,768]{3,2,1,0:T(8,128)(2,1)} %copy-done.3) | copy-start | bytes 3538948
  344.8 0.7 copy-start.14
  366.9 0.6 copy-start.33

commit v4 on v3

v4 whole, which is shorter than its diff:
```python
import functools

import jax
import jax.numpy as jnp
from jax import lax
from jax.experimental import pallas as pl
from jax.experimental.pallas import tpu as pltpu
from jax.sharding import PartitionSpec as P

MESH = pl.DeviceIdType.MESH
HEADS = 12
HEAD_DIM = 64
BUCKETS = 32
TOK = 128
D = 768
CAP = 10
SLOTS = 48
CTX, EXP, ZED = 16, 8, 4
LEN = TOK * CTX
QUERIES = 256
CHUNK = 128
epsilon = 1e-06
bucket_edges = (12, 16, 23, 32, 46, 64, 91)
low = jnp.bfloat16
wide = jnp.float32
ANY = pl.BlockSpec(memory_space=pl.ANY)


def spot():
    c, e = lax.axis_index("ctx"), lax.axis_index("exp")
    return c, e, c // 4, (c // 2) % 2, c % 2


def greet(peers):
    barrier = pltpu.get_barrier_semaphore()
    for peer in peers:
        pl.semaphore_signal(barrier, inc=1, device_id=peer, device_id_type=MESH)
    pl.semaphore_wait(barrier, len(peers))


def push(src, dst, send, recv, to):
    return pltpu.make_async_remote_copy(
        src_ref=src, dst_ref=dst, send_sem=send, recv_sem=recv, device_id=to, device_id_type=MESH
    )


def group(kind):
    c, e, z, xh, k = spot()
    if kind == "exp":
        return EXP, e, lambda i: (c, i)
    if kind == "z":
        return ZED, z, lambda i: (i * 4 + xh * 2 + k, e)
    if kind == "x":
        return 2, xh, lambda i: (z * 4 + i * 2 + k, e)
    if kind == "core":
        return 2, k, lambda i: (z * 4 + xh * 2 + i, e)
    if kind == "quad":
        return 4, xh * 2 + k, lambda i: (z * 4 + i, e)
    return CTX, c, lambda i: (i, e)


SIZES = {"exp": EXP, "z": ZED, "x": 2, "core": 2, "quad": 4}


def head_of(c):
    return jnp.minimum((c // 4) * 3 + c % 4, HEADS - 1)


def owns(c):
    return c % 4 < 3


def columns(c):
    return pl.ds(pl.multiple_of(c * TOK, TOK), TOK)


def when(condition, step):
    if condition is None:
        step()
    else:
        pl.when(condition)(step)


def heads_parts(kind, me, x, out):
    if kind == "to_heads":
        return lambda to: x.at[:, head_of(to)], out.at[:, :, columns(me)], None, owns
    if kind == "from_heads":
        return lambda to: x.at[:, :, columns(to)], out.at[head_of(me)], owns, None
    return lambda to: x.at[to], out.at[head_of(me)], owns, None


def swaps_kernel(plan, *refs):
    n = len(plan)
    xs, outs, (send, recv, here) = refs[:n], refs[n : 2 * n], refs[2 * n :]
    kinds = dict.fromkeys("ctx" if kind not in SIZES else kind for kind, axis, keep in plan)
    if "ctx" in kinds:
        kinds = [kind for kind in kinds if kind in ("ctx", "exp")]
    peers = []
    for kind in kinds:
        size, me, device = group(kind)
        peers += [device(lax.rem(me + i, size)) for i in range(1, size)]
    greet(peers)
    copies, count = [], 0
    for (kind, axis, keep), x, out in zip(plan, xs, outs):
        size, me, device = group(kind)
        if kind in SIZES:
            part = lambda i: x if axis is None else x.at[(slice(None),) * axis + (i,)]
            sends = receives = None
        else:
            part, place, sends, receives = heads_parts(kind, me, x, out)
        for i in range(1, size):
            to, source = lax.rem(me + i, size), lax.rem(me + size - i, size)
            if kind in SIZES:
                place = out.at[me if keep else i - 1]
            copy = push(part(to), place, send.at[count], recv.at[count], device(to))
            if sends is not None:
                out_if, in_if = sends(me), sends(source)
            elif receives is not None:
                out_if, in_if = receives(to), receives(me)
            else:
                out_if = in_if = None
            when(out_if, copy.start)
            copies.append((copy, out_if, in_if))
            count += 1
    own = []
    for n, ((kind, axis, keep), x, out) in enumerate(zip(plan, xs, outs)):
        size, me, device = group(kind)
        if kind in SIZES and keep:
            part = x if axis is None else x.at[(slice(None),) * axis + (me,)]
            own.append((pltpu.make_async_copy(part, out.at[me], here.at[n]), None))
        elif kind not in SIZES:
            part, place, sends, receives = heads_parts(kind, me, x, out)
            own.append((pltpu.make_async_copy(part(me), place, here.at[n]), owns(me)))
    for copy, condition in own:
        when(condition, copy.start)
    for copy, out_if, in_if in copies:
        when(out_if, copy.wait_send)
        when(in_if, copy.wait_recv)
    for copy, condition in own:
        when(condition, copy.wait)


def swaps(ident, *items):
    shapes, total = [], 0
    for x, kind, axis, keep in items:
        block = x.shape if axis is None else x.shape[:axis] + x.shape[axis + 1 :]
        if kind == "to_heads":
            shape = (x.shape[0], HEAD_DIM, LEN)
        elif kind == "from_heads":
            shape = (HEADS, x.shape[0], HEAD_DIM, TOK)
        elif kind == "head_rows":
            shape = (HEADS, *x.shape[1:])
        else:
            shape = (SIZES[kind] - (not keep), *block)
        shapes.append(jax.ShapeDtypeStruct(shape, x.dtype))
        total += SIZES.get(kind, CTX) - 1
    return pl.pallas_call(
        functools.partial(swaps_kernel, [item[1:] for item in items]),
        out_shape=shapes,
        in_specs=[ANY] * len(items),
        out_specs=[ANY] * len(items),
        scratch_shapes=[
            pltpu.SemaphoreType.DMA((total,)),
            pltpu.SemaphoreType.DMA((total,)),
            pltpu.SemaphoreType.DMA((len(items),)),
        ],
        compiler_params=pltpu.CompilerParams(
            collective_id=ident, has_side_effects=True, vmem_limit_bytes=2 << 20
        ),
    )(*[item[0] for item in items])


def swap(x, kind, ident, axis=None):
    return swaps(ident, (x, kind, axis, True))[0]


def add_up(x, kind, axis, others):
    mine = lax.dynamic_index_in_dim(x, group(kind)[1], axis, keepdims=False)
    return mine.astype(wide) + jnp.sum(others.astype(wide), axis=0)


def quad_slab(out, xh, k):
    return out.at[:, xh * 2 + k]


def quad_parts(w, out, here, send, recv):
    c, e, z, xh, k = spot()
    side, twin = (z * 4 + (1 - xh) * 2 + k, e), (z * 4 + xh * 2 + 1 - k, e)
    mine, theirs = quad_slab(out, xh, k), quad_slab(out, 1 - xh, k)
    across = push(w, mine, send.at[0], recv.at[0], side)
    pair = push(w, mine, send.at[1], recv.at[1], twin)
    hand = push(theirs, theirs, send.at[2], recv.at[2], twin)
    own = pltpu.make_async_copy(w, mine, here)

    def begin():
        across.start()
        pair.start()
        own.start()

    def forward():
        across.wait_recv()
        hand.start()

    def end():
        across.wait_send()
        pair.wait()
        hand.wait()
        own.wait()

    return begin, forward, end


def spread_parts(x, out, here, send, recv):
    c, e, z, xh, k = spot()
    at = lambda z, xh, k: z * 4 + xh * 2 + k
    forth = [lax.rem(z + i, 4) for i in range(1, 4)]
    back = [lax.rem(z + 4 - i, 4) for i in range(1, 4)]
    side, twin = (at(z, 1 - xh, k), e), (at(z, xh, 1 - k), e)
    mine, theirs = at(z, xh, k), at(z, 1 - xh, k)
    held = [mine, theirs] + [at(p, xh, k) for p in back] + [at(p, 1 - xh, k) for p in back]
    across = push(x, out.at[mine], send.at[0], recv.at[0], side)
    first = [
        push(x, out.at[mine], send.at[1 + i], recv.at[1 + i], (at(p, xh, k), e))
        for i, p in enumerate(forth)
    ]
    second = [
        push(out.at[theirs], out.at[theirs], send.at[4 + i], recv.at[4 + i], (at(p, xh, k), e))
        for i, p in enumerate(forth)
    ]
    pair = [
        push(x if n == 0 else out.at[b], out.at[b], send.at[7 + n], recv.at[7 + n], twin)
        for n, b in enumerate(held)
    ]
    own = pltpu.make_async_copy(x, out.at[mine], here)

    def begin():
        for copy in [across, *first, pair[0], own]:
            copy.start()

    def middle():
        across.wait_recv()
        for copy in [*second, pair[1]]:
            copy.start()

    def late():
        for copy, hand in zip(first, pair[2:5]):
            copy.wait_recv()
            hand.start()

    def end():
        for copy, hand in zip(second, pair[5:]):
            copy.wait_recv()
            hand.start()
        for copy in pair:
            copy.wait()
        for copy in [across, *first, *second]:
            copy.wait_send()
        own.wait()

    return begin, middle, late, end


def cross_peers():
    c, e, z, xh, k = spot()
    at = lambda z, xh, k: (z * 4 + xh * 2 + k, e)
    return [at(z, 1 - xh, k), at(z, xh, 1 - k)] + [at(lax.rem(z + i, 4), xh, k) for i in (1, 2, 3)]


def open_kernel(packed, x, eight, mine, x_all, here, send, recv, x_send, x_recv):
    c, e, z, xh, k = spot()
    exps = [lax.rem(e + i, EXP) for i in range(1, EXP)]
    peers = [lax.rem(c + i, CTX) for i in range(1, CTX)]
    greet([(c, p) for p in exps] + [(p, e) for p in peers])
    x_begin, x_middle, x_late, x_end = spread_parts(x, x_all, here.at[0], x_send, x_recv)
    rows = [
        push(packed, eight.at[e], send.at[i], recv.at[i], (c, p)) for i, p in enumerate(exps)
    ]
    own_rows = pltpu.make_async_copy(packed, eight.at[e], here.at[1])
    for copy in rows:
        copy.start()
    own_rows.start()
    x_begin()
    x_middle()
    for copy in rows:
        copy.wait_recv()
    own_rows.wait()
    heads = [
        push(eight.at[:, head_of(p)], mine.at[c], send.at[6 + i], recv.at[6 + i], (p, e))
        for i, p in enumerate(peers, 1)
    ]
    own_head = pltpu.make_async_copy(eight.at[:, head_of(c)], mine.at[c], here.at[2])
    for p, copy in zip(peers, heads):
        pl.when(owns(p))(copy.start)
    pl.when(owns(c))(own_head.start)
    x_late()
    for p, copy in zip(peers, heads):
        pl.when(owns(p))(copy.wait_send)
        pl.when(owns(c))(copy.wait_recv)
    pl.when(owns(c))(own_head.wait)
    x_end()
    for copy in rows:
        copy.wait_send()


def opening(packed, x, ident):
    shapes = ((EXP, *packed.shape), (CTX, EXP, *packed.shape[1:]), (CTX, *x.shape))
    sems = pltpu.SemaphoreType.DMA
    return pl.pallas_call(
        open_kernel,
        out_shape=[jax.ShapeDtypeStruct(s, low) for s in shapes],
        in_specs=[ANY, ANY],
        out_specs=[ANY] * 3,
        scratch_shapes=[sems((3,)), sems((22,)), sems((22,)), sems((15,)), sems((15,))],
        compiler_params=pltpu.CompilerParams(
            collective_id=ident, has_side_effects=True, vmem_limit_bytes=2 << 20
        ),
    )(packed, x)


def lists_kernel(x, w, x_all, w_all, here, send, recv, w_send, w_recv):
    c, e, z, xh, k = spot()
    greet(cross_peers())
    size, me, device = group("z")
    copies = []
    for i in range(1, size):
        to = device(lax.rem(me + i, size))
        copies.append(push(x, x_all.at[me], send.at[i - 1], recv.at[i - 1], to))
    w_begin, w_forward, w_end = quad_parts(w, w_all, here.at[0], w_send, w_recv)
    own = pltpu.make_async_copy(x, x_all.at[me], here.at[1])
    for copy in copies:
        copy.start()
    w_begin()
    own.start()
    w_forward()
    for copy in copies:
        copy.wait()
    own.wait()
    w_end()


def gather_lists(x, w, ident):
    sems = pltpu.SemaphoreType.DMA
    shapes = ((ZED, *x.shape), (2, 4, *w.shape[1:]))
    return pl.pallas_call(
        lists_kernel,
        out_shape=[jax.ShapeDtypeStruct(s, low) for s in shapes],
        in_specs=[pl.BlockSpec(memory_space=pltpu.VMEM)] * 2,
        out_specs=[ANY] * 2,
        scratch_shapes=[sems((2,))] + [sems((3,))] * 4,
        compiler_params=pltpu.CompilerParams(
            collective_id=ident, has_side_effects=True, vmem_limit_bytes=4 << 20
        ),
    )(x, w)


def return_kernel(x, g, x_out, g_own, g_out, held, total, here, send, recv, g_send, g_recv):
    c, e, z, xh, k = spot()
    greet(cross_peers())
    size, me, device = group("z")
    copies = []
    for i in range(1, size):
        to = lax.rem(me + i, size)
        copies.append(push(x.at[to], x_out.at[i - 1], send.at[i - 1], recv.at[i - 1], device(to)))
    twin, side = group("core")[2](1 - k), group("x")[2](1 - xh)
    across = push(g.at[:, :, 1 - k], held, g_send.at[0], g_recv.at[0], twin)
    across.start()
    for copy in copies:
        copy.start()
    across.wait()

    def add(n, carry):
        a, b, rows = n // 8, n // 4 % 2, pl.ds(pl.multiple_of(n % 4 * 48, 16), 48)
        both = g[a, b, k, rows, :].astype(wide) + held[a, b, rows, :].astype(wide)
        total[a, b, rows, :] = both.astype(low)
        return carry

    lax.fori_loop(0, 16, add, 0)
    other = push(total.at[:, 1 - xh], g_out, g_send.at[1], g_recv.at[1], side)
    other.start()
    own = pltpu.make_async_copy(total.at[:, xh], g_own, here)
    own.start()
    own.wait()
    for copy in copies:
        copy.wait()
    other.wait()


def return_lists(x, g, ident):
    sems = pltpu.SemaphoreType.DMA
    half = (2, *g.shape[3:])
    return pl.pallas_call(
        return_kernel,
        out_shape=[
            jax.ShapeDtypeStruct(s, low) for s in ((ZED - 1, *x.shape[1:]), half, half)
        ],
        in_specs=[ANY, pl.BlockSpec(memory_space=pltpu.VMEM)],
        out_specs=[ANY] * 3,
        scratch_shapes=[
            pltpu.VMEM((2, 2, *g.shape[3:]), low),
            pltpu.VMEM((2, 2, *g.shape[3:]), low),
            sems,
            sems((3,)),
            sems((3,)),
            sems((2,)),
            sems((2,)),
        ],
        compiler_params=pltpu.CompilerParams(
            collective_id=ident, has_side_effects=True, vmem_limit_bytes=7 << 20
        ),
    )(x, g)


def to_heads(x, ident):
    return swaps(ident, (x, "to_heads", None, True))[0]


def from_heads(x, ident):
    return swaps(ident, (x, "from_heads", None, True))[0]


def near_buckets(shape, before):
    offset = (
        lax.broadcasted_iota(jnp.int32, shape, 0)
        - before
        - lax.broadcasted_iota(jnp.int32, shape, 1)
    )
    distance = jnp.abs(offset)
    far = jnp.full(shape, 8, jnp.int32)
    for edge in bucket_edges:
        far = far + (distance >= edge).astype(jnp.int32)
    return jnp.where(distance < 8, distance, far) + jnp.where(offset > 0, BUCKETS // 2, 0)


def tile_rows(chunk, block):
    tile = jnp.clip(chunk - 2 * block + 2, 0, 5)
    return pl.ds(pl.multiple_of(tile * CHUNK, CHUNK), CHUNK)


def chunk_rows(chunk):
    return pl.ds(pl.multiple_of(chunk * CHUNK, CHUNK), CHUNK)


def forward_kernel(
    qkv_ref, table_ref, x_ref, w_ref, p_ref, o_ref, low_ref, inv_ref, x_all, w_all,
    keys, bias, scores, here, x_send, x_recv, w_send, w_recv,
):
    block = pl.program_id(0)
    x_begin, x_middle, x_late, x_end = spread_parts(x_ref, x_all, here.at[0], x_send, x_recv)
    w_begin, w_forward, w_end = quad_parts(w_ref, w_all, here.at[1], w_send, w_recv)

    @pl.when(block == 0)
    def _():
        greet(cross_peers())
        x_begin()
        w_begin()

    @pl.when(block == 2)
    def _():
        x_middle()

    @pl.when(block == 5)
    def _():
        x_late()

    @pl.when(block == 0)
    def _():
        keys[...] = qkv_ref[1].T
        ids = near_buckets(bias.shape, 2 * CHUNK)
        tiles = jnp.zeros(ids.shape, wide)
        for b in range(BUCKETS):
            tiles = jnp.where(ids == b, table_ref[b : b + 1, 0:1], tiles)
        bias[...] = tiles

    here = pl.ds(pl.multiple_of(block * QUERIES, QUERIES), QUERIES)
    queries = qkv_ref[0, :, here]

    def score(chunk, top):
        rows = chunk_rows(chunk)
        part = jnp.dot(keys[rows, :], queries, preferred_element_type=wide)
        part = part + bias[tile_rows(chunk, block), :]
        scores[rows, :] = part
        return jnp.maximum(top, jnp.max(part.reshape(CHUNK // 8, 8, QUERIES), axis=0))

    top = lax.fori_loop(
        0, LEN // CHUNK, score, jnp.full((8, QUERIES), -1e30, wide), unroll=4
    )
    top = jnp.max(top, axis=0, keepdims=True)

    def weigh(chunk, total):
        rows = chunk_rows(chunk)
        part = jnp.exp(scores[rows, :] - top)
        p_ref[rows, :] = part.astype(low)
        return total + jnp.sum(part.reshape(CHUNK // 8, 8, QUERIES), axis=0)

    total = lax.fori_loop(0, LEN // CHUNK, weigh, jnp.zeros((8, QUERIES), wide), unroll=4)
    inverse = 1.0 / jnp.sum(total, axis=0, keepdims=True)
    out = jnp.dot(qkv_ref[2], p_ref[...], preferred_element_type=wide) * inverse
    o_ref[...] = out
    low_ref[0] = out.astype(low)
    inv_ref[...] = inverse


    @pl.when(block == LEN // QUERIES - 1)
    def _():
        w_forward()
        x_end()
        w_end()


def attend(qkv, table, x, w, ident):
    whole = lambda *shape: pl.BlockSpec(shape, lambda i: (0,) * len(shape))
    return pl.pallas_call(
        forward_kernel,
        grid=(LEN // QUERIES,),
        out_shape=(
            pltpu.HBM((LEN, LEN), low),
            jax.ShapeDtypeStruct((HEAD_DIM, LEN), wide),
            jax.ShapeDtypeStruct((1, HEAD_DIM, LEN), low),
            jax.ShapeDtypeStruct((1, LEN), wide),
            jax.ShapeDtypeStruct((CTX, *x.shape), low),
            jax.ShapeDtypeStruct((2, 4, *w.shape[1:]), low),
        ),
        in_specs=[whole(3, HEAD_DIM, LEN), whole(BUCKETS, 128), ANY, ANY],
        out_specs=(
            pl.BlockSpec((LEN, QUERIES), lambda i: (0, i)),
            pl.BlockSpec((HEAD_DIM, QUERIES), lambda i: (0, i)),
            pl.BlockSpec((1, HEAD_DIM, QUERIES), lambda i: (0, 0, i)),
            pl.BlockSpec((1, QUERIES), lambda i: (0, i)),
            ANY,
            ANY,
        ),
        scratch_shapes=[
            pltpu.VMEM((LEN, HEAD_DIM), low),
            pltpu.VMEM((6 * CHUNK, QUERIES), wide),
            pltpu.VMEM((LEN, QUERIES), wide),
            pltpu.SemaphoreType.DMA((2,)),
            pltpu.SemaphoreType.DMA((15,)),
            pltpu.SemaphoreType.DMA((15,)),
            pltpu.SemaphoreType.DMA((3,)),
            pltpu.SemaphoreType.DMA((3,)),
        ],
        compiler_params=pltpu.CompilerParams(
            collective_id=ident, has_side_effects=True, vmem_limit_bytes=11 << 20
        ),
    )(qkv, table, x, w)


def backward_kernel(
    qkv_ref, p_ref, o_ref, inv_ref, do_ref, x_ref, g_ref, l_ref,
    grad_ref, sums_ref, x_all, g_out, l_out,
    values, dk, dv, tiles, slopes, here, x_send, x_recv, send, recv,
):
    block = pl.program_id(0)
    x_begin, x_middle, x_late, x_end = spread_parts(x_ref, x_all, here, x_send, x_recv)
    size, me, device = group("x")
    across = push(g_ref.at[:, 1 - me], g_out, send.at[0], recv.at[0], device(1 - me))
    size, z, device_z = group("z")
    around = []
    for i in range(1, size):
        to = lax.rem(z + i, size)
        around.append(
            push(l_ref.at[to], l_out.at[i - 1], send.at[i], recv.at[i], device_z(to))
        )

    @pl.when(block == 0)
    def _():
        greet(cross_peers())
        x_begin()
        for copy in around:
            copy.start()

    @pl.when(block == 1)
    def _():
        x_middle()
        across.start()

    @pl.when(block == 5)
    def _():
        x_late()

    @pl.when(block == 0)
    def _():
        values[...] = qkv_ref[2].T
        dk[...] = jnp.zeros(dk.shape, wide)
        dv[...] = jnp.zeros(dv.shape, wide)
        tiles[...] = jnp.zeros(tiles.shape, wide)

    here = pl.ds(pl.multiple_of(block * QUERIES, QUERIES), QUERIES)
    scaled = (do_ref[0].astype(wide) * inv_ref[...]).astype(low)
    delta = jnp.sum(scaled.astype(wide) * o_ref[...], axis=0, keepdims=True)

    def slope(chunk, carry):
        rows = chunk_rows(chunk)
        part = jnp.dot(values[rows, :], scaled, preferred_element_type=wide)
        part = p_ref[rows, :].astype(wide) * (part - delta)
        slopes[rows, :] = part.astype(low)
        near = tile_rows(chunk, block)
        tiles[near, :] = tiles[near, :] + part
        return carry

    lax.fori_loop(0, LEN // CHUNK, slope, 0, unroll=4)
    grad_ref[0, :, here] = jnp.dot(
        qkv_ref[1], slopes[...], preferred_element_type=wide
    ).astype(low)
    queries = qkv_ref[0, :, here].T
    turned = scaled.T

    def gather(chunk, carry):
        rows = pl.ds(pl.multiple_of(chunk * 512, 512), 512)
        dk[rows, :] = dk[rows, :] + jnp.dot(
            slopes[rows, :], queries, preferred_element_type=wide
        )
        dv[rows, :] = dv[rows, :] + jnp.dot(p_ref[rows, :], turned, preferred_element_type=wide)
        return carry

    lax.fori_loop(0, LEN // 512, gather, 0)

    @pl.when(block == LEN // QUERIES - 1)
    def _():
        grad_ref[1] = dk[...].T.astype(low)
        grad_ref[2] = dv[...].T.astype(low)
        sums_ref[...] = tiles[...]
        for copy in around:
            copy.wait()
        x_end()
        across.wait()


def attend_back(qkv, probs, out, inverse, grad_out, x, grads, late, ident):
    whole = lambda *shape: pl.BlockSpec(shape, lambda i: (0,) * len(shape))
    return pl.pallas_call(
        backward_kernel,
        grid=(LEN // QUERIES,),
        out_shape=(
            jax.ShapeDtypeStruct((3, HEAD_DIM, LEN), low),
            jax.ShapeDtypeStruct((6 * CHUNK, QUERIES), wide),
            jax.ShapeDtypeStruct((CTX, *x.shape), low),
            jax.ShapeDtypeStruct(grads.shape[:1] + grads.shape[2:], low),
            jax.ShapeDtypeStruct((ZED - 1, *late.shape[1:]), low),
        ),
        in_specs=[
            whole(3, HEAD_DIM, LEN),
            pl.BlockSpec((LEN, QUERIES), lambda i: (0, i)),
            pl.BlockSpec((HEAD_DIM, QUERIES), lambda i: (0, i)),
            pl.BlockSpec((1, QUERIES), lambda i: (0, i)),
            pl.BlockSpec((1, HEAD_DIM, QUERIES), lambda i: (0, 0, i)),
            ANY,
            ANY,
            ANY,
        ],
        out_specs=(whole(3, HEAD_DIM, LEN), whole(6 * CHUNK, QUERIES), ANY, ANY, ANY),
        scratch_shapes=[
            pltpu.VMEM((LEN, HEAD_DIM), low),
            pltpu.VMEM((LEN, HEAD_DIM), wide),
            pltpu.VMEM((LEN, HEAD_DIM), wide),
            pltpu.VMEM((6 * CHUNK, QUERIES), wide),
            pltpu.VMEM((LEN, QUERIES), low),
            pltpu.SemaphoreType.DMA,
            pltpu.SemaphoreType.DMA((15,)),
            pltpu.SemaphoreType.DMA((15,)),
            pltpu.SemaphoreType.DMA((4,)),
            pltpu.SemaphoreType.DMA((4,)),
        ],
        compiler_params=pltpu.CompilerParams(
            collective_id=ident, has_side_effects=True, vmem_limit_bytes=14 << 20
        ),
    )(
        qkv,
        pltpu.with_memory_space_constraint(probs, pltpu.HBM),
        out, inverse, grad_out, x, grads, late
    )


def finish_kernel(
    rows_ref, late_ref, others_ref, wq_ref, wkv_ref, gain_ref,
    gq_ref, gkv_ref, gout_ref, router_ref, gain_one_ref, gain_two_ref, table_ref,
):
    c, e, z, xh, k = spot()
    late = late_ref[e] + jnp.sum(others_ref[...], axis=0)
    gout_ref[...] = late[:6, :D]
    router_ref[...] = late[:6, D + 67 : D + 83]
    gain_two_ref[...] = late[:6, D + 65 : D + 66]
    parts = [
        jnp.concatenate(
            [rows_ref[h, :, n * HEAD_DIM : (n + 1) * HEAD_DIM] for h in range(HEADS)], axis=1
        )[:6]
        for n in range(3)
    ]
    gq_ref[...] = parts[0]
    gkv_ref[:, :D] = parts[1]
    gkv_ref[:, D:] = parts[2]
    along = jnp.sum(wq_ref[...].astype(wide) * parts[0], axis=1, keepdims=True)
    along = along + jnp.sum(wkv_ref[:, :D].astype(wide) * parts[1], axis=1, keepdims=True)
    along = along + jnp.sum(wkv_ref[:, D:].astype(wide) * parts[2], axis=1, keepdims=True)
    gain_one_ref[...] = along / gain_ref[...]
    device = c * EXP + e
    buckets = rows_ref[pl.ds(device % 4 * 3, 3), 6, :]
    chosen = lax.broadcasted_iota(jnp.int32, buckets.shape, 1) == device // 4
    table_ref[...] = jnp.sum(jnp.where(chosen, buckets, 0.0), axis=1, keepdims=True)


def finish(by_head, late, others, wq, wkv, gain):
    shapes = [(6, D), (6, 2 * D), (6, D), (6, 16), (6, 1), (6, 1), (3, 1)]
    return pl.pallas_call(
        finish_kernel,
        out_shape=[jax.ShapeDtypeStruct(s, wide) for s in shapes],
        compiler_params=pltpu.CompilerParams(vmem_limit_bytes=8 << 20),
    )(by_head, late, others, wq, wkv, gain.astype(wide)[:, None])


def plain(kernel, shapes, megabytes, *args):
    return pl.pallas_call(
        kernel,
        out_shape=[jax.ShapeDtypeStruct(shape, kind) for shape, kind in shapes],
        compiler_params=pltpu.CompilerParams(vmem_limit_bytes=megabytes << 20),
    )(*args)


def iota(shape, axis):
    return lax.broadcasted_iota(jnp.int32, shape, axis)


def pack_kernel(wq_ref, wkv_ref, wo_ref, extra_ref, out_ref):
    empty = jnp.zeros((4, 128), wide)
    extra = extra_ref[...].astype(wide)
    wq, wkv, wo = (ref[...].astype(wide) for ref in (wq_ref, wkv_ref, wo_ref))
    for h in range(HEADS):
        at = h * HEAD_DIM
        query, key = wq[:, at : at + HEAD_DIM], wkv[:, at : at + HEAD_DIM]
        value = wkv[:, D + at : D + at + HEAD_DIM]
        upper = jnp.concatenate([query, key], axis=1)
        lower = jnp.concatenate([value, extra], axis=1)
        out_ref[h] = jnp.concatenate([upper, lower, empty], axis=0).astype(low)
    for n in range(3):
        upper, lower = (wo[:, (2 * n + i) * 128 : (2 * n + i + 1) * 128] for i in range(2))
        out_ref[HEADS + n] = jnp.concatenate([upper, lower, empty], axis=0).astype(low)


def six_rows(rows, first):
    shape = (rows // 16 * 6, rows)
    column = iota((1, rows), 1)
    inner = column % 16 - first
    place = jnp.where((inner >= 0) & (inner < 6), column // 16 * 6 + inner, -1)
    return (iota(shape, 0) == place).astype(low)


def project_kernel(mine_ref, x_ref, eight_ref, qkv_ref, h_ref, table_ref, first_ref, second_ref):
    c, e, z, xh, k = spot()
    mine = mine_ref[...]
    upper = jnp.dot(six_rows(2048, 0), mine, preferred_element_type=wide)
    lower = jnp.dot(six_rows(2048, 6), mine, preferred_element_type=wide)
    lower_turned = lower.T
    gain = lower_turned[64:65, :]
    weight_qk, weight_v = upper.T.astype(low), lower_turned[:64].astype(low)
    for n in range(4):
        rows = slice(n * 512, (n + 1) * 512)
        x = x_ref[rows, :].astype(wide)
        scale = lax.rsqrt(jnp.mean(x * x, axis=1, keepdims=True) + epsilon)
        h = (x * scale * gain).astype(low)
        h_ref[rows, :] = h
        both = dot(weight_qk, h, (1, 1)).astype(low)
        qkv_ref[0, :, rows] = both[:64]
        qkv_ref[1, :, rows] = both[64:]
        qkv_ref[2, :, rows] = dot(weight_v, h, (1, 1)).astype(low)
    head = head_of(c)
    column = jnp.broadcast_to(lower[:, 66:67], (D, 128))
    row = iota((BUCKETS, D), 1)
    wanted = (row // 24 == iota((BUCKETS, D), 0)) & (row % 24 == head // 3 * 6 + head % 3)
    table_ref[...] = jnp.dot(wanted.astype(low), column.astype(low), preferred_element_type=wide)
    pick = [six_rows(128, 0), six_rows(128, 6)]
    part = lambda n, i: jnp.dot(
        pick[i], eight_ref[:, n].reshape(128, 128), preferred_element_type=wide
    )
    first_ref[:, :128] = part(0, 1).astype(low)
    for n in range(3):
        for i in range(2):
            at = 128 + (2 * n + i) * 128
            first_ref[:, at : at + 128] = part(HEADS + n, i).astype(low)
    for pair in range(HEADS // 2):
        pieces = []
        for h in (2 * pair, 2 * pair + 1):
            pieces += [part(h, 0), part(h, 1)[:, :64]]
        pieces = jnp.concatenate(pieces, axis=1).astype(low)
        if pair < 2:
            first_ref[:, 896 + pair * 384 : 896 + (pair + 1) * 384] = pieces
        else:
            second_ref[:, (pair - 2) * 384 : (pair - 1) * 384] = pieces


def route_kernel(
    att_ref, x_ref, cot_ref, route_ref, full_ref,
    residual_ref, h_ref, probs_ref, dispatch_ref, out_ref,
):
    wo, small = full_ref[:, 128:896], full_ref[:, :128]
    gain = small.astype(wide).T[65:66, :]
    attended = att_ref[...].astype(wide).T.astype(low)
    residual = x_ref[...].astype(wide) + jnp.dot(attended, wo, preferred_element_type=wide)
    residual_ref[...] = residual
    scale = lax.rsqrt(jnp.mean(residual * residual, axis=1, keepdims=True) + epsilon)
    h_two = (residual * scale * gain).astype(low)
    h_ref[...] = h_two
    logits = jnp.dot(h_two, small, preferred_element_type=wide)[:, 67:83]
    logits = jnp.exp(logits - jnp.max(logits, axis=1, keepdims=True))
    probs = logits / jnp.sum(logits, axis=1, keepdims=True)
    probs_ref[...] = probs
    route = route_ref[...]
    choose = (route == iota((TOK, 16), 1)).astype(wide)
    before = (iota((TOK, TOK), 1) < iota((TOK, TOK), 0)).astype(low)
    earlier = jnp.dot(before, choose.astype(low), preferred_element_type=wide)
    slot = jnp.sum(earlier * choose, axis=1, keepdims=True).astype(jnp.int32)
    target = route // 2 * SLOTS + route % 2 * CAP + slot
    places = iota((TOK, EXP * SLOTS), 1)
    dispatch = jnp.concatenate(
        [(places == target).astype(wide), (places == target + 2 * CAP).astype(wide)], axis=0
    )
    dispatch_ref[...] = dispatch.astype(low)
    gate = jnp.sum(probs * choose, axis=1, keepdims=True)
    grad_y = (gate * cot_ref[...].astype(wide)).astype(low)
    turned = dispatch.T.astype(low)
    out = jnp.dot(turned[:, :TOK], h_two, preferred_element_type=wide)
    out = out + jnp.dot(turned[:, TOK:], grad_y, preferred_element_type=wide)
    out_ref[...] = out.astype(low)


def combine_kernel(
    back_ref, dispatch_ref, residual_ref, cot_ref, probs_ref, route_ref, h_ref, full_ref, att_ref,
    mixed_ref, grad_ref, grad_att_ref, late_ref,
):
    wo, small = full_ref[:, 128:896], full_ref[:, :128]
    gain = small.astype(wide).T[65:66, :]
    returned = jnp.dot(dispatch_ref[...], back_ref[...], preferred_element_type=wide)
    tokens, grad_h = returned[:TOK], returned[TOK:]
    residual, probs = residual_ref[...], probs_ref[...]
    choose = (route_ref[...] == iota((TOK, 16), 1)).astype(wide)
    gate = jnp.sum(probs * choose, axis=1, keepdims=True)
    mixed_ref[...] = (residual + gate * tokens).astype(low)
    grad = cot_ref[...].astype(wide)
    grad_choice = choose * jnp.sum(grad * tokens, axis=1, keepdims=True)
    grad_logits = probs * (grad_choice - jnp.sum(probs * grad_choice, axis=1, keepdims=True))
    spread = (iota((16, 128), 0) + 67 == iota((16, 128), 1)).astype(low)
    upper = grad_logits.astype(low)
    lower = (grad_logits - upper.astype(wide)).astype(low)
    upper = jnp.dot(upper, spread, preferred_element_type=wide).astype(low)
    lower = jnp.dot(lower, spread, preferred_element_type=wide).astype(low)
    grad_h = grad_h + dot(upper, small, (1, 1)) + dot(lower, small, (1, 1))
    scale = lax.rsqrt(jnp.mean(residual * residual, axis=1, keepdims=True) + epsilon)
    along = grad_h * gain
    mean = jnp.mean(along * residual, axis=1, keepdims=True)
    grad = grad + scale * along - (scale * scale * scale * mean) * residual
    grad_ref[...] = grad
    branch = grad.astype(low)
    grad_att_ref[...] = dot(wo, branch, (1, 1)).astype(low)
    late_ref[:, :D] = jnp.dot(att_ref[...], branch, preferred_element_type=wide).astype(low)
    turned = h_ref[...].astype(wide).T.astype(low)
    extra = jnp.dot(turned, upper, preferred_element_type=wide)
    extra = extra + jnp.dot(turned, lower, preferred_element_type=wide)
    gains = (grad_h * residual * scale).T
    gains = jnp.sum(gains, axis=1, keepdims=True)
    late_ref[:, D:] = jnp.where(iota((D, 128), 1) == 65, gains, extra).astype(low)


def rms_scale(values_in, gain_vec):
    return (
        values_in
        * lax.rsqrt(jnp.mean(values_in * values_in, axis=-1, keepdims=True) + epsilon)
        * gain_vec
    )


def dot(a, b, dims=(1, 0)):
    return lax.dot_general(
        a, b, (((dims[0],), (dims[1],)), ((), ())), preferred_element_type=wide
    )


def shards(
    tokens,
    cotangent,
    routes,
    query_weight,
    kv_weight,
    out_weight,
    norm_gain_one,
    norm_gain_two,
    router_weight,
    bias_table,
    expert_in,
    expert_out,
):
    x_rows = tokens[0].astype(wide)

    extra = jnp.concatenate(
        [
            norm_gain_one[:, None],
            norm_gain_two[:, None],
            jnp.pad(bias_table, (0, 3))[:, None],
            router_weight,
            jnp.zeros((6, 45), low),
        ],
        axis=1,
    )
    packed = plain(
        pack_kernel, [((15, 16, 128), low)], 4, query_weight, kv_weight, out_weight, extra
    )[0]
    eight, mine, x_all = opening(packed, tokens[0], 1)
    head_qkv, h_all, head_table, block, block_qkv = plain(
        project_kernel,
        [
            ((3, HEAD_DIM, LEN), low),
            ((LEN, D), low),
            ((BUCKETS, 128), wide),
            ((48, 128 + 2 * D), low),
            ((48, 2 * D), low),
        ],
        28,
        mine.reshape(2048, 128),
        x_all.reshape(LEN, D),
        eight,
    )
    probs, attended, attended_head, inverse, full, experts_out = attend(
        head_qkv, head_table, block, expert_out, 18
    )
    full = full.reshape(D, 2 * D + 128)
    full_out = full[:, :896]
    gain_one = full[:, 64].astype(wide)
    attended_low = from_heads(attended_head, 5).reshape(D, TOK)
    routed = (TOK, D)
    residual, h_two, route_probs, dispatch, outgoing = plain(
        route_kernel,
        [
            (routed, wide),
            (routed, low),
            ((TOK, 16), wide),
            ((2 * TOK, EXP * SLOTS), low),
            ((EXP * SLOTS, D), low),
        ],
        16,
        attended_low,
        tokens[0],
        cotangent[0],
        routes[0],
        full_out,
    )
    received = swap(outgoing.reshape(EXP, SLOTS, D), "exp", 6, 0).reshape(EXP * SLOTS, D)

    row = jnp.arange(4 * 80, dtype=jnp.int32)
    source = row % 80 // CAP * SLOTS + row // 80 * CAP + row % CAP
    compact = (source[:, None] == jnp.arange(EXP * SLOTS, dtype=jnp.int32)[None, :]).astype(low)
    lists, experts_in = gather_lists(
        dot(compact, received).astype(low), jnp.swapaxes(expert_in, 1, 2), 7
    )
    lists = lists.reshape(ZED, 4, 80, D)
    experts_here = experts_in.reshape(2, D, D), experts_out.reshape(2, D, D)
    partial, grads_in, grads_out = [], [], []
    for n in range(2):
        rows = lists[:, n].reshape(ZED * 80, D)
        grads = lists[:, 2 + n].reshape(ZED * 80, D)
        weight_in, weight_out = experts_here[0][n], experts_here[1][n]
        pre_act = dot(rows, weight_in, (1, 1))
        hidden_wide, gelu_back = jax.vjp(jax.nn.gelu, pre_act)
        hidden = hidden_wide.astype(low)
        grad_hidden = dot(grads, weight_out, (1, 1))
        grad_pre = gelu_back(grad_hidden)[0].astype(low)
        partial.append(dot(hidden, weight_out).astype(low).reshape(ZED, 80, D))
        partial.append(dot(grad_pre, weight_in).astype(low).reshape(ZED, 80, D))
        grads_in.append(dot(grad_pre, rows, (0, 0)).astype(low))
        grads_out.append(dot(hidden, grads, (0, 0)).astype(low))
    partial = jnp.stack([partial[0], partial[2], partial[1], partial[3]], axis=1)
    partial = partial.reshape(ZED, 320, D)
    grads_out = jnp.stack(grads_out).reshape(2, 2, 2, 192, D)
    others, grads_own, grads_other = return_lists(partial, grads_out, 8)
    grad_expert_out = grads_own.astype(wide) + grads_other.astype(wide)
    summed = add_up(partial, "z", 0, others).astype(low)
    spread = dot(compact, summed, (0, 0)).astype(low).reshape(EXP, SLOTS, D)
    expert_grads = jnp.stack(grads_in).reshape(2, 2, 2, 192, D)
    back, others = swaps(9, (spread, "exp", 0, True), (expert_grads, "core", 2, False))
    expert_grads = add_up(expert_grads, "core", 2, others).astype(low)
    mixed_rows, grad_residual, grad_attended, late = plain(
        combine_kernel,
        [(routed, low), (routed, wide), ((D, TOK), low), ((D, 896), low)],
        20,
        back.reshape(EXP * SLOTS, D),
        dispatch,
        residual,
        cotangent[0],
        route_probs,
        routes[0],
        h_two,
        full_out,
        attended_low,
    )
    late = late.reshape(8, 2, 48, 896)
    head_grad, others = swaps(
        10,
        (grad_attended.reshape(1, HEADS, HEAD_DIM, TOK), "to_heads", None, True),
        (late, "core", 1, False),
    )
    late = add_up(late, "core", 1, others).astype(low).reshape(ZED, 2, 48, 896)
    head_grads, tile_sums, qkv_full, others, late_others = attend_back(
        head_qkv, probs, attended, inverse, head_grad, block_qkv, expert_grads, late, 19
    )
    qkv_full = qkv_full.reshape(D, 2 * D)
    late = add_up(late, "z", 0, late_others).astype(low)
    grad_expert_in = jnp.swapaxes(add_up(expert_grads, "x", 1, others[None]), 1, 2)

    tile = lambda n, half: tile_sums[n * CHUNK : (n + 1) * CHUNK, half * TOK : (half + 1) * TOK]
    near = jnp.concatenate([tile(n, 0) + tile(n + 1, 1) for n in (1, 2, 3)], axis=0)
    bucket_range = jnp.arange(BUCKETS, dtype=jnp.int32)
    bucket_sums = jnp.sum(
        jnp.where(
            near_buckets(near.shape, CHUNK)[None] == bucket_range[:, None, None], near[None], 0.0
        ),
        axis=(1, 2),
    )
    bucket_sums = bucket_sums + jnp.where(
        bucket_range == BUCKETS // 2 - 1, jnp.sum(tile(0, 0) + tile(0, 1) + tile(1, 1)), 0.0
    )
    bucket_sums = bucket_sums + jnp.where(
        bucket_range == BUCKETS - 1, jnp.sum(tile(4, 0) + tile(5, 0) + tile(5, 1)), 0.0
    )
    sixth = jnp.arange(EXP * TOK, dtype=jnp.int32) % 8 == 6
    place = jnp.arange(D, dtype=jnp.int32)
    place = place // 6 % EXP * TOK + place // 48 * 8 + place % 6
    by_owner = (jnp.arange(EXP * TOK, dtype=jnp.int32)[:, None] == place[None, :]).astype(low)
    head_weights = dot(h_all, head_grads.reshape(192, LEN), (0, 1)).astype(low)
    head_weights = dot(by_owner, head_weights)
    head_weights = head_weights + jnp.where(
        sixth[:, None], jnp.pad(bucket_sums, (0, 192 - BUCKETS))[None, :], 0.0
    )
    head_weights = head_weights.astype(low).reshape(EXP, TOK, 192)
    grad_qkv, others, late_others = swaps(
        11,
        (head_grads, "from_heads", None, True),
        (head_weights, "exp", 0, False),
        (late, "x", 0, False),
    )
    grad_qkv = grad_qkv.reshape(3 * D, TOK)
    head_weights = add_up(head_weights, "exp", 0, others).reshape(CTX, 8, 192)
    late = add_up(late, "x", 0, late_others).reshape(EXP, 6, 896)
    late = jnp.pad(late, ((0, 0), (0, 2), (0, 0)))
    by_head, others = swaps(
        12, (head_weights, "head_rows", None, True), (late, "exp", 0, False)
    )
    finished = finish(by_head, late, others, query_weight, kv_weight, norm_gain_one)

    grad_h_one = dot(grad_qkv[:D], full[:, 896:], (0, 1))
    grad_h_one = grad_h_one + dot(grad_qkv[D:], qkv_full, (0, 1))
    norm_one_back = jax.vjp(lambda x: rms_scale(x, gain_one), x_rows)[1]
    grad_tokens = grad_residual + norm_one_back(grad_h_one)[0]
    return (
        mixed_rows[None],
        grad_tokens[None],
        *finished[:3],
        finished[4][:, 0],
        finished[5][:, 0],
        finished[3],
        finished[6][:, 0],
        grad_expert_in,
        grad_expert_out,
    )


def solution(mesh):
    rows = P("exp", "ctx", None)
    shared, vector = P(("ctx", "exp"), None), P(("ctx", "exp"))
    expert_in, expert_out = P("exp", None, "ctx"), P("exp", "ctx", None)
    return jax.shard_map(
        shards,
        mesh=mesh,
        in_specs=(rows, rows, rows, shared, shared, shared, vector, vector, shared, vector)
        + (expert_in, expert_out),
        out_specs=(rows, rows, shared, shared, shared, vector, vector, shared, vector)
        + (expert_in, expert_out),
        check_vma=False,
    )
```

time: 384 us -> 284 us (0.74)
  Pallas kernels: 260 us -> 223 us
  local copies, waits for them, and re-layouts: 48.8 us -> 23.6 us
  matrix products: 38.4 us -> 18.7 us
  other arithmetic: 32.6 us -> 16.7 us
    pallas_call x10 -> x6, Pallas kernels: 158 us -> 71.8 us  [swaps(): pl.pallas_call(functools.partial(swaps_kernel, [item[1:] for item in item...]
    pallas_call x2 -> x9, Pallas kernels: 74.3 us -> 123 us  [the longest x1 37.9 us: opening(): pl.pallas_call(open_kernel, out_shape=[jax.ShapeDtypeStruct(s, low) for s...]
    dot_general x24 -> x17, matrix products: 35.7 us -> 18.7 us  [dot(): lax.dot_general(a, b, (((dims[0],), (dims[1],)), ((), ())), preferred_ele...]
    slice x9 -> x5, local copies, waits for them, and re-layouts: 10.6 us -> 1.85 us  [the longest x1 1.51 us: shards(): full_out = full[:, :896]]
    reshape x6 -> x0, local copies, waits for them, and re-layouts: 4.47 us -> none  [the longest x1 1.66 us: shards(): by_head[:, :6].reshape(HEADS, 6, 3, HEAD_DIM)]
    reduce_sum x9 -> x2, other arithmetic: 6.06 us -> 1.62 us  [the longest x1 0.88 us: shards(): jnp.sum(jnp.where(near_buckets(near.shape, CHUNK)[None] == bucket_range[:...]
    convert_element_type x8 -> x4, other arithmetic: 7.35 us -> 3.39 us  [the longest x1 1.9 us: shards(): expert_grads = add_up(expert_grads, 'core', 2, others).astype(low)]
    unnamed x92 -> x118, local copies, waits for them, and re-layouts: 16.7 us -> 16.2 us
where the time goes in v4:
time: 284 us; the launch traced here: 283 us
  Pallas kernels  223 us (79%)
  local copies, waits for them, and re-layouts  23.6 us (8%)
  matrix products  18.7 us (7%)
  other arithmetic  16.7 us (6%)
    pallas_call x6, Pallas kernels, swaps(): pl.pallas_call(functools.partial(swaps_kernel, [item[1:] for item in item...  71.8 us
    pallas_call x1, Pallas kernels, opening(): pl.pallas_call(open_kernel, out_shape=[jax.ShapeDtypeStruct(s, low) for s...  37.9 us
    pallas_call x1, Pallas kernels, attend_back(): pl.pallas_call(backward_kernel, grid=(LEN // QUERIES,), out_shape=(jax.Sh...  28.3 us
    pallas_call x1, Pallas kernels, gather_lists(): pl.pallas_call(lists_kernel, out_shape=[jax.ShapeDtypeStruct(s, low) for...  26.5 us
    pallas_call x1, Pallas kernels, return_lists(): pl.pallas_call(return_kernel, out_shape=[jax.ShapeDtypeStruct(s, low) for...  24.6 us
    pallas_call x1, Pallas kernels, attend(): pl.pallas_call(forward_kernel, grid=(LEN // QUERIES,), out_shape=(pltpu.H...  24.4 us
    dot_general x17, matrix products, dot(): lax.dot_general(a, b, (((dims[0],), (dims[1],)), ((), ())), preferred_ele...  18.7 us
    unnamed x118, local copies, waits for them, and re-layouts  16.2 us

profile of v4, /device:TPU:1, one launch (start us, length us, event | category | flops | bytes accessed | tf_op | source)
XLA Modules:
  0.0 283.3 jit_solution(15937575007177890692)
XLA Ops:
  2.9 0.8 concatenate.8.extra_ref
  6.0 0.9 copy-done.6
  6.9 37.9 %shard_map.204 = (bf16[8,15,16,128]{3,2,1,0:T(8,128)(2,1)S(1)}, bf16[16,8,16,128]{3,2,1,0:T(8,128)(2,1)S(1)}, bf16[16,128,768]{2,1,0:T(8,128)(2,1)S(1)}) custom-call(bf16[15,16,128]{2,1,0:T(8,128)(2,1)S(1)} %shard_map.203.packed, bf16[128,768]{1,0:T(8,128)(2,1)S(1)} %bitcast.129), custom_call_target="tpu_custom_call" | custom-call | tf_op jit(solution)/shard_map/pallas_call | solution.py:308
  44.8 4.7 %shard_map.205 = (bf16[3,64,2048]{2,1,0:T(8,128)(2,1)S(1)}, bf16[2048,768]{1,0:T(8,128)(2,1)S(1)}, f32[32,128]{1,0:T(8,128)S(1)}, bf16[48,1664]{1,0:T(8,128)(2,1)S(1)}, bf16[48,1536]{1,0:T(8,128)(2,1)S(1)}) custom-call(bf16[2048,128]{1,0:T(8,128)(2,1)S(1)} %bitcast.141, bf16[2048,768]{1,0:T(8,128)(2,1)S(1)} %bitcast.118, ...), custom_call_target="tpu_custom_call" | custom-call | tf_op jit(solution)/shard_map/pallas_call | solution.py:712
  49.5 24.4 %shard_map.206 = (bf16[2048,2048]{1,0:T(8,128)(2,1)}, f32[64,2048]{1,0:T(8,128)S(1)}, bf16[1,64,2048]{2,1,0:T(8,128)(2,1)S(1)}, f32[1,2048]{1,0:T(1,128)S(1)}, b...) custom-call(bf16[3,64,2048]{2,1,0:T(8,128)(2,1)S(1)} %get-tuple-element.63.qkv_ref, ...), custom_call_target="tpu_custom_call" | custom-call | tf_op jit(solution)/shard_map/pallas_call | solution.py:512
  74.0 0.9 copy-done
  74.8 1.4 copy-done.4
  76.2 1.5 copy-done.10
  77.7 0.8 copy-done.25
  78.6 8.1 %shard_map.207 = bf16[12,1,64,128]{3,2,1,0:T(8,128)(2,1)S(1)} custom-call(bf16[1,64,2048]{2,1,0:T(8,128)(2,1)S(1)} %get-tuple-element.66.refs_0_), custom_call_target="tpu_custom_call" | custom-call | tf_op jit(solution)/shard_map/pallas_call | solution.py:157
  86.8 1.5 slice.112.full_ref
  88.3 1.6 shard_map.208
  90.0 11.3 %shard_map.209 = bf16[8,48,768]{2,1,0:T(8,128)(2,1)S(1)} custom-call(bf16[8,48,768]{2,1,0:T(8,128)(2,1)S(1)} %bitcast.140), custom_call_target="tpu_custom_call" | custom-call | tf_op jit(solution)/shard_map/pallas_call | solution.py:157
  101.8 26.5 %shard_map.210 = (bf16[4,320,768]{2,1,0:T(8,128)(2,1)S(1)}, bf16[2,4,192,768]{3,2,1,0:T(8,128)(2,1)S(1)}) custom-call(bf16[320,768]{1,0:T(8,128)(2,1)S(1)} %convolution_convert_fusion.5.x, bf16[2,192,768]{2,1,0:T(8,128)(2,1)S(1)} %bitcast.139), custom_call_target="tpu_custom_call" | custom-call | tf_op jit(solution)/shard_map/pallas_call | solution.py:344
  128.6 1.8 copy-done.5
  131.3 1.0 fusion.24
  133.5 1.0 fusion.17
  136.9 0.9 convolution_convert_fusion.2
  137.8 0.9 convolution_convert_fusion.3
  138.9 24.6 %shard_map.211 = (bf16[3,320,768]{2,1,0:T(8,128)(2,1)S(1)}, bf16[2,192,768]{2,1,0:T(8,128)(2,1)S(1)}, bf16[2,192,768]{2,1,0:T(8,128)(2,1)S(1)}) custom-call(bf16[4,320,768]{2,1,0:T(8,128)(2,1)S(1)} %bitcast.116, bf16[2,2,2,192,768]{4,3,2,1,0:T(8,128)(2,1)S(1)} %pad_maximum_fusion.1.g), custom_call_target="tpu_custom_call" | custom-call | tf_op jit(solution)/shard_map/pallas_call | solution.py:391
  163.5 1.3 convert_reduce_fusion
  164.8 1.9 convolution_convert_fusion.4
  166.7 0.8 convolution_convert_fusion
  167.9 0.8 convolution_convert_fusion.1
  169.0 0.8 copy-done.49
  169.8 11.3 %shard_map.212 = (bf16[8,48,768]{2,1,0:T(8,128)(2,1)S(1)}, bf16[1,2,2,192,768]{4,3,2,1,0:T(8,128)(2,1)S(1)}) custom-call(bf16[8,48,768]{2,1,0:T(8,128)(2,1)S(1)} %bitcast.125, bf16[2,2,2,192,768]{4,3,2,1,0:T(8,128)(2,1)S(1)} %pad_maximum_fusion.refs_1_), custom_call_target="tpu_custom_call" | custom-call | tf_op jit(solution)/shard_map/pallas_call | solution.py:157
  181.1 1.0 copy-done.9
  182.2 2.0 shard_map.213
  184.1 1.3 convert_reduce_fusion.3
  185.4 9.4 %shard_map.214 = (bf16[1,64,2048]{2,1,0:T(8,128)(2,1)S(1)}, bf16[1,8,48,896]{3,2,1,0:T(8,128)(2,1)S(1)}) custom-call(bf16[1,12,64,128]{3,2,1,0:T(8,128)(2,1)S(1)} %bitcast.142, bf16[8,2,48,896]{3,2,1,0:T(8,128)(2,1)S(1)} %bitcast.119), custom_call_target="tpu_custom_call" | custom-call | tf_op jit(solution)/shard_map/pallas_call | solution.py:157
  194.9 0.9 copy-done.13
  196.4 1.9 fusion.1.g_ref
  198.5 1.0 copy-done.14
  199.9 28.3 %shard_map.215 = (bf16[3,64,2048]{2,1,0:T(8,128)(2,1)S(1)}, f32[768,256]{1,0:T(8,128)S(1)}, bf16[16,48,1536]{2,1,0:T(8,128)(2,1)S(1)}, bf16[2,192,768]{2,1,0:T(8,128)(2,1)S(1)}, bf16[3,2,48,896]{3,2,1,0:T(8,128)(2,1)S(1)}) custom-call(bf16[3,64,2048]{2,1,0:T(8,128)(2,1)S(1)} %copy-done.1, bf16[2048,2048]{1,0:T(8,128)(2,1)} %get-tuple-element.80.p_ref, ...), custom_call_target="tpu_custom_call" | custom-call | tf_op jit(solution)/shard_map/pallas_call | solution.py:631
  228.3 1.4 copy-done.2
  230.8 0.9 select_reduce_fusion
  231.7 1.3 fusion.82
  233.0 4.3 %fusion.5 = bf16[1024,192]{0,1:T(8,128)(2,1)} fusion(s32[768]{0:T(1024)S(1)} %fusion.62, bf16[192,2048]{1,0:T(8,128)(2,1)S(1)} %bitcast.134, bf16[2048,768]{1,0:T(8,128)(2,1)} %copy-done.47, f32[192]{0:T(256)S(1)} %pad.13, pred[1024]{0:T(1024)(128)(4,1)S(1)} %fusion.65), kind=kOutput, calls=%fused_computation.30 | convolution fusion | flops 907493376 | bytes 4330240 | tf_op jit(solution)/shard_map/dot_general | solution.py:871
  237.3 1.2 copy.61
  238.5 1.2 convert_reduce_fusion.1
  239.7 19.9 %shard_map.216 = (bf16[12,3,64,128]{3,2,1,0:T(8,128)(2,1)S(1)}, bf16[7,128,192]{2,1,0:T(8,128)(2,1)S(1)}, bf16[1,48,896]{2,1,0:T(8,128)(2,1)S(1)}) custom-call(bf16[3,64,2048]{2,1,0:T(8,128)(2,1)S(1)} %get-tuple-element.89.refs_0_, bf16[8,128,192]{2,1,0:T(8,128)(2,1)S(1)} %bitcast.121, bf16[2,48,896]{2,1,0:T(8,128)(2,1)S(1)} %fusion.33.refs_2_), custom_call_target="tpu_custom_call" | custom-call | tf_op jit(solution)/shard_map/pallas_call | solution.py:157
  259.6 0.9 fusion.89
  260.6 2.0 fusion.29
  262.6 0.9 fusion.32
  264.2 1.0 convert_add_fusion.7.refs_0_
  266.0 1.0 add.331
  267.0 11.9 %shard_map.217 = (f32[12,8,192]{2,1,0:T(8,128)S(1)}, f32[7,8,896]{2,1,0:T(8,128)S(1)}) custom-call(f32[16,8,192]{2,1,0:T(8,128)S(1)} %convert_add_fusion.7.refs_0_, f32[8,8,896]{2,1,0:T(8,128)S(1)} %pad.14.refs_1_.late_ref), custom_call_target="tpu_custom_call" | custom-call | tf_op jit(solution)/shard_map/pallas_call | solution.py:157
  281.6 1.7 fusion.10
  (149 shorter events, 17.1 us)
Async XLA Ops:
  44.8 4.8 %copy-start.21 = (bf16[2,192,768]{2,1,0:T(8,128)(2,1)S(1)}, bf16[2,192,768]{2,1,0:T(8,128)(2,1)}, u32[]{:S(2)}) copy-start(bf16[2,192,768]{2,1,0:T(8,128)(2,1)} %w_ref.1) | copy-start | bytes 1769476
  49.5 37.1 %copy-start.38 = (bf16[48,1536]{1,0:T(8,128)(2,1)}, bf16[48,1536]{1,0:T(8,128)(2,1)S(1)}, u32[]{:S(2)}) copy-start(bf16[48,1536]{1,0:T(8,128)(2,1)S(1)} %get-tuple-element.86.x_ref) | copy-start | bytes 442372
  49.5 37.1 %copy-start.47 = (bf16[2048,768]{1,0:T(8,128)(2,1)}, bf16[2048,768]{1,0:T(8,128)(2,1)S(1)}, u32[]{:S(2)}) copy-start(bf16[2048,768]{1,0:T(8,128)(2,1)S(1)} %get-tuple-element.90) | copy-start | bytes 9437188
  49.5 37.1 %copy-start.54 = (s32[1,128,1]{1,2,0:T(1,128)S(1)}, s32[1,128,1]{1,2,0:T(1,128)}, u32[]{:S(2)}) copy-start(s32[1,128,1]{1,2,0:T(1,128)} %param.14) | copy-start | bytes 1540
  74.8 1.4 copy-start.4
  76.2 1.5 copy-start.10
  86.8 1.5 copy-start.22
  86.8 1.5 copy-start.7
  86.8 1.5 copy-start.11
  90.0 38.4 %copy-start.28 = (f32[128,768]{1,0:T(8,128)}, f32[128,768]{1,0:T(8,128)S(1)}, u32[]{:S(2)}) copy-start(f32[128,768]{1,0:T(8,128)S(1)} %get-tuple-element.75.residual_ref) | copy-start | bytes 1179652
  90.0 38.4 %copy-start.34 = (bf16[128,768]{1,0:T(8,128)(2,1)}, bf16[128,768]{1,0:T(8,128)(2,1)S(1)}, u32[]{:S(2)}) copy-start(bf16[128,768]{1,0:T(8,128)(2,1)S(1)} %get-tuple-element.77.h_ref) | copy-start | bytes 589828
  90.0 38.4 %copy-start.36 = (bf16[256,384]{1,0:T(8,128)(2,1)}, bf16[256,384]{1,0:T(8,128)(2,1)S(1)}, u32[]{:S(2)}) copy-start(bf16[256,384]{1,0:T(8,128)(2,1)S(1)} %get-tuple-element.74.dispatch_ref) | copy-start | bytes 589828
  90.0 38.4 %copy-start.42 = (f32[128,16]{1,0:T(8,128)}, f32[128,16]{1,0:T(8,128)S(1)}, u32[]{:S(2)}) copy-start(f32[128,16]{1,0:T(8,128)S(1)} %get-tuple-element.76.probs_ref) | copy-start | bytes 24580
  90.0 11.8 %copy-start.24 = (bf16[2,768,192]{1,2,0:T(8,128)(2,1)S(1)}, bf16[2,768,192]{1,2,0:T(8,128)(2,1)}, u32[]{:S(2)}) copy-start(bf16[2,768,192]{1,2,0:T(8,128)(2,1)} %param.22) | copy-start | bytes 1769476
  128.4 2.0 copy-start.5
  128.6 2.8 copy-start.52
  128.6 5.0 %copy-start.50 = (bf16[4,1,80,768]{3,2,1,0:T(8,128)(2,1)}, bf16[4,1,80,768]{3,2,1,0:T(8,128)(2,1)S(1)}, u32[]{:S(2)}) copy-start(bf16[4,1,80,768]{3,2,1,0:T(8,128)(2,1)S(1)} %get-tuple-element.120) | copy-start | bytes 1474564
  132.3 1.2 copy-start.55
  134.6 1.3 copy-start.57
  163.5 1.3 copy-start.15
  163.5 1.3 copy-start.17
  164.8 1.9 copy-start.53
  164.8 1.9 copy-start.56
  166.7 1.0 copy-start.51
  166.7 1.2 copy-start.58
  167.6 1.4 copy-start.48
  169.7 12.4 %copy-start.12 = (bf16[1,128,768]{2,1,0:T(8,128)(2,1)S(1)}, bf16[1,128,768]{2,1,0:T(8,128)(2,1)}, u32[]{:S(2)}) copy-start(bf16[1,128,768]{2,1,0:T(8,128)(2,1)} %param.13) | copy-start | bytes 589828
  169.7 12.4 %copy-start.23 = (s32[128,1]{1,0:T(8,128)S(1)}, s32[128,1]{1,0:T(8,128)}, u32[]{:S(2)}) copy-start(s32[128,1]{1,0:T(8,128)} %copy-done.22) | copy-start | bytes 1540
  169.7 12.4 %copy-start.29 = (f32[128,768]{1,0:T(8,128)S(1)}, f32[128,768]{1,0:T(8,128)}, u32[]{:S(2)}) copy-start(f32[128,768]{1,0:T(8,128)} %copy-done.28) | copy-start | bytes 1179652
  169.7 12.4 %copy-start.35 = (bf16[128,768]{1,0:T(8,128)(2,1)S(1)}, bf16[128,768]{1,0:T(8,128)(2,1)}, u32[]{:S(2)}) copy-start(bf16[128,768]{1,0:T(8,128)(2,1)} %copy-done.34) | copy-start | bytes 589828
  169.7 12.4 %copy-start.37 = (bf16[256,384]{1,0:T(8,128)(2,1)S(1)}, bf16[256,384]{1,0:T(8,128)(2,1)}, u32[]{:S(2)}) copy-start(bf16[256,384]{1,0:T(8,128)(2,1)} %copy-done.36) | copy-start | bytes 589828
  169.7 12.4 %copy-start.43 = (f32[128,16]{1,0:T(8,128)S(1)}, f32[128,16]{1,0:T(8,128)}, u32[]{:S(2)}) copy-start(f32[128,16]{1,0:T(8,128)} %copy-done.42) | copy-start | bytes 24580
  181.1 1.0 copy-start.9
  184.1 10.7 %copy-start.30 = (f32[128,768]{1,0:T(8,128)}, f32[128,768]{1,0:T(8,128)S(1)}, u32[]{:S(2)}) copy-start(f32[128,768]{1,0:T(8,128)S(1)} %get-tuple-element.79) | copy-start | bytes 1179652
  198.3 1.1 copy-start.14
  198.4 1.3 copy-start.1
  198.4 1.4 copy-start.26
  198.4 1.5 copy-start.33
  198.4 1.5 copy-start.39
  228.3 1.4 copy-start.2
  229.7 3.3 %copy-start.19 = (bf16[2,192,768]{2,1,0:T(8,128)(2,1)}, bf16[2,192,768]{2,1,0:T(8,128)(2,1)S(1)}, u32[]{:S(2)}) copy-start(bf16[2,192,768]{2,1,0:T(8,128)(2,1)S(1)} %get-tuple-element.106) | copy-start | bytes 1769476
  239.6 20.0 %copy-start.3 = (bf16[16,48,1536]{2,1,0:T(8,128)(2,1)S(1)}, bf16[16,48,1536]{2,1,0:T(8,128)(2,1)}, u32[]{:S(2)}) copy-start(bf16[16,48,1536]{2,1,0:T(8,128)(2,1)} %copy-done.2) | copy-start | bytes 7077892
  260.6 2.0 copy-start.31
  263.5 15.4 %copy-start.41 = (bf16[6,1536]{1,0:T(8,128)(2,1)S(1)}, bf16[6,1536]{1,0:T(8,128)(2,1)}, u32[]{:S(2)}) copy-start(bf16[6,1536]{1,0:T(8,128)(2,1)} %wkv_ref.3) | copy-start | bytes 55300
  263.5 15.4 %copy-start.45 = (bf16[6,768]{1,0:T(8,128)(2,1)S(1)}, bf16[6,768]{1,0:T(8,128)(2,1)}, u32[]{:S(2)}) copy-start(bf16[6,768]{1,0:T(8,128)(2,1)} %wq_ref.3) | copy-start | bytes 27652
  264.2 17.4 %copy-start.16 = (bf16[2,192,768]{2,1,0:T(8,128)(2,1)S(1)}, bf16[2,192,768]{2,1,0:T(8,128)(2,1)}, u32[]{:S(2)}) copy-start(bf16[2,192,768]{2,1,0:T(8,128)(2,1)} %copy-done.15) | copy-start | bytes 1769476
  264.2 17.4 %copy-start.18 = (bf16[2,192,768]{2,1,0:T(8,128)(2,1)S(1)}, bf16[2,192,768]{2,1,0:T(8,128)(2,1)}, u32[]{:S(2)}) copy-start(bf16[2,192,768]{2,1,0:T(8,128)(2,1)} %copy-done.17) | copy-start | bytes 1769476
  266.0 15.6 %copy-start.20 = (bf16[2,192,768]{2,1,0:T(8,128)(2,1)S(1)}, bf16[2,192,768]{2,1,0:T(8,128)(2,1)}, u32[]{:S(2)}) copy-start(bf16[2,192,768]{2,1,0:T(8,128)(2,1)} %copy-done.19) | copy-start | bytes 1769476
  (11 other events, 9.1 us)

commit v5 on v4

--- a/solution.py
+++ b/solution.py
@@ -210,54 +210,98 @@
     return begin, forward, end
 
 
+def ring_parts(src, at, send, recv):
+    c, e, z, xh, k = spot()
+    size, me, device = group("z")
+    above, below, beyond = (lax.rem(me + i, 4) for i in (1, 3, 2))
+    rows = src.shape[0]
+    cut = rows // 32 * 16
+    upper, lower = pl.ds(0, rows - cut), pl.ds(rows - cut, cut)
+    up = push(src, at(me), send.at[0], recv.at[0], device(above))
+    down = push(src, at(me), send.at[1], recv.at[1], device(below))
+    on_up = at(below).at[upper, :]
+    on_down = at(above).at[lower, :]
+    on_up = push(on_up, on_up, send.at[2], recv.at[2], device(above))
+    on_down = push(on_down, on_down, send.at[3], recv.at[3], device(below))
+
+    def begin():
+        up.start()
+        down.start()
+
+    def relay():
+        up.wait_recv()
+        on_up.start()
+        down.wait_recv()
+        on_down.start()
+
+    def arrive():
+        on_up.wait_recv()
+        on_down.wait_recv()
+
+    def end():
+        for copy in (up, down, on_up, on_down):
+            copy.wait_send()
+
+    return begin, relay, arrive, end
+
+
 def spread_parts(x, out, here, send, recv):
     c, e, z, xh, k = spot()
     at = lambda z, xh, k: z * 4 + xh * 2 + k
-    forth = [lax.rem(z + i, 4) for i in range(1, 4)]
-    back = [lax.rem(z + 4 - i, 4) for i in range(1, 4)]
+    around = [lax.rem(z + i, 4) for i in (3, 1, 2)]
     side, twin = (at(z, 1 - xh, k), e), (at(z, xh, 1 - k), e)
     mine, theirs = at(z, xh, k), at(z, 1 - xh, k)
-    held = [mine, theirs] + [at(p, xh, k) for p in back] + [at(p, 1 - xh, k) for p in back]
+    held = [mine, theirs] + [at(p, xh, k) for p in around] + [at(p, 1 - xh, k) for p in around]
     across = push(x, out.at[mine], send.at[0], recv.at[0], side)
-    first = [
-        push(x, out.at[mine], send.at[1 + i], recv.at[1 + i], (at(p, xh, k), e))
-        for i, p in enumerate(forth)
-    ]
-    second = [
-        push(out.at[theirs], out.at[theirs], send.at[4 + i], recv.at[4 + i], (at(p, xh, k), e))
-        for i, p in enumerate(forth)
-    ]
+    first = ring_parts(
+        x, lambda p: out.at[at(p, xh, k)], send.at[pl.ds(1, 4)], recv.at[pl.ds(1, 4)]
+    )
+    second = ring_parts(
+        out.at[theirs],
+        lambda p: out.at[at(p, 1 - xh, k)],
+        send.at[pl.ds(5, 4)],
+        recv.at[pl.ds(5, 4)],
+    )
     pair = [
-        push(x if n == 0 else out.at[b], out.at[b], send.at[7 + n], recv.at[7 + n], twin)
+        push(x if n == 0 else out.at[b], out.at[b], send.at[9 + n], recv.at[9 + n], twin)
         for n, b in enumerate(held)
     ]
     own = pltpu.make_async_copy(x, out.at[mine], here)
 
     def begin():
-        for copy in [across, *first, pair[0], own]:
-            copy.start()
+        across.start()
+        first[0]()
+        pair[0].start()
+        own.start()
 
     def middle():
         across.wait_recv()
-        for copy in [*second, pair[1]]:
-            copy.start()
-
-    def late():
-        for copy, hand in zip(first, pair[2:5]):
-            copy.wait_recv()
-            hand.start()
+        second[0]()
+        pair[1].start()
+
+    def relay_first():
+        first[1]()
+        pair[2].start()
+        pair[3].start()
+
+    def relay_second():
+        second[1]()
+        pair[5].start()
+        pair[6].start()
 
     def end():
-        for copy, hand in zip(second, pair[5:]):
-            copy.wait_recv()
-            hand.start()
+        first[2]()
+        pair[4].start()
+        second[2]()
+        pair[7].start()
         for copy in pair:
             copy.wait()
-        for copy in [across, *first, *second]:
-            copy.wait_send()
+        across.wait_send()
+        first[3]()
+        second[3]()
         own.wait()
 
-    return begin, middle, late, end
+    return begin, middle, relay_first, relay_second, end
 
 
 def cross_peers():
@@ -271,7 +315,9 @@
     exps = [lax.rem(e + i, EXP) for i in range(1, EXP)]
     peers = [lax.rem(c + i, CTX) for i in range(1, CTX)]
     greet([(c, p) for p in exps] + [(p, e) for p in peers])
-    x_begin, x_middle, x_late, x_end = spread_parts(x, x_all, here.at[0], x_send, x_recv)
+    x_begin, x_middle, x_first, x_second, x_end = spread_parts(
+        x, x_all, here.at[0], x_send, x_recv
+    )
     rows = [
         push(packed, eight.at[e], send.at[i], recv.at[i], (c, p)) for i, p in enumerate(exps)
     ]
@@ -292,7 +338,8 @@
     for p, copy in zip(peers, heads):
         pl.when(owns(p))(copy.start)
     pl.when(owns(c))(own_head.start)
-    x_late()
+    x_first()
+    x_second()
     for p, copy in zip(peers, heads):
         pl.when(owns(p))(copy.wait_send)
         pl.when(owns(c))(copy.wait_recv)
@@ -310,7 +357,7 @@
         out_shape=[jax.ShapeDtypeStruct(s, low) for s in shapes],
         in_specs=[ANY, ANY],
         out_specs=[ANY] * 3,
-        scratch_shapes=[sems((3,)), sems((22,)), sems((22,)), sems((15,)), sems((15,))],
+        scratch_shapes=[sems((3,)), sems((22,)), sems((22,)), sems((17,)), sems((17,))],
         compiler_params=pltpu.CompilerParams(
             collective_id=ident, has_side_effects=True, vmem_limit_bytes=2 << 20
         ),
@@ -320,20 +367,17 @@
 def lists_kernel(x, w, x_all, w_all, here, send, recv, w_send, w_recv):
     c, e, z, xh, k = spot()
     greet(cross_peers())
-    size, me, device = group("z")
-    copies = []
-    for i in range(1, size):
-        to = device(lax.rem(me + i, size))
-        copies.append(push(x, x_all.at[me], send.at[i - 1], recv.at[i - 1], to))
+    me = group("z")[1]
+    x_begin, x_relay, x_arrive, x_end = ring_parts(x, lambda p: x_all.at[p], send, recv)
     w_begin, w_forward, w_end = quad_parts(w, w_all, here.at[0], w_send, w_recv)
     own = pltpu.make_async_copy(x, x_all.at[me], here.at[1])
-    for copy in copies:
-        copy.start()
+    x_begin()
     w_begin()
     own.start()
+    x_relay()
     w_forward()
-    for copy in copies:
-        copy.wait()
+    x_arrive()
+    x_end()
     own.wait()
     w_end()
 
@@ -346,7 +390,7 @@
         out_shape=[jax.ShapeDtypeStruct(s, low) for s in shapes],
         in_specs=[pl.BlockSpec(memory_space=pltpu.VMEM)] * 2,
         out_specs=[ANY] * 2,
-        scratch_shapes=[sems((2,))] + [sems((3,))] * 4,
+        scratch_shapes=[sems((2,)), sems((4,)), sems((4,)), sems((3,)), sems((3,))],
         compiler_params=pltpu.CompilerParams(
             collective_id=ident, has_side_effects=True, vmem_limit_bytes=4 << 20
         ),
@@ -445,7 +489,9 @@
     keys, bias, scores, here, x_send, x_recv, w_send, w_recv,
 ):
     block = pl.program_id(0)
-    x_begin, x_middle, x_late, x_end = spread_parts(x_ref, x_all, here.at[0], x_send, x_recv)
+    x_begin, x_middle, x_first, x_second, x_end = spread_parts(
+        x_ref, x_all, here.at[0], x_send, x_recv
+    )
     w_begin, w_forward, w_end = quad_parts(w_ref, w_all, here.at[1], w_send, w_recv)
 
     @pl.when(block == 0)
@@ -458,9 +504,13 @@
     def _():
         x_middle()
 
-    @pl.when(block == 5)
+    @pl.when(block == 4)
     def _():
-        x_late()
+        x_first()
+
+    @pl.when(block == 6)
+    def _():
+        x_second()
 
     @pl.when(block == 0)
     def _():
@@ -520,7 +570,7 @@
             jax.ShapeDtypeStruct((CTX, *x.shape), low),
             jax.ShapeDtypeStruct((2, 4, *w.shape[1:]), low),
         ),
-        in_specs=[whole(3, HEAD_DIM, LEN), whole(BUCKETS, 128), ANY, ANY],
+        in_specs=[whole(3, HEAD_DIM, LEN), whole(BUCKETS, 128), ANY, whole(*w.shape)],
         out_specs=(
             pl.BlockSpec((LEN, QUERIES), lambda i: (0, i)),
             pl.BlockSpec((HEAD_DIM, QUERIES), lambda i: (0, i)),
@@ -534,13 +584,13 @@
             pltpu.VMEM((6 * CHUNK, QUERIES), wide),
             pltpu.VMEM((LEN, QUERIES), wide),
             pltpu.SemaphoreType.DMA((2,)),
-            pltpu.SemaphoreType.DMA((15,)),
-            pltpu.SemaphoreType.DMA((15,)),
+            pltpu.SemaphoreType.DMA((17,)),
+            pltpu.SemaphoreType.DMA((17,)),
             pltpu.SemaphoreType.DMA((3,)),
             pltpu.SemaphoreType.DMA((3,)),
         ],
         compiler_params=pltpu.CompilerParams(
-            collective_id=ident, has_side_effects=True, vmem_limit_bytes=11 << 20
+            collective_id=ident, has_side_effects=True, vmem_limit_bytes=13 << 20
         ),
     )(qkv, table, x, w)
 
@@ -551,7 +601,9 @@
     values, dk, dv, tiles, slopes, here, x_send, x_recv, send, recv,
 ):
     block = pl.program_id(0)
-    x_begin, x_middle, x_late, x_end = spread_parts(x_ref, x_all, here, x_send, x_recv)
+    x_begin, x_middle, x_first, x_second, x_end = spread_parts(
+        x_ref, x_all, here, x_send, x_recv
+    )
     size, me, device = group("x")
     across = push(g_ref.at[:, 1 - me], g_out, send.at[0], recv.at[0], device(1 - me))
     size, z, device_z = group("z")
@@ -566,17 +618,21 @@
     def _():
         greet(cross_peers())
         x_begin()
-        for copy in around:
-            copy.start()
-
-    @pl.when(block == 1)
+
+    @pl.when(block == 2)
     def _():
         x_middle()
         across.start()
 
+    @pl.when(block == 3)
+    def _():
+        x_first()
+        for copy in around:
+            copy.start()
+
     @pl.when(block == 5)
     def _():
-        x_late()
+        x_second()
 
     @pl.when(block == 0)
     def _():
@@ -656,8 +712,8 @@
             pltpu.VMEM((6 * CHUNK, QUERIES), wide),
             pltpu.VMEM((LEN, QUERIES), low),
             pltpu.SemaphoreType.DMA,
-            pltpu.SemaphoreType.DMA((15,)),
-            pltpu.SemaphoreType.DMA((15,)),
+            pltpu.SemaphoreType.DMA((17,)),
+            pltpu.SemaphoreType.DMA((17,)),
             pltpu.SemaphoreType.DMA((4,)),
             pltpu.SemaphoreType.DMA((4,)),
         ],
@@ -859,12 +915,88 @@
     late_ref[:, D:] = jnp.where(iota((D, 128), 1) == 65, gains, extra).astype(low)
 
 
-def rms_scale(values_in, gain_vec):
-    return (
-        values_in
-        * lax.rsqrt(jnp.mean(values_in * values_in, axis=-1, keepdims=True) + epsilon)
-        * gain_vec
-    )
+def expert_kernel(lists_ref, in_ref, out_ref, partial_ref, grad_in_ref, grad_out_ref):
+    for n in range(2):
+        rows = lists_ref[:, n].reshape(ZED * 80, D)
+        grads = lists_ref[:, 2 + n].reshape(ZED * 80, D)
+        weight_in, weight_out = in_ref[n], out_ref[n]
+        pre = dot(rows, weight_in, (1, 1))
+        square = pre * pre
+        bend = jnp.tanh(0.7978845608028654 * (pre + 0.044715 * square * pre))
+        hidden = (0.5 * pre * (1.0 + bend)).astype(low)
+        slope = 0.5 * (1.0 + bend) + 0.5 * pre * (1.0 - bend * bend) * (
+            0.7978845608028654 * (1.0 + 0.134145 * square)
+        )
+        grad_pre = (dot(grads, weight_out, (1, 1)) * slope).astype(low)
+        y = jnp.dot(hidden, weight_out, preferred_element_type=wide).astype(low)
+        partial_ref[:, n * 80 : (n + 1) * 80, :] = y.reshape(ZED, 80, D)
+        back = jnp.dot(grad_pre, weight_in, preferred_element_type=wide).astype(low)
+        partial_ref[:, 160 + n * 80 : 160 + (n + 1) * 80, :] = back.reshape(ZED, 80, D)
+        grad_in_ref[n] = dot(grad_pre, rows, (0, 0)).astype(low)
+        grad_out_ref[n] = dot(hidden, grads, (0, 0)).astype(low)
+
+
+def unlist_kernel(partial_ref, others_ref, out_ref):
+    c, e, z, xh, k = spot()
+    total = partial_ref[z].astype(wide) + jnp.sum(others_ref[...].astype(wide), axis=0)
+    row = iota((EXP * SLOTS, 1), 0)
+    inner = row % SLOTS
+    source = jnp.where(inner < 4 * CAP, inner // CAP * 80 + row // SLOTS * CAP + inner % CAP, -1)
+    pick = (iota((EXP * SLOTS, 320), 1) == source).astype(low)
+    out = jnp.dot(pick, total.astype(low), preferred_element_type=wide).astype(low)
+    out_ref[...] = out.reshape(EXP, SLOTS, D)
+
+
+def head_weights_kernel(grads_ref, h_ref, tiles_ref, late_ref, others_ref, out_ref, sum_ref):
+    c, e, z, xh, k = spot()
+    grads = grads_ref[...].reshape(192, LEN)
+    product = jnp.dot(grads, h_ref[...], preferred_element_type=wide).astype(low)
+    column = iota((1, EXP * TOK), 1)
+    place = (column % TOK // 8 * EXP + column // TOK) * 6 + column % 8
+    place = jnp.where(column % 8 < 6, place, -1)
+    by_owner = (iota((D, EXP * TOK), 0) == place).astype(low)
+    product = jnp.dot(product, by_owner, preferred_element_type=wide).T
+    tile = lambda n, half: tiles_ref[
+        n * CHUNK : (n + 1) * CHUNK, half * TOK : (half + 1) * TOK
+    ]
+    near = jnp.concatenate([tile(n, 0) + tile(n + 1, 1) for n in (1, 2, 3)], axis=0)
+    ids = near_buckets(near.shape, CHUNK)
+    lane = iota((1, 192), 1)
+    buckets = jnp.zeros((1, 192), wide)
+    for b in range(BUCKETS):
+        part = jnp.sum(jnp.where(ids == b, near, 0.0), axis=0, keepdims=True)
+        if b == BUCKETS // 2 - 1:
+            part = part + jnp.sum(tile(0, 0) + tile(0, 1) + tile(1, 1), axis=0, keepdims=True)
+        if b == BUCKETS - 1:
+            part = part + jnp.sum(tile(4, 0) + tile(5, 0) + tile(5, 1), axis=0, keepdims=True)
+        buckets = jnp.where(lane == b, jnp.sum(part, axis=1, keepdims=True), buckets)
+    sixth = iota((EXP * TOK, 1), 0) % 8 == 6
+    product = jnp.where(sixth, buckets, product)
+    out_ref[...] = product.astype(low).reshape(EXP, TOK, 192)
+    total = late_ref[z].astype(wide) + jnp.sum(others_ref[...].astype(wide), axis=0)
+    sum_ref[...] = total.astype(low)
+
+
+def owners_kernel(own_ref, others_ref, late_ref, late_others_ref, out_ref, sum_ref):
+    c, e, z, xh, k = spot()
+    total = own_ref[e].astype(wide) + jnp.sum(others_ref[...].astype(wide), axis=0)
+    out_ref[...] = total.reshape(CTX, 8, 192)
+    late = late_ref[xh].astype(wide) + late_others_ref[0].astype(wide)
+    empty = jnp.zeros((2, 896), wide)
+    for n in range(EXP):
+        sum_ref[n] = jnp.concatenate([late[6 * n : 6 * n + 6], empty], axis=0)
+
+
+def tokens_kernel(grads_ref, first_ref, second_ref, x_ref, residual_ref, out_ref):
+    grads = grads_ref[...].reshape(3 * D, TOK).astype(wide).T.astype(low)
+    grad_h = dot(grads[:, :D], first_ref[:, 896:], (1, 1))
+    grad_h = grad_h + dot(grads[:, D:], second_ref[...], (1, 1))
+    gain = first_ref[:, :128].astype(wide).T[64:65, :]
+    x = x_ref[...].astype(wide)
+    scale = lax.rsqrt(jnp.mean(x * x, axis=1, keepdims=True) + epsilon)
+    along = grad_h * gain
+    mean = jnp.mean(along * x, axis=1, keepdims=True)
+    out_ref[...] = residual_ref[...] + scale * along - (scale * scale * scale * mean) * x
 
 
 def dot(a, b, dims=(1, 0)):
@@ -887,8 +1019,6 @@
     expert_in,
     expert_out,
 ):
-    x_rows = tokens[0].astype(wide)
-
     extra = jnp.concatenate(
         [
             norm_gain_one[:, None],
@@ -921,8 +1051,6 @@
         head_qkv, head_table, block, expert_out, 18
     )
     full = full.reshape(D, 2 * D + 128)
-    full_out = full[:, :896]
-    gain_one = full[:, 64].astype(wide)
     attended_low = from_heads(attended_head, 5).reshape(D, TOK)
     routed = (TOK, D)
     residual, h_two, route_probs, dispatch, outgoing = plain(
@@ -939,7 +1067,7 @@
         tokens[0],
         cotangent[0],
         routes[0],
-        full_out,
+        full,
     )
     received = swap(outgoing.reshape(EXP, SLOTS, D), "exp", 6, 0).reshape(EXP * SLOTS, D)
 
@@ -951,28 +1079,18 @@
     )
     lists = lists.reshape(ZED, 4, 80, D)
     experts_here = experts_in.reshape(2, D, D), experts_out.reshape(2, D, D)
-    partial, grads_in, grads_out = [], [], []
-    for n in range(2):
-        rows = lists[:, n].reshape(ZED * 80, D)
-        grads = lists[:, 2 + n].reshape(ZED * 80, D)
-        weight_in, weight_out = experts_here[0][n], experts_here[1][n]
-        pre_act = dot(rows, weight_in, (1, 1))
-        hidden_wide, gelu_back = jax.vjp(jax.nn.gelu, pre_act)
-        hidden = hidden_wide.astype(low)
-        grad_hidden = dot(grads, weight_out, (1, 1))
-        grad_pre = gelu_back(grad_hidden)[0].astype(low)
-        partial.append(dot(hidden, weight_out).astype(low).reshape(ZED, 80, D))
-        partial.append(dot(grad_pre, weight_in).astype(low).reshape(ZED, 80, D))
-        grads_in.append(dot(grad_pre, rows, (0, 0)).astype(low))
-        grads_out.append(dot(hidden, grads, (0, 0)).astype(low))
-    partial = jnp.stack([partial[0], partial[2], partial[1], partial[3]], axis=1)
-    partial = partial.reshape(ZED, 320, D)
-    grads_out = jnp.stack(grads_out).reshape(2, 2, 2, 192, D)
+    partial, grads_in, grads_out = plain(
+        expert_kernel,
+        [((ZED, 320, D), low), ((2, D, D), low), ((2, D, D), low)],
+        28,
+        lists,
+        *experts_here,
+    )
+    grads_out = grads_out.reshape(2, 2, 2, 192, D)
     others, grads_own, grads_other = return_lists(partial, grads_out, 8)
     grad_expert_out = grads_own.astype(wide) + grads_other.astype(wide)
-    summed = add_up(partial, "z", 0, others).astype(low)
-    spread = dot(compact, summed, (0, 0)).astype(low).reshape(EXP, SLOTS, D)
-    expert_grads = jnp.stack(grads_in).reshape(2, 2, 2, 192, D)
+    spread = plain(unlist_kernel, [((EXP, SLOTS, D), low)], 12, partial, others)[0]
+    expert_grads = grads_in.reshape(2, 2, 2, 192, D)
     back, others = swaps(9, (spread, "exp", 0, True), (expert_grads, "core", 2, False))
     expert_grads = add_up(expert_grads, "core", 2, others).astype(low)
     mixed_rows, grad_residual, grad_attended, late = plain(
@@ -986,7 +1104,7 @@
         route_probs,
         routes[0],
         h_two,
-        full_out,
+        full,
         attended_low,
     )
     late = late.reshape(8, 2, 48, 896)
@@ -1000,53 +1118,41 @@
         head_qkv, probs, attended, inverse, head_grad, block_qkv, expert_grads, late, 19
     )
     qkv_full = qkv_full.reshape(D, 2 * D)
-    late = add_up(late, "z", 0, late_others).astype(low)
     grad_expert_in = jnp.swapaxes(add_up(expert_grads, "x", 1, others[None]), 1, 2)
 
-    tile = lambda n, half: tile_sums[n * CHUNK : (n + 1) * CHUNK, half * TOK : (half + 1) * TOK]
-    near = jnp.concatenate([tile(n, 0) + tile(n + 1, 1) for n in (1, 2, 3)], axis=0)
-    bucket_range = jnp.arange(BUCKETS, dtype=jnp.int32)
-    bucket_sums = jnp.sum(
-        jnp.where(
-            near_buckets(near.shape, CHUNK)[None] == bucket_range[:, None, None], near[None], 0.0
-        ),
-        axis=(1, 2),
-    )
-    bucket_sums = bucket_sums + jnp.where(
-        bucket_range == BUCKETS // 2 - 1, jnp.sum(tile(0, 0) + tile(0, 1) + tile(1, 1)), 0.0
-    )
-    bucket_sums = bucket_sums + jnp.where(
-        bucket_range == BUCKETS - 1, jnp.sum(tile(4, 0) + tile(5, 0) + tile(5, 1)), 0.0
-    )
-    sixth = jnp.arange(EXP * TOK, dtype=jnp.int32) % 8 == 6
-    place = jnp.arange(D, dtype=jnp.int32)
-    place = place // 6 % EXP * TOK + place // 48 * 8 + place % 6
-    by_owner = (jnp.arange(EXP * TOK, dtype=jnp.int32)[:, None] == place[None, :]).astype(low)
-    head_weights = dot(h_all, head_grads.reshape(192, LEN), (0, 1)).astype(low)
-    head_weights = dot(by_owner, head_weights)
-    head_weights = head_weights + jnp.where(
-        sixth[:, None], jnp.pad(bucket_sums, (0, 192 - BUCKETS))[None, :], 0.0
-    )
-    head_weights = head_weights.astype(low).reshape(EXP, TOK, 192)
-    grad_qkv, others, late_others = swaps(
-        11,
+    head_weights, late = plain(
+        head_weights_kernel,
+        [((EXP, TOK, 192), low), ((2, 48, 896), low)],
+        20,
+        head_grads,
+        h_all,
+        tile_sums,
+        late,
+        late_others,
+    )
+    others, late_others = swaps(
+        11, (head_weights, "exp", 0, False), (late, "x", 0, False)
+    )
+    head_weights, late = plain(
+        owners_kernel,
+        [((CTX, 8, 192), wide), ((EXP, 8, 896), wide)],
+        8,
+        head_weights,
+        others,
+        late,
+        late_others,
+    )
+    grad_qkv, by_head, others = swaps(
+        12,
         (head_grads, "from_heads", None, True),
-        (head_weights, "exp", 0, False),
-        (late, "x", 0, False),
-    )
-    grad_qkv = grad_qkv.reshape(3 * D, TOK)
-    head_weights = add_up(head_weights, "exp", 0, others).reshape(CTX, 8, 192)
-    late = add_up(late, "x", 0, late_others).reshape(EXP, 6, 896)
-    late = jnp.pad(late, ((0, 0), (0, 2), (0, 0)))
-    by_head, others = swaps(
-        12, (head_weights, "head_rows", None, True), (late, "exp", 0, False)
+        (head_weights, "head_rows", None, True),
+        (late, "exp", 0, False),
     )
     finished = finish(by_head, late, others, query_weight, kv_weight, norm_gain_one)
 
-    grad_h_one = dot(grad_qkv[:D], full[:, 896:], (0, 1))
-    grad_h_one = grad_h_one + dot(grad_qkv[D:], qkv_full, (0, 1))
-    norm_one_back = jax.vjp(lambda x: rms_scale(x, gain_one), x_rows)[1]
-    grad_tokens = grad_residual + norm_one_back(grad_h_one)[0]
+    grad_tokens = plain(
+        tokens_kernel, [(routed, wide)], 16, grad_qkv, full, qkv_full, tokens[0], grad_residual
+    )[0]
     return (
         mixed_rows[None],
         grad_tokens[None],

time: 284 us -> 263 us (0.926)
  matrix products: 18.7 us -> 0.47 us
  other arithmetic: 16.7 us -> 8.28 us
    dot_general x17 -> x1, matrix products: 18.7 us -> 0.47 us  [dot(): lax.dot_general(a, b, (((dims[0],), (dims[1],)), ((), ())), preferred_ele...]
    pallas_call x4 -> x9, Pallas kernels: 8.39 us -> 19.9 us  [plain(): pl.pallas_call(kernel, out_shape=[jax.ShapeDtypeStruct(shape, kind) for s...]
    unnamed x118 -> x84, local copies, waits for them, and re-layouts: 16.2 us -> 21.5 us
    reduce_sum x5 -> x0, other arithmetic: 4.82 us -> none  [the longest x3 3.19 us: add_up(): return mine.astype(wide) + jnp.sum(others.astype(wide), axis=0)]
    pallas_call x1, Pallas kernels: 26.5 us -> 22.1 us  [gather_lists(): pl.pallas_call(lists_kernel, out_shape=[jax.ShapeDtypeStruct(s, low) for...]
    pallas_call x6, Pallas kernels: 71.8 us -> 68 us  [swaps(): pl.pallas_call(functools.partial(swaps_kernel, [item[1:] for item in item...]
    add x5 -> x0, other arithmetic: 3.28 us -> none  [the longest x2 1.71 us: add_up(): return mine.astype(wide) + jnp.sum(others.astype(wide), axis=0)]
where the time goes in v5:
time: 263 us; the launch traced here: 261 us
  Pallas kernels  225 us (86%)
  local copies, waits for them, and re-layouts  25.9 us (10%)
  other arithmetic  8.28 us (3%)
    pallas_call x6, Pallas kernels, swaps(): pl.pallas_call(functools.partial(swaps_kernel, [item[1:] for item in item...  68 us
    pallas_call x1, Pallas kernels, opening(): pl.pallas_call(open_kernel, out_shape=[jax.ShapeDtypeStruct(s, low) for s...  37.8 us
    pallas_call x1, Pallas kernels, attend_back(): pl.pallas_call(backward_kernel, grid=(LEN // QUERIES,), out_shape=(jax.Sh...  27.9 us
    pallas_call x1, Pallas kernels, return_lists(): pl.pallas_call(return_kernel, out_shape=[jax.ShapeDtypeStruct(s, low) for...  24.4 us
    pallas_call x1, Pallas kernels, attend(): pl.pallas_call(forward_kernel, grid=(LEN // QUERIES,), out_shape=(pltpu.H...  24.2 us
    pallas_call x1, Pallas kernels, gather_lists(): pl.pallas_call(lists_kernel, out_shape=[jax.ShapeDtypeStruct(s, low) for...  22.1 us
    unnamed x84, local copies, waits for them, and re-layouts  21.5 us
    pallas_call x9, Pallas kernels, plain(): pl.pallas_call(kernel, out_shape=[jax.ShapeDtypeStruct(shape, kind) for s...  19.9 us

profile of v5, /device:TPU:1, one launch (start us, length us, event | category | flops | bytes accessed | tf_op | source)
XLA Modules:
  0.0 260.9 jit_solution(16224456419527449042)
XLA Ops:
  0.6 0.8 copy.30
  1.4 0.7 pad_bitcast_fusion
  2.2 0.8 copy.31
  2.9 0.8 concatenate.3.extra_ref
  3.7 0.7 copy-done.36
  4.4 0.7 copy-done.38
  5.1 0.7 copy-done.40
  6.0 0.9 copy-done.14
  6.9 37.8 %shard_map.204 = (bf16[8,15,16,128]{3,2,1,0:T(8,128)(2,1)S(1)}, bf16[16,8,16,128]{3,2,1,0:T(8,128)(2,1)S(1)}, bf16[16,128,768]{2,1,0:T(8,128)(2,1)S(1)}) custom-call(bf16[15,16,128]{2,1,0:T(8,128)(2,1)S(1)} %shard_map.203.packed, bf16[128,768]{1,0:T(8,128)(2,1)S(1)} %bitcast.61), custom_call_target="tpu_custom_call" | custom-call | tf_op jit(solution)/shard_map/pallas_call | solution.py:355
  44.7 4.7 %shard_map.205 = (bf16[3,64,2048]{2,1,0:T(8,128)(2,1)S(1)}, bf16[2048,768]{1,0:T(8,128)(2,1)S(1)}, f32[32,128]{1,0:T(8,128)S(1)}, bf16[48,1664]{1,0:T(8,128)(2,1)S(1)}, bf16[48,1536]{1,0:T(8,128)(2,1)S(1)}) custom-call(bf16[2048,128]{1,0:T(8,128)(2,1)S(1)} %bitcast.70, bf16[2048,768]{1,0:T(8,128)(2,1)S(1)} %bitcast.50, ...), custom_call_target="tpu_custom_call" | custom-call | tf_op jit(solution)/shard_map/pallas_call | solution.py:768
  49.4 1.6 copy-done.5
  51.7 24.2 %shard_map.206 = (bf16[2048,2048]{1,0:T(8,128)(2,1)}, f32[64,2048]{1,0:T(8,128)S(1)}, bf16[1,64,2048]{2,1,0:T(8,128)(2,1)S(1)}, f32[1,2048]{1,0:T(1,128)S(1)}, b...) custom-call(bf16[3,64,2048]{2,1,0:T(8,128)(2,1)S(1)} %get-tuple-element.70.qkv_ref, ...), custom_call_target="tpu_custom_call" | custom-call | tf_op jit(solution)/shard_map/pallas_call | solution.py:562
  76.0 0.9 copy-done.3
  76.8 1.4 copy-done.12
  78.3 0.8 copy-done.26
  79.1 8.1 %shard_map.207 = bf16[12,1,64,128]{3,2,1,0:T(8,128)(2,1)S(1)} custom-call(bf16[1,64,2048]{2,1,0:T(8,128)(2,1)S(1)} %get-tuple-element.73.refs_0_), custom_call_target="tpu_custom_call" | custom-call | tf_op jit(solution)/shard_map/pallas_call | solution.py:157
  87.3 1.6 shard_map.208
  88.9 10.2 %shard_map.209 = bf16[8,48,768]{2,1,0:T(8,128)(2,1)S(1)} custom-call(bf16[8,48,768]{2,1,0:T(8,128)(2,1)S(1)} %bitcast.69), custom_call_target="tpu_custom_call" | custom-call | tf_op jit(solution)/shard_map/pallas_call | solution.py:157
  99.7 22.1 %shard_map.210 = (bf16[4,320,768]{2,1,0:T(8,128)(2,1)S(1)}, bf16[2,4,192,768]{3,2,1,0:T(8,128)(2,1)S(1)}) custom-call(bf16[320,768]{1,0:T(8,128)(2,1)S(1)} %convolution_convert_fusion.x, bf16[2,192,768]{2,1,0:T(8,128)(2,1)S(1)} %bitcast.68), custom_call_target="tpu_custom_call" | custom-call | tf_op jit(solution)/shard_map/pallas_call | solution.py:388
  121.8 6.1 %shard_map.211 = (bf16[4,320,768]{2,1,0:T(8,128)(2,1)S(1)}, bf16[2,768,768]{2,1,0:T(8,128)(2,1)S(1)}, bf16[2,768,768]{2,1,0:T(8,128)(2,1)S(1)}) custom-call(bf16[4,4,80,768]{3,2,1,0:T(8,128)(2,1)S(1)} %bitcast.58, bf16[2,768,768]{2,1,0:T(8,128)(2,1)S(1)} %bitcast.55, bf16[2,768,768]{2,1,0:T(8,128)(2,1)S(1)} %bitcast.54), custom_call_target="tpu_custom_call" | custom-call | tf_op jit(solution)/shard_map/pallas_call | solution.py:768
  128.0 24.4 %shard_map.212 = (bf16[3,320,768]{2,1,0:T(8,128)(2,1)S(1)}, bf16[2,192,768]{2,1,0:T(8,128)(2,1)S(1)}, bf16[2,192,768]{2,1,0:T(8,128)(2,1)S(1)}) custom-call(bf16[4,320,768]{2,1,0:T(8,128)(2,1)S(1)} %get-tuple-element.79.x.partial_ref, bf16[2,2,2,192,768]{4,3,2,1,0:T(8,128)(2,1)S(1)} %bitcast.56), custom_call_target="tpu_custom_call" | custom-call | tf_op jit(solution)/shard_map/pallas_call | solution.py:435
  152.4 0.8 copy-done.22
  153.2 0.9 shard_map.213.refs_0_
  154.1 11.1 %shard_map.214 = (bf16[8,48,768]{2,1,0:T(8,128)(2,1)S(1)}, bf16[1,2,2,192,768]{4,3,2,1,0:T(8,128)(2,1)S(1)}) custom-call(bf16[8,48,768]{2,1,0:T(8,128)(2,1)S(1)} %shard_map.213.refs_0_, bf16[2,2,2,192,768]{4,3,2,1,0:T(8,128)(2,1)S(1)} %bitcast.48), custom_call_target="tpu_custom_call" | custom-call | tf_op jit(solution)/shard_map/pallas_call | solution.py:157
  165.2 1.0 copy-done.16
  166.2 2.0 shard_map.215
  168.2 9.4 %shard_map.216 = (bf16[1,64,2048]{2,1,0:T(8,128)(2,1)S(1)}, bf16[1,8,48,896]{3,2,1,0:T(8,128)(2,1)S(1)}) custom-call(bf16[1,12,64,128]{3,2,1,0:T(8,128)(2,1)S(1)} %bitcast.71, bf16[8,2,48,896]{3,2,1,0:T(8,128)(2,1)S(1)} %bitcast.51), custom_call_target="tpu_custom_call" | custom-call | tf_op jit(solution)/shard_map/pallas_call | solution.py:157
  177.6 1.1 copy-done.9
  178.7 0.9 copy-done.20
  179.5 0.7 copy-done.32
  180.2 1.3 constant_dynamic-slice_fusion
  181.5 1.3 fusion.1.l_ref.late_ref
  182.8 1.7 fusion.g_ref
  184.6 27.9 %shard_map.217 = (bf16[3,64,2048]{2,1,0:T(8,128)(2,1)S(1)}, f32[768,256]{1,0:T(8,128)S(1)}, bf16[16,48,1536]{2,1,0:T(8,128)(2,1)S(1)}, bf16[2,192,768]{2,1,0:T(8,128)(2,1)S(1)}, bf16[3,2,48,896]{3,2,1,0:T(8,128)(2,1)S(1)}) custom-call(bf16[3,64,2048]{2,1,0:T(8,128)(2,1)S(1)} %copy-done.4, bf16[2048,2048]{1,0:T(8,128)(2,1)} %get-tuple-element.89.p_ref, ...), custom_call_target="tpu_custom_call" | custom-call | tf_op jit(solution)/shard_map/pallas_call | solution.py:687
  212.5 0.9 copy-done.7
  213.4 1.4 copy-done.10
  214.8 0.9 copy-done.18
  215.7 0.8 copy-done.23
  216.5 0.8 copy-done.28
  217.3 3.4 %fusion.2 = (f32[2,768,192]{1,2,0:T(8,128)}, f32[2,192,768]{2,1,0:T(8,128)}) fusion(bf16[2,192,768]{2,1,0:T(8,128)(2,1)} %copy-done.23, bf16[2,2,192,768]{3,2,1,0:T(8,128)(2,1)} %copy-done, s32[]{:T(128)S(6)} %select_n.69, bf16[2,192,768]{2,1,0:T(8,128)(2,1)} %copy-done.22, bf16[2,192,768]{2,1,0:T(8,128)(2,1)} %copy-done.21), kind=kLoop, calls=%fused_computation.6 | loop fusion | flops 1769472 | bytes 4718596 | tf_op jit(solution)/shard_map/transpose | solution.py:1121
  220.7 1.0 copy-done.29
  221.7 2.2 shard_map.218
  224.0 13.6 %shard_map.219 = (bf16[7,128,192]{2,1,0:T(8,128)(2,1)S(1)}, bf16[1,48,896]{2,1,0:T(8,128)(2,1)S(1)}) custom-call(bf16[8,128,192]{2,1,0:T(8,128)(2,1)S(1)} %get-tuple-element.102.refs_0_.own_ref, bf16[2,48,896]{2,1,0:T(8,128)(2,1)S(1)} %get-tuple-element.103.refs_1_.late_ref), custom_call_target="tpu_custom_call" | custom-call | tf_op jit(solution)/shard_map/pallas_call | solution.py:157
  237.8 15.7 %shard_map.221 = (bf16[12,3,64,128]{3,2,1,0:T(8,128)(2,1)S(1)}, f32[12,8,192]{2,1,0:T(8,128)S(1)}, f32[7,8,896]{2,1,0:T(8,128)S(1)}) custom-call(bf16[3,64,2048]{2,1,0:T(8,128)(2,1)S(1)} %copy-done.8, f32[16,8,192]{2,1,0:T(8,128)S(1)} %get-tuple-element.106.refs_1_, f32[8,8,896]{2,1,0:T(8,128)S(1)} %get-tuple-element.107.refs_2_.late_ref), custom_call_target="tpu_custom_call" | custom-call | tf_op jit(solution)/shard_map/pallas_call | solution.py:157
  253.4 0.8 shard_map.223
  256.1 1.7 copy-done.11
  257.8 1.0 copy-done.31
  258.8 2.2 shard_map.222
  (74 shorter events, 3.6 us)
Async XLA Ops:
  3.7 0.7 copy-start.36
  4.4 0.7 copy-start.38
  5.1 0.7 copy-start.40
  5.9 0.9 copy-start.14
  44.7 7.0 %copy-start.24 = (bf16[2,192,768]{2,1,0:T(8,128)(2,1)S(1)}, bf16[2,192,768]{2,1,0:T(8,128)(2,1)}, u32[]{:S(2)}) copy-start(bf16[2,192,768]{2,1,0:T(8,128)(2,1)} %w_ref.1) | copy-start | bytes 1769476
  49.4 1.6 copy-start.5
  51.1 0.6 copy-start.34
  51.7 35.5 %copy-start.41 = (s32[1,128,1]{1,2,0:T(1,128)S(1)}, s32[1,128,1]{1,2,0:T(1,128)}, u32[]{:S(2)}) copy-start(s32[1,128,1]{1,2,0:T(1,128)} %param.14) | copy-start | bytes 1540
  51.7 35.6 %copy-start.15 = (bf16[1,128,768]{2,1,0:T(8,128)(2,1)S(1)}, bf16[1,128,768]{2,1,0:T(8,128)(2,1)}, u32[]{:S(2)}) copy-start(bf16[1,128,768]{2,1,0:T(8,128)(2,1)} %param.12) | copy-start | bytes 589828
  51.7 35.6 %copy-start.17 = (bf16[1,128,768]{2,1,0:T(8,128)(2,1)S(1)}, bf16[1,128,768]{2,1,0:T(8,128)(2,1)}, u32[]{:S(2)}) copy-start(bf16[1,128,768]{2,1,0:T(8,128)(2,1)} %param.13) | copy-start | bytes 589828
  76.0 0.9 copy-start.3
  76.8 1.4 copy-start.12
  78.3 0.8 copy-start.26
  88.9 10.7 %copy-start.25 = (bf16[2,768,192]{1,2,0:T(8,128)(2,1)S(1)}, bf16[2,768,192]{1,2,0:T(8,128)(2,1)}, u32[]{:S(2)}) copy-start(bf16[2,768,192]{1,2,0:T(8,128)(2,1)} %param.22) | copy-start | bytes 1769476
  88.9 32.9 %copy-start.13 = (bf16[2,4,192,768]{3,2,1,0:T(8,128)(2,1)S(1)}, bf16[2,4,192,768]{3,2,1,0:T(8,128)(2,1)}, u32[]{:S(2)}) copy-start(bf16[2,4,192,768]{3,2,1,0:T(8,128)(2,1)} %copy-done.12) | copy-start | bytes 7077892
  128.0 26.1 %copy-start.1 = (bf16[2,768,768]{2,1,0:T(8,128)(2,1)}, bf16[2,768,768]{2,1,0:T(8,128)(2,1)S(1)}, u32[]{:S(2)}) copy-start(bf16[2,768,768]{2,1,0:T(8,128)(2,1)S(1)} %get-tuple-element.82) | copy-start | bytes 7077892
  152.4 0.8 copy-start.22
  153.2 0.9 copy-start.21
  165.2 1.0 copy-start.16
  168.2 9.4 %copy-start.30 = (f32[128,768]{1,0:T(8,128)}, f32[128,768]{1,0:T(8,128)S(1)}, u32[]{:S(2)}) copy-start(f32[128,768]{1,0:T(8,128)S(1)} %get-tuple-element.110.residual_ref) | copy-start | bytes 1179652
  177.6 1.1 copy-start.9
  178.7 0.9 copy-start.20
  179.5 0.7 copy-start.32
  180.2 2.6 copy-start.2
  182.8 1.8 copy-start.4
  182.8 1.8 copy-start.27
  182.8 1.8 copy-start.33
  182.8 1.8 copy-start.35
  184.6 27.9 %copy-start = (bf16[2,2,192,768]{3,2,1,0:T(8,128)(2,1)}, bf16[2,2,192,768]{3,2,1,0:T(8,128)(2,1)S(1)}, u32[]{:S(2)}) copy-start(bf16[2,2,192,768]{3,2,1,0:T(8,128)(2,1)S(1)} %fusion.g_ref) | copy-start | bytes 3538948
  212.5 0.9 copy-start.7
  213.4 1.4 copy-start.10
  214.8 0.9 copy-start.18
  215.7 0.8 copy-start.23
  216.5 0.8 copy-start.28
  217.3 3.4 %copy-start.6 = (bf16[2048,768]{1,0:T(8,128)(2,1)S(1)}, bf16[2048,768]{1,0:T(8,128)(2,1)}, u32[]{:S(2)}) copy-start(bf16[2048,768]{1,0:T(8,128)(2,1)} %copy-done.5) | copy-start | bytes 9437188
  217.3 3.4 %copy-start.8 = (bf16[3,64,2048]{2,1,0:T(8,128)(2,1)S(1)}, bf16[3,64,2048]{2,1,0:T(8,128)(2,1)}, u32[]{:S(2)}) copy-start(bf16[3,64,2048]{2,1,0:T(8,128)(2,1)} %copy-done.7) | copy-start | bytes 2359300
  217.3 3.4 %copy-start.19 = (f32[768,256]{1,0:T(8,128)S(1)}, f32[768,256]{1,0:T(8,128)}, u32[]{:S(2)}) copy-start(f32[768,256]{1,0:T(8,128)} %copy-done.18) | copy-start | bytes 2359300
  220.7 1.0 copy-start.29
  237.6 15.8 %copy-start.37 = (bf16[6,1536]{1,0:T(8,128)(2,1)S(1)}, bf16[6,1536]{1,0:T(8,128)(2,1)}, u32[]{:S(2)}) copy-start(bf16[6,1536]{1,0:T(8,128)(2,1)} %wkv_ref.3) | copy-start | bytes 55300
  237.6 15.8 %copy-start.39 = (bf16[6,768]{1,0:T(8,128)(2,1)S(1)}, bf16[6,768]{1,0:T(8,128)(2,1)}, u32[]{:S(2)}) copy-start(bf16[6,768]{1,0:T(8,128)(2,1)} %wq_ref.3) | copy-start | bytes 27652
  256.1 1.7 copy-start.11
  257.8 1.0 copy-start.31

commit v6 on v5

--- a/solution.py
+++ b/solution.py
@@ -564,11 +564,11 @@
         grid=(LEN // QUERIES,),
         out_shape=(
             pltpu.HBM((LEN, LEN), low),
-            jax.ShapeDtypeStruct((HEAD_DIM, LEN), wide),
+            pltpu.HBM((HEAD_DIM, LEN), wide),
             jax.ShapeDtypeStruct((1, HEAD_DIM, LEN), low),
             jax.ShapeDtypeStruct((1, LEN), wide),
-            jax.ShapeDtypeStruct((CTX, *x.shape), low),
-            jax.ShapeDtypeStruct((2, 4, *w.shape[1:]), low),
+            pltpu.HBM((CTX, *x.shape), low),
+            pltpu.HBM((2, 4, *w.shape[1:]), low),
         ),
         in_specs=[whole(3, HEAD_DIM, LEN), whole(BUCKETS, 128), ANY, whole(*w.shape)],
         out_specs=(
@@ -690,8 +690,8 @@
         out_shape=(
             jax.ShapeDtypeStruct((3, HEAD_DIM, LEN), low),
             jax.ShapeDtypeStruct((6 * CHUNK, QUERIES), wide),
-            jax.ShapeDtypeStruct((CTX, *x.shape), low),
-            jax.ShapeDtypeStruct(grads.shape[:1] + grads.shape[2:], low),
+            pltpu.HBM((CTX, *x.shape), low),
+            pltpu.HBM(grads.shape[:1] + grads.shape[2:], low),
             jax.ShapeDtypeStruct((ZED - 1, *late.shape[1:]), low),
         ),
         in_specs=[
@@ -977,6 +977,14 @@
     sum_ref[...] = total.astype(low)
 
 
+def halves_kernel(late_ref, late_others_ref, grads_ref, others_ref, late_out, grads_out):
+    k = spot()[4]
+    late = late_ref[:, k].astype(wide) + late_others_ref[0].astype(wide)
+    late_out[...] = late.astype(low).reshape(ZED, 2, 48, 896)
+    grads = grads_ref[:, :, k].astype(wide) + others_ref[0].astype(wide)
+    grads_out[...] = grads.astype(low)
+
+
 def owners_kernel(own_ref, others_ref, late_ref, late_others_ref, out_ref, sum_ref):
     c, e, z, xh, k = spot()
     total = own_ref[e].astype(wide) + jnp.sum(others_ref[...].astype(wide), axis=0)
@@ -1091,8 +1099,7 @@
     grad_expert_out = grads_own.astype(wide) + grads_other.astype(wide)
     spread = plain(unlist_kernel, [((EXP, SLOTS, D), low)], 12, partial, others)[0]
     expert_grads = grads_in.reshape(2, 2, 2, 192, D)
-    back, others = swaps(9, (spread, "exp", 0, True), (expert_grads, "core", 2, False))
-    expert_grads = add_up(expert_grads, "core", 2, others).astype(low)
+    back, expert_others = swaps(9, (spread, "exp", 0, True), (expert_grads, "core", 2, False))
     mixed_rows, grad_residual, grad_attended, late = plain(
         combine_kernel,
         [(routed, low), (routed, wide), ((D, TOK), low), ((D, 896), low)],
@@ -1113,7 +1120,15 @@
         (grad_attended.reshape(1, HEADS, HEAD_DIM, TOK), "to_heads", None, True),
         (late, "core", 1, False),
     )
-    late = add_up(late, "core", 1, others).astype(low).reshape(ZED, 2, 48, 896)
+    late, expert_grads = plain(
+        halves_kernel,
+        [((ZED, 2, 48, 896), low), ((2, 2, 192, D), low)],
+        14,
+        late,
+        others,
+        expert_grads,
+        expert_others,
+    )
     head_grads, tile_sums, qkv_full, others, late_others = attend_back(
         head_qkv, probs, attended, inverse, head_grad, block_qkv, expert_grads, late, 19
     )

time: 263 us -> 258 us (0.981)
  other arithmetic: 8.28 us -> 5.31 us
    convert_element_type x2 -> x0, other arithmetic: 2.97 us -> none  [the longest x1 1.71 us: shards(): expert_grads = add_up(expert_grads, 'core', 2, others).astype(low)]
    unnamed x84 -> x78, local copies, waits for them, and re-layouts: 21.5 us -> 19.8 us
    pallas_call x9 -> x10, Pallas kernels: 19.9 us -> 20.6 us  [plain(): pl.pallas_call(kernel, out_shape=[jax.ShapeDtypeStruct(shape, kind) for s...]
where the time goes in v6:
time: 258 us; the launch traced here: 257 us
  Pallas kernels  226 us (88%)
  local copies, waits for them, and re-layouts  23.6 us (9%)
  other arithmetic  5.31 us (2%)
    pallas_call x6, Pallas kernels, swaps(): pl.pallas_call(functools.partial(swaps_kernel, [item[1:] for item in item...  68 us
    pallas_call x1, Pallas kernels, opening(): pl.pallas_call(open_kernel, out_shape=[jax.ShapeDtypeStruct(s, low) for s...  37.8 us
    pallas_call x1, Pallas kernels, attend_back(): pl.pallas_call(backward_kernel, grid=(LEN // QUERIES,), out_shape=(jax.Sh...  28.2 us
    pallas_call x1, Pallas kernels, attend(): pl.pallas_call(forward_kernel, grid=(LEN // QUERIES,), out_shape=(pltpu.H...  24.6 us
    pallas_call x1, Pallas kernels, return_lists(): pl.pallas_call(return_kernel, out_shape=[jax.ShapeDtypeStruct(s, low) for...  24.4 us
    pallas_call x1, Pallas kernels, gather_lists(): pl.pallas_call(lists_kernel, out_shape=[jax.ShapeDtypeStruct(s, low) for...  22 us
    pallas_call x10, Pallas kernels, plain(): pl.pallas_call(kernel, out_shape=[jax.ShapeDtypeStruct(shape, kind) for s...  20.6 us
    unnamed x78, local copies, waits for them, and re-layouts  19.8 us

profile of v6, /device:TPU:1, one launch (start us, length us, event | category | flops | bytes accessed | tf_op | source)
XLA Modules:
  0.0 256.8 jit_solution(18030908863163460436)
XLA Ops:
  0.6 0.8 copy.30
  1.4 0.7 pad_bitcast_fusion
  2.2 0.8 copy.31
  2.9 0.8 concatenate.3.extra_ref
  3.7 0.7 copy-done.33
  4.4 0.7 copy-done.35
  5.1 0.7 copy-done.37
  6.0 0.9 copy-done.11
  6.9 37.8 %shard_map.204 = (bf16[8,15,16,128]{3,2,1,0:T(8,128)(2,1)S(1)}, bf16[16,8,16,128]{3,2,1,0:T(8,128)(2,1)S(1)}, bf16[16,128,768]{2,1,0:T(8,128)(2,1)S(1)}) custom-call(bf16[15,16,128]{2,1,0:T(8,128)(2,1)S(1)} %shard_map.203.packed, bf16[128,768]{1,0:T(8,128)(2,1)S(1)} %bitcast.47), custom_call_target="tpu_custom_call" | custom-call | tf_op jit(solution)/shard_map/pallas_call | solution.py:355
  44.7 4.8 %shard_map.205 = (bf16[3,64,2048]{2,1,0:T(8,128)(2,1)S(1)}, bf16[2048,768]{1,0:T(8,128)(2,1)S(1)}, f32[32,128]{1,0:T(8,128)S(1)}, bf16[48,1664]{1,0:T(8,128)(2,1)S(1)}, bf16[48,1536]{1,0:T(8,128)(2,1)S(1)}) custom-call(bf16[2048,128]{1,0:T(8,128)(2,1)S(1)} %bitcast.55, bf16[2048,768]{1,0:T(8,128)(2,1)S(1)} %bitcast.38, ...), custom_call_target="tpu_custom_call" | custom-call | tf_op jit(solution)/shard_map/pallas_call | solution.py:768
  49.5 1.6 copy-done.2
  51.1 0.7 copy-done.31
  51.8 24.6 %shard_map.206 = (bf16[2048,2048]{1,0:T(8,128)(2,1)}, f32[64,2048]{1,0:T(8,128)}, bf16[1,64,2048]{2,1,0:T(8,128)(2,1)S(1)}, f32[1,2048]{1,0:T(1,128)S(1)}, bf16[...) custom-call(bf16[3,64,2048]{2,1,0:T(8,128)(2,1)S(1)} %get-tuple-element.72.qkv_ref, ...), custom_call_target="tpu_custom_call" | custom-call | tf_op jit(solution)/shard_map/pallas_call | solution.py:562
  76.3 8.2 %shard_map.207 = bf16[12,1,64,128]{3,2,1,0:T(8,128)(2,1)S(1)} custom-call(bf16[1,64,2048]{2,1,0:T(8,128)(2,1)S(1)} %get-tuple-element.75.refs_0_), custom_call_target="tpu_custom_call" | custom-call | tf_op jit(solution)/shard_map/pallas_call | solution.py:157
  84.6 0.7 copy.33.route_ref
  85.3 1.7 copy-done
  87.0 0.9 copy-done.12
  88.0 0.9 copy-done.14
  88.9 0.8 copy-done.18
  89.7 1.6 shard_map.208
  91.4 10.3 %shard_map.209 = bf16[8,48,768]{2,1,0:T(8,128)(2,1)S(1)} custom-call(bf16[8,48,768]{2,1,0:T(8,128)(2,1)S(1)} %bitcast.54), custom_call_target="tpu_custom_call" | custom-call | tf_op jit(solution)/shard_map/pallas_call | solution.py:157
  102.2 22.0 %shard_map.210 = (bf16[4,320,768]{2,1,0:T(8,128)(2,1)S(1)}, bf16[2,4,192,768]{3,2,1,0:T(8,128)(2,1)S(1)}) custom-call(bf16[320,768]{1,0:T(8,128)(2,1)S(1)} %convolution_convert_fusion.x, bf16[2,192,768]{2,1,0:T(8,128)(2,1)S(1)} %bitcast.53), custom_call_target="tpu_custom_call" | custom-call | tf_op jit(solution)/shard_map/pallas_call | solution.py:388
  124.2 6.2 %shard_map.211 = (bf16[4,320,768]{2,1,0:T(8,128)(2,1)S(1)}, bf16[2,768,768]{2,1,0:T(8,128)(2,1)S(1)}, bf16[2,768,768]{2,1,0:T(8,128)(2,1)S(1)}) custom-call(bf16[4,4,80,768]{3,2,1,0:T(8,128)(2,1)S(1)} %bitcast.44, bf16[2,768,768]{2,1,0:T(8,128)(2,1)S(1)} %bitcast.41, bf16[2,768,768]{2,1,0:T(8,128)(2,1)S(1)} %bitcast.40), custom_call_target="tpu_custom_call" | custom-call | tf_op jit(solution)/shard_map/pallas_call | solution.py:768
  130.4 24.4 %shard_map.212 = (bf16[3,320,768]{2,1,0:T(8,128)(2,1)S(1)}, bf16[2,192,768]{2,1,0:T(8,128)(2,1)S(1)}, bf16[2,192,768]{2,1,0:T(8,128)(2,1)S(1)}) custom-call(bf16[4,320,768]{2,1,0:T(8,128)(2,1)S(1)} %get-tuple-element.81.x.partial_ref, bf16[2,2,2,192,768]{4,3,2,1,0:T(8,128)(2,1)S(1)} %bitcast.42), custom_call_target="tpu_custom_call" | custom-call | tf_op jit(solution)/shard_map/pallas_call | solution.py:435
  154.9 0.9 shard_map.213.refs_0_
  155.9 11.0 %shard_map.214 = (bf16[8,48,768]{2,1,0:T(8,128)(2,1)S(1)}, bf16[1,2,2,192,768]{4,3,2,1,0:T(8,128)(2,1)S(1)}) custom-call(bf16[8,48,768]{2,1,0:T(8,128)(2,1)S(1)} %shard_map.213.refs_0_, bf16[2,2,2,192,768]{4,3,2,1,0:T(8,128)(2,1)S(1)} %bitcast.34), custom_call_target="tpu_custom_call" | custom-call | tf_op jit(solution)/shard_map/pallas_call | solution.py:157
  166.9 2.0 shard_map.215
  169.0 9.4 %shard_map.216 = (bf16[1,64,2048]{2,1,0:T(8,128)(2,1)S(1)}, bf16[1,8,48,896]{3,2,1,0:T(8,128)(2,1)S(1)}) custom-call(bf16[1,12,64,128]{3,2,1,0:T(8,128)(2,1)S(1)} %bitcast.56, bf16[8,2,48,896]{3,2,1,0:T(8,128)(2,1)S(1)} %bitcast.36), custom_call_target="tpu_custom_call" | custom-call | tf_op jit(solution)/shard_map/pallas_call | solution.py:157
  178.8 0.5 copy-done.26
  179.4 28.2 %shard_map.218 = (bf16[3,64,2048]{2,1,0:T(8,128)(2,1)S(1)}, f32[768,256]{1,0:T(8,128)S(1)}, bf16[16,48,1536]{2,1,0:T(8,128)(2,1)}, bf16[2,192,768]{2,1,0:T(8,128)(2,1)}, bf16[3,2,48,896]{3,2,1,0:T(8,128)(2,1)S(1)}) custom-call(bf16[3,64,2048]{2,1,0:T(8,128)(2,1)S(1)} %get-tuple-element.72.qkv_ref, bf16[2048,2048]{1,0:T(8,128)(2,1)} %get-tuple-element.91.p_ref, ...), custom_call_target="tpu_custom_call" | custom-call | tf_op jit(solution)/shard_map/pallas_call | solution.py:687
  207.7 0.9 copy-done.4
  208.6 0.9 copy-done.16
  209.5 0.8 copy-done.27
  210.3 3.4 %fusion = (f32[2,768,192]{1,2,0:T(8,128)}, f32[2,192,768]{2,1,0:T(8,128)}) fusion(bf16[2,192,768]{2,1,0:T(8,128)(2,1)} %get-tuple-element.124, s32[]{:T(128)S(6)} %select_n.55, bf16[2,192,768]{2,1,0:T(8,128)(2,1)} %copy-done.21, bf16[2,192,768]{2,1,0:T(8,128)(2,1)} %copy-done.20, bf16[2,2,192,768]{3,2,1,0:T(8,128)(2,1)} %copy-done.8), kind=kLoop, calls=%fused_computation.2 | loop fusion | flops 1769472 | bytes 4718596 | tf_op jit(solution)/shard_map/transpose | solution.py:1136
  213.7 1.1 copy-done.17
  214.8 1.0 copy-done.28
  215.9 2.3 shard_map.219
  218.1 13.3 %shard_map.220 = (bf16[7,128,192]{2,1,0:T(8,128)(2,1)S(1)}, bf16[1,48,896]{2,1,0:T(8,128)(2,1)S(1)}) custom-call(bf16[8,128,192]{2,1,0:T(8,128)(2,1)S(1)} %get-tuple-element.106.refs_0_.own_ref, bf16[2,48,896]{2,1,0:T(8,128)(2,1)S(1)} %get-tuple-element.107.refs_1_.late_ref), custom_call_target="tpu_custom_call" | custom-call | tf_op jit(solution)/shard_map/pallas_call | solution.py:157
  231.6 15.8 %shard_map.222 = (bf16[12,3,64,128]{3,2,1,0:T(8,128)(2,1)S(1)}, f32[12,8,192]{2,1,0:T(8,128)S(1)}, f32[7,8,896]{2,1,0:T(8,128)S(1)}) custom-call(bf16[3,64,2048]{2,1,0:T(8,128)(2,1)S(1)} %copy-done.5, f32[16,8,192]{2,1,0:T(8,128)S(1)} %get-tuple-element.110.refs_1_, f32[8,8,896]{2,1,0:T(8,128)S(1)} %get-tuple-element.111.refs_2_.late_ref), custom_call_target="tpu_custom_call" | custom-call | tf_op jit(solution)/shard_map/pallas_call | solution.py:157
  247.4 0.8 copy-done.22
  248.3 0.8 shard_map.224
  249.0 0.6 reduce
  249.6 0.6 reduce.1
  250.3 0.6 reduce.2
  250.9 1.7 copy-done.9
  252.6 1.1 copy-done.23
  253.6 1.0 copy-done.30
  254.6 2.2 shard_map.223
  (66 shorter events, 1.5 us)
Async XLA Ops:
  3.7 0.7 copy-start.33
  4.4 0.7 copy-start.35
  5.1 0.7 copy-start.37
  5.9 0.9 copy-start.11
  44.7 7.1 %copy-start.24 = (bf16[2,192,768]{2,1,0:T(8,128)(2,1)S(1)}, bf16[2,192,768]{2,1,0:T(8,128)(2,1)}, u32[]{:S(2)}) copy-start(bf16[2,192,768]{2,1,0:T(8,128)(2,1)} %w_ref.1) | copy-start | bytes 1769476
  49.5 1.6 copy-start.2
  51.1 0.7 copy-start.31
  51.7 32.8 %copy-start.38 = (s32[1,128,1]{1,2,0:T(1,128)S(1)}, s32[1,128,1]{1,2,0:T(1,128)}, u32[]{:S(2)}) copy-start(s32[1,128,1]{1,2,0:T(1,128)} %param.14) | copy-start | bytes 1540
  85.3 1.7 copy-start
  87.0 0.9 copy-start.12
  88.0 0.9 copy-start.14
  88.9 0.8 copy-start.18
  91.4 10.9 %copy-start.25 = (bf16[2,768,192]{1,2,0:T(8,128)(2,1)S(1)}, bf16[2,768,192]{1,2,0:T(8,128)(2,1)}, u32[]{:S(2)}) copy-start(bf16[2,768,192]{1,2,0:T(8,128)(2,1)} %param.22) | copy-start | bytes 1769476
  91.4 32.8 %copy-start.10 = (bf16[2,4,192,768]{3,2,1,0:T(8,128)(2,1)S(1)}, bf16[2,4,192,768]{3,2,1,0:T(8,128)(2,1)}, u32[]{:S(2)}) copy-start(bf16[2,4,192,768]{3,2,1,0:T(8,128)(2,1)} %get-tuple-element.80) | copy-start | bytes 7077892
  154.9 0.9 copy-start.20
  154.9 1.0 copy-start.21
  155.9 11.0 %copy-start.1 = (bf16[16,48,1664]{2,1,0:T(8,128)(2,1)S(1)}, bf16[16,48,1664]{2,1,0:T(8,128)(2,1)}, u32[]{:S(2)}) copy-start(bf16[16,48,1664]{2,1,0:T(8,128)(2,1)} %get-tuple-element.76) | copy-start | bytes 7667716
  155.9 11.0 %copy-start.15 = (bf16[1,128,768]{2,1,0:T(8,128)(2,1)S(1)}, bf16[1,128,768]{2,1,0:T(8,128)(2,1)}, u32[]{:S(2)}) copy-start(bf16[1,128,768]{2,1,0:T(8,128)(2,1)} %param.13) | copy-start | bytes 589828
  155.9 11.0 %copy-start.19 = (s32[128,1]{1,0:T(8,128)S(1)}, s32[128,1]{1,0:T(8,128)}, u32[]{:S(2)}) copy-start(s32[128,1]{1,0:T(8,128)} %copy.33.route_ref) | copy-start | bytes 1540
  168.9 9.9 %copy-start.29 = (f32[128,768]{1,0:T(8,128)}, f32[128,768]{1,0:T(8,128)S(1)}, u32[]{:S(2)}) copy-start(f32[128,768]{1,0:T(8,128)S(1)} %get-tuple-element.114.residual_ref) | copy-start | bytes 1179652
  178.3 1.0 copy-start.26
  178.3 1.1 copy-start.32
  178.8 28.8 %copy-start.6 = (bf16[4,2,48,896]{3,2,1,0:T(8,128)(2,1)}, bf16[4,2,48,896]{3,2,1,0:T(8,128)(2,1)S(1)}, u32[]{:S(2)}) copy-start(bf16[4,2,48,896]{3,2,1,0:T(8,128)(2,1)S(1)} %get-tuple-element.101.l_ref.late_ref) | copy-start | bytes 2064388
  178.8 28.8 %copy-start.8 = (bf16[2,2,192,768]{3,2,1,0:T(8,128)(2,1)}, bf16[2,2,192,768]{3,2,1,0:T(8,128)(2,1)S(1)}, u32[]{:S(2)}) copy-start(bf16[2,2,192,768]{3,2,1,0:T(8,128)(2,1)S(1)} %get-tuple-element.100.g_ref) | copy-start | bytes 3538948
  207.6 0.9 copy-start.4
  208.5 0.9 copy-start.16
  209.4 0.8 copy-start.27
  210.3 3.4 %copy-start.3 = (bf16[2048,768]{1,0:T(8,128)(2,1)S(1)}, bf16[2048,768]{1,0:T(8,128)(2,1)}, u32[]{:S(2)}) copy-start(bf16[2048,768]{1,0:T(8,128)(2,1)} %copy-done.2) | copy-start | bytes 9437188
  210.3 3.4 %copy-start.5 = (bf16[3,64,2048]{2,1,0:T(8,128)(2,1)S(1)}, bf16[3,64,2048]{2,1,0:T(8,128)(2,1)}, u32[]{:S(2)}) copy-start(bf16[3,64,2048]{2,1,0:T(8,128)(2,1)} %copy-done.4) | copy-start | bytes 2359300
  210.3 3.4 %copy-start.7 = (bf16[4,2,48,896]{3,2,1,0:T(8,128)(2,1)S(1)}, bf16[4,2,48,896]{3,2,1,0:T(8,128)(2,1)}, u32[]{:S(2)}) copy-start(bf16[4,2,48,896]{3,2,1,0:T(8,128)(2,1)} %copy-done.6) | copy-start | bytes 2064388
  213.7 1.1 copy-start.17
  214.8 1.0 copy-start.28
  231.4 16.8 %copy-start.34 = (bf16[6,1536]{1,0:T(8,128)(2,1)S(1)}, bf16[6,1536]{1,0:T(8,128)(2,1)}, u32[]{:S(2)}) copy-start(bf16[6,1536]{1,0:T(8,128)(2,1)} %wkv_ref.3) | copy-start | bytes 55300
  231.4 16.8 %copy-start.36 = (bf16[6,768]{1,0:T(8,128)(2,1)S(1)}, bf16[6,768]{1,0:T(8,128)(2,1)}, u32[]{:S(2)}) copy-start(bf16[6,768]{1,0:T(8,128)(2,1)} %wq_ref.3) | copy-start | bytes 27652
  231.6 19.3 %copy-start.13 = (bf16[1,128,768]{2,1,0:T(8,128)(2,1)S(1)}, bf16[1,128,768]{2,1,0:T(8,128)(2,1)}, u32[]{:S(2)}) copy-start(bf16[1,128,768]{2,1,0:T(8,128)(2,1)} %param.12) | copy-start | bytes 589828
  247.4 0.8 copy-start.22
  250.9 1.7 copy-start.9
  252.6 1.1 copy-start.23
  253.6 1.0 copy-start.30
